TPU v7x, 32 devices: a whole 2x2x4 slice. The times are simulated.
32 devices in a mesh: dp: 8 (over z, x), seq: 4 (over y, core).
Axes of the slice: x: 2, y: 2, z: 4, core: 2. Of those that a mesh axis runs over, the one named last changes fastest.
Arguments:
- hidden: bfloat16 [8, 512, 5120], P('dp', 'seq'), may hold values from -6 to 6
- queries: bfloat16 [8, 512, 2560], P('dp', 'seq'), may hold values from -9 to 9
- keys: bfloat16 [8, 512, 512], P('dp', 'seq'), may hold values from -9 to 9
- value_weight: bfloat16 [5120, 512], P('dp'), may hold values from -0.078125 to 0.078125
- doc_ids: int32 [8, 512], P('dp', 'seq'), may hold values from 0 to 3, never falling along the last dimension, each value on 1 to 256 neighbouring positions
- cotangent: bfloat16 [8, 512, 2560], P('dp', 'seq'), may hold values from -6 to 6
Outputs:
- attn_out: bfloat16 [8, 512, 2560], P('dp', 'seq')
- grad_queries: bfloat16 [8, 512, 2560], P('dp', 'seq')
- grad_keys: bfloat16 [8, 512, 512], P('dp', 'seq')
- grad_hidden: bfloat16 [8, 512, 5120], P('dp', 'seq')
- grad_weight: float32 [5120, 512], P('dp')
Inputs may be any that keep to these rules, and one draw needn't show every extreme that they name: `doc_ids`: document numbers never fall along a span; one document has exactly 256 tokens, none more.
All inputs are finite; a program needn't handle non-finite values.
Results may differ from a plain program's by a relative error of at most 0.025.
Values may be sent and summed in bfloat16 or wider, within the bound.
No kernel may reach another device: no remote copies, remote signals or barrier semaphores. Data moves between devices by JAX's collectives and lax.ppermute only.
A program may use at most 128 MiB of HBM per device.

v0:
```python
import jax
import jax.numpy as jnp
from jax import lax
from jax.sharding import PartitionSpec as P

QUERY_HEADS = 20
KEY_VALUE_HEADS = 4
HEAD_SIZE = 128
QUERY_PER_KV = 5


def body(hidden, queries, keys, value_weight, doc_ids, cotangent):
    tokens = hidden[0]
    row_count = tokens.shape[0]
    width = value_weight.shape[1]
    scale = HEAD_SIZE ** (-0.5)
    shard_list = lax.axis_size("seq")
    my_index = lax.axis_index("seq")
    full_weight = lax.all_gather(value_weight, "dp", axis=0, tiled=True)
    values_sum = jnp.dot(tokens, full_weight, preferred_element_type=jnp.float32)
    values = values_sum.astype(jnp.bfloat16)
    every_key, every_value, all_docs = (
        lax.all_gather(keys[0], "seq", axis=0, tiled=True),
        lax.all_gather(values, "seq", axis=0, tiled=True),
        lax.all_gather(doc_ids[0], "seq", axis=0, tiled=True),
    )
    query_head_rows = queries[0].reshape(row_count, KEY_VALUE_HEADS, QUERY_PER_KV, HEAD_SIZE)
    gradient_heads = cotangent[0].reshape(row_count, KEY_VALUE_HEADS, QUERY_PER_KV, HEAD_SIZE)
    query_docs = doc_ids[0]
    query_pos = my_index * row_count + jnp.arange(row_count, dtype=jnp.int32)
    local_pos = jnp.arange(row_count, dtype=jnp.int32)

    def block_scores(shard):
        start_offset = shard * row_count
        key_tile = lax.dynamic_slice_in_dim(every_key, start_offset, row_count, 0).reshape(
            row_count, KEY_VALUE_HEADS, HEAD_SIZE
        )
        value_tile = lax.dynamic_slice_in_dim(every_value, start_offset, row_count, 0).reshape(
            row_count, KEY_VALUE_HEADS, HEAD_SIZE
        )
        doc_block = lax.dynamic_slice_in_dim(all_docs, start_offset, row_count, 0)
        scores = (
            jnp.einsum(
                "qhgd,khd->hgqk", query_head_rows, key_tile, preferred_element_type=jnp.float32
            )
            * scale
        )
        allow = ((start_offset + local_pos)[None, :] <= query_pos[:, None]) & (
            doc_block[None, :] == query_docs[:, None]
        )
        return (jnp.where(allow, scores, -1e30), allow, key_tile, value_tile)

    def forward_step(shard, carry):
        peak, total, out_acc = carry
        masked, allow, key_tile, value_tile = block_scores(shard)
        new_peak = jnp.maximum(peak, jnp.max(masked, axis=-1))
        expd = jnp.where(allow, jnp.exp(masked - new_peak[..., None]), 0.0)
        factor = jnp.exp(peak - new_peak)
        total = total * factor + jnp.sum(expd, axis=-1)
        out_acc = out_acc * factor[..., None] + jnp.einsum(
            "hgqk,khd->hgqd",
            expd.astype(jnp.bfloat16),
            value_tile,
            preferred_element_type=jnp.float32,
        )
        return (new_peak, total, out_acc)

    head_layout = (KEY_VALUE_HEADS, QUERY_PER_KV, row_count)
    start_state = (
        jnp.full(head_layout, -1e30, jnp.float32),
        jnp.zeros(head_layout, jnp.float32),
        jnp.zeros((KEY_VALUE_HEADS, QUERY_PER_KV, row_count, HEAD_SIZE), jnp.float32),
    )
    peak, total, out_acc = lax.fori_loop(0, shard_list, forward_step, start_state)
    attn_b = (out_acc / total[..., None]).astype(jnp.bfloat16).transpose(2, 0, 1, 3)
    delta = jnp.sum(
        gradient_heads.astype(jnp.float32) * attn_b.astype(jnp.float32), axis=-1
    ).transpose(1, 2, 0)

    def gradient_update(shard, carry):
        dq_acc, grad_buf = carry
        masked, allow, key_tile, value_tile = block_scores(shard)
        probs = jnp.where(allow, jnp.exp(masked - peak[..., None]), 0.0) / total[..., None]
        probs_b = probs.astype(jnp.bfloat16)
        dprob = jnp.einsum(
            "qhgd,khd->hgqk", gradient_heads, value_tile, preferred_element_type=jnp.float32
        )
        dscore = (probs * (dprob - delta[..., None])).astype(jnp.bfloat16)
        dq_acc = dq_acc + jnp.einsum(
            "hgqk,khd->qhgd", dscore, key_tile, preferred_element_type=jnp.float32
        )
        dk_block = (
            jnp.einsum(
                "hgqk,qhgd->khd", dscore, query_head_rows, preferred_element_type=jnp.float32
            )
            * scale
        ).astype(jnp.bfloat16)
        dv_block = jnp.einsum(
            "hgqk,qhgd->khd", probs_b, gradient_heads, preferred_element_type=jnp.float32
        ).astype(jnp.bfloat16)
        paired = jnp.concatenate(
            (dk_block.reshape(row_count, width), dv_block.reshape(row_count, width)), axis=1
        )
        grad_buf = lax.dynamic_update_slice_in_dim(grad_buf, paired, shard * row_count, 0)
        return (dq_acc, grad_buf)

    blank_buffer = jnp.zeros((row_count * shard_list, 2 * width), jnp.bfloat16)
    dq_acc, grad_buf = lax.fori_loop(
        0,
        shard_list,
        gradient_update,
        (
            jnp.zeros((row_count, KEY_VALUE_HEADS, QUERY_PER_KV, HEAD_SIZE), jnp.float32),
            blank_buffer,
        ),
    )
    grad_queries = (dq_acc * scale).astype(jnp.bfloat16).reshape(row_count, QUERY_HEADS * HEAD_SIZE)
    summed = lax.psum_scatter(
        grad_buf.astype(jnp.float32).astype(jnp.bfloat16), "seq", scatter_dimension=0, tiled=True
    ).astype(jnp.float32)
    grad_keys = summed[:, :width].astype(jnp.bfloat16)
    grad_values = summed[:, width:].astype(jnp.bfloat16)
    grad_hidden = jnp.einsum(
        "kc,dc->kd", grad_values, full_weight, preferred_element_type=jnp.float32
    ).astype(jnp.bfloat16)
    partial_rows = lax.psum_scatter(
        jnp.einsum("kd,kc->dc", tokens, grad_values, preferred_element_type=jnp.float32).astype(
            jnp.bfloat16
        ),
        "dp",
        scatter_dimension=0,
        tiled=True,
    )
    grad_weight = lax.psum(partial_rows, "seq").astype(jnp.float32)
    return (
        attn_b.reshape(row_count, QUERY_HEADS * HEAD_SIZE)[None],
        grad_queries[None],
        grad_keys[None],
        grad_hidden[None],
        grad_weight,
    )


def solution(mesh):
    in_specs = (
        P("dp", "seq", None),
        P("dp", "seq", None),
        P("dp", "seq", None),
        P("dp", None),
        P("dp", "seq"),
        P("dp", "seq", None),
    )
    out_specs = (
        P("dp", "seq", None),
        P("dp", "seq", None),
        P("dp", "seq", None),
        P("dp", "seq", None),
        P("dp", None),
    )
    return jax.shard_map(body, mesh=mesh, in_specs=in_specs, out_specs=out_specs, check_vma=False)
```

profile of v0, /device:TPU:0, one launch (start us, length us, event | category | flops | bytes accessed | tf_op | source)
XLA Modules:
  0.0 360.2 jit_solution(5966865301399358691)
XLA Ops:
  8.0 1.5 copy.58
  9.5 1.1 copy.59
  11.1 6.0 %all-gather = s32[1,512]{1,0:T(1,128)S(1)} all-gather(s32[1,128]{1,0:T(1,128)S(1)} %copy-done.15), channel_id=2, replica_groups=mesh['dp'=8,'seq'=4] {'seq'}, dimensions={1}, use_global_device_ids=true | all-gather | bytes 2560 | tf_op jit(solution)/shard_map/all_gather | solution.py:25
  17.1 8.2 %all-gather.1 = bf16[1,512,512]{1,2,0:T(8,128)(2,1)} all-gather(bf16[1,128,512]{1,2,0:T(8,128)(2,1)S(1)} %copy.57), channel_id=3, replica_groups=mesh['dp'=8,'seq'=4] {'seq'}, dimensions={1}, use_global_device_ids=true | all-gather | bytes 655360 | tf_op jit(solution)/shard_map/all_gather | solution.py:23
  25.2 73.9 %all-gather.4.cloned.1.call-done = bf16[5120,512]{1,0:T(8,128)(2,1)} async-done(((bf16[640,512]{1,0:T(8,128)(2,1)}), bf16[5120,512]{1,0:T(8,128)(2,1)}) %all-gather.4.cloned.1.call-update) | async-done | bytes 5242896 | tf_op jit(solution)/shard_map/all_gather | solution.py:19
  99.2 3.3 fusion.37
  102.5 7.2 %all_gather.15 = bf16[512,512]{1,0:T(8,128)(2,1)S(1)} all-gather(bf16[128,512]{1,0:T(8,128)(2,1)S(1)} %fusion.37), channel_id=1, replica_groups=mesh['dp'=8,'seq'=4] {'seq'}, dimensions={0}, use_global_device_ids=true | all-gather | bytes 655360 | tf_op jit(solution)/shard_map/all_gather | solution.py:24
  110.7 24.1 %while.34 = (s32[]{:T(128)}, f32[4,5,128]{2,1,0:T(8,128)S(1)}, f32[4,5,128]{2,1,0:T(8,128)S(1)}, f32[4,5,128,128]{3,2,1,0:T(8,128)}, s32[512]{0:T(512)S(1)}, /*i...) while((s32[]{:T(128)}, f32[4,5,128]{2,1,0:T(8,128)S(1)}, ...), condition=%wide.region_3.4_spmd.clone, body=%wide.region_0.3_spmd.clone.sunk | while | flops 171766528 | bytes 18714888 | solution.py:74
  111.9 1.5 fusion.83
  117.9 1.5 fusion.83
  124.0 1.5 fusion.83
  130.0 1.5 fusion.83
  134.8 2.8 copy.61
  137.6 2.4 multiply_reduce_fusion
  140.1 1.1 broadcast_in_dim.105.clone
  141.2 35.1 %while.35 = (s32[]{:T(128)}, f32[128,4,5,128]{0,3,2,1:T(8,128)}, bf16[512,1024]{1,0:T(8,128)(2,1)}, bf16[512,512]{0,1:T(8,128)(2,1)}, s32[512]{0:T(512)S(1)}, /*...) while((s32[]{:T(128)}, f32[128,4,5,128]{0,3,2,1:T(8,128)}, ...), condition=%wide.region_6.7_spmd.clone, body=%wide.region_5.6_spmd.clone.sunk | while | flops 423805184 | bytes 14670309 | solution.py:108
  147.2 2.3 fusion.98
  153.8 1.1 copy.94
  155.6 2.8 fusion.98
  164.5 2.8 fusion.98
  173.4 2.8 fusion.98
  176.3 22.9 %reduce-scatter.5.cloned.1.call-done = bf16[128,1024]{1,0:T(8,128)(2,1)} async-done(((bf16[512,1024]{1,0:T(8,128)(2,1)}), bf16[128,1024]{1,0:T(8,128)(2,1)}) %reduce-scatter.5.cloned.1.call-update) | async-done | bytes 262160 | tf_op jit(solution)/shard_map/reduce_scatter | solution.py:118
  199.3 4.8 %fusion.32 = bf16[5120,512]{0,1:T(8,128)(2,1)} fusion(bf16[1,128,5120]{2,1,0:T(8,128)(2,1)S(1)} %copy-done, bf16[128,1024]{1,0:T(8,128)(2,1)} %reduce-scatter.5.cloned.1.call-done), kind=kOutput, calls=%fused_computation.52 | convolution fusion | flops 673710080 | bytes 6684672 | tf_op jit(solution)/shard_map/kd,kc->dc/dot_general | solution.py:127
  204.1 8.0 %copy.89 = bf16[5120,512]{1,0:T(8,128)(2,1)} copy(bf16[5120,512]{0,1:T(8,128)(2,1)} %fusion.32) | data formatting | bytes 10485760
  212.1 1.2 copy-done.3
  214.3 2.2 copy.66
  216.6 1.1 copy.65
  218.3 96.5 %reduce-scatter.7.cloned.1.call-done = bf16[640,512]{1,0:T(8,128)(2,1)} async-done(((bf16[5120,512]{1,0:T(8,128)(2,1)}), bf16[640,512]{1,0:T(8,128)(2,1)}) %reduce-scatter.7.cloned.1.call-update) | async-done | bytes 655376
  314.8 2.2 copy.90
  317.0 5.4 %fusion.33 = bf16[1,128,5120]{2,1,0:T(8,128)(2,1)} fusion(bf16[5120,512]{1,0:T(8,128)(2,1)} %all-gather.4.cloned.1.call-done, bf16[128,1024]{1,0:T(8,128)(2,1)S(1)} %copy-done.8), kind=kOutput, calls=%fused_computation.54 | convolution fusion | flops 671744000 | bytes 6684672 | tf_op jit(solution)/shard_map/kc,dc->kd/dot_general | solution.py:123
  322.3 28.9 %all-reduce.2.cloned.1.call-done = bf16[640,512]{0,1:T(8,128)(2,1)} async-done(((bf16[640,512]{0,1:T(8,128)(2,1)}), bf16[640,512]{0,1:T(8,128)(2,1)}) %all-reduce.2.cloned.1.call-update) | async-done | bytes 655376 | tf_op jit(solution)/shard_map/psum | solution.py:134
  351.3 2.4 copy.67
  (201 shorter events, 44.6 us)
Async XLA Ops:
  7.2 92.0 %copy-start = (bf16[1,128,5120]{2,1,0:T(8,128)(2,1)S(1)}, bf16[1,128,5120]{2,1,0:T(8,128)(2,1)}, u32[]{:S(2)}) copy-start(bf16[1,128,5120]{2,1,0:T(8,128)(2,1)} %param.10) | copy-start | bytes 3932164
  7.2 92.0 %all-gather.4.cloned.1.call-start = ((), (), s32[]{:S(2)}) async-start(), calls=%async_computation.2 | async-start | bytes 5898240 | tf_op jit(solution)/shard_map/all_gather | solution.py:19
  7.9 191.4 %reduce-scatter.5.cloned.1.call-start = ((), (), s32[]{:S(2)}) async-start(), calls=%async_computation.3 | async-start | bytes 1310720 | tf_op jit(solution)/shard_map/reduce_scatter | solution.py:118
  8.0 2.6 copy-start.14
  8.0 2.7 copy-start.9
  137.6 3.6 copy-start.5
  141.2 2.3 copy-start.12
  141.2 2.3 copy-start.16
  141.2 2.4 copy-start.10
  147.2 2.3 copy-start.11
  147.2 2.3 copy-start.13
  147.2 2.3 copy-start.17
  147.2 2.3 copy-start.19
  149.6 2.3 copy-start.10
  155.6 2.8 copy-start.11
  155.6 2.8 copy-start.13
  155.6 2.8 copy-start.17
  155.6 2.8 copy-start.19
  158.5 2.3 copy-start.10
  164.5 2.8 copy-start.11
  164.5 2.8 copy-start.13
  164.5 2.8 copy-start.17
  164.5 2.8 copy-start.19
  167.4 2.3 copy-start.10
  173.4 2.8 copy-start.11
  173.4 2.8 copy-start.13
  173.4 2.8 copy-start.17
  173.4 2.8 copy-start.19
  176.3 138.5 %reduce-scatter.7.cloned.1.call-start = ((), (), s32[]{:S(2)}) async-start(), calls=%async_computation.5 | async-start | bytes 5898240
  212.0 139.2 %all-reduce.2.cloned.1.call-start = ((), (), s32[]{:S(2)}) async-start(), calls=%async_computation.4 | async-start | bytes 1310720 | tf_op jit(solution)/shard_map/psum | solution.py:134
  213.3 3.2 copy-start.7
  214.3 3.3 copy-start.8
  (25 other events, 32.3 us)
Sparse Core Ops, SparseCore 0:
  10.2 88.9 all-gather.3
  176.4 22.8 reduce-scatter.4
  212.2 102.5 reduce-scatter.6
  317.7 33.5 all-reduce.1
where the time goes:
time: 362 us; the launch traced here: 360 us
  waiting for transfers between devices  223 us (62%)
  local copies, waits for them, and re-layouts  52.1 us (14%)
  matrix products  40.6 us (11%)
  blocking collectives  21.3 us (6%)
  between operations  13.9 us (4%)
  other arithmetic  8.28 us (2%)
    unnamed x5, waiting for transfers between devices  97.2 us
    all_gather x1, waiting for transfers between devices, body(): full_weight = lax.all_gather(value_weight, 'dp', axis=0, tiled=True)  73.9 us
    psum x1, waiting for transfers between devices, body(): grad_weight = lax.psum(partial_rows, 'seq').astype(jnp.float32)  28.9 us
    reduce_scatter x1, waiting for transfers between devices, body(): lax.psum_scatter(grad_buf.astype(jnp.float32).astype(jnp.bfloat16), 'seq'...  22.9 us
    unnamed x28, local copies, waits for them, and re-layouts  21.1 us
    dot_general x4, matrix products, gradient_update(): jnp.einsum('hgqk,khd->qhgd', dscore, key_tile, preferred_element_type=jnp...  10.7 us
    while x92, local copies, waits for them, and re-layouts  10.6 us
    dot_general x8, matrix products, block_scores(): jnp.einsum('qhgd,khd->hgqk', query_head_rows, key_tile, preferred_element...  8.28 us
  transfers between devices with their start and end apart: 4, of which 4 were waited for; matrix products, arithmetic and copies ran while one was open for 4% of the time, Pallas kernels for 0%

commit v1 on v0

--- a/solution.py
+++ b/solution.py
@@ -1,12 +1,21 @@
+import functools
+
 import jax
 import jax.numpy as jnp
 from jax import lax
+from jax.experimental import pallas as pl
+from jax.experimental.pallas import tpu as pltpu
 from jax.sharding import PartitionSpec as P
 
 QUERY_HEADS = 20
 KEY_VALUE_HEADS = 4
 HEAD_SIZE = 128
 QUERY_PER_KV = 5
+
+BF = jnp.bfloat16
+F32 = jnp.float32
+VM = pl.BlockSpec(memory_space=pltpu.VMEM)
+ANY = pl.BlockSpec(memory_space=pl.ANY)
 
 
 def body(hidden, queries, keys, value_weight, doc_ids, cotangent):
@@ -141,6 +150,403 @@
     )
 
 
+N_DP = 8
+ROWS = 128
+SHARD = 640
+HALF = SHARD // 2
+WINDOW = 384
+PAD = WINDOW - HALF
+WIDE = N_DP * WINDOW
+CORE_KV = 256
+CORE_Q = 1280
+
+
+def params():
+    return pltpu.CompilerParams(vmem_limit_bytes=50 * 1024 * 1024)
+
+
+def cost(flops, nbytes):
+    return pl.CostEstimate(flops=int(flops), bytes_accessed=int(nbytes), transcendentals=0)
+
+
+def sds(shape, dtype=BF):
+    return jax.ShapeDtypeStruct(shape, dtype)
+
+
+def swap(x, axis, k):
+    size = lax.axis_size(axis)
+    return lax.ppermute(x, axis, [(i, i ^ k) for i in range(size)])
+
+
+def weight_part_kernel(w_ref, o_ref, sem):
+    s = lax.axis_index("seq")
+    y, c = s // 2, s % 2
+    copy = pltpu.make_async_copy(
+        w_ref.at[pl.ds(pl.multiple_of(y * HALF, HALF), HALF), pl.ds(pl.multiple_of(c * CORE_KV, CORE_KV), CORE_KV)],
+        o_ref,
+        sem,
+    )
+    copy.start()
+    copy.wait()
+
+
+def weight_part(w):
+    return pl.pallas_call(
+        weight_part_kernel,
+        out_shape=sds((HALF, CORE_KV)),
+        in_specs=[ANY],
+        out_specs=ANY,
+        scratch_shapes=[pltpu.SemaphoreType.DMA],
+        compiler_params=params(),
+        cost_estimate=cost(0, 2 * HALF * CORE_KV * 2),
+    )(w)
+
+
+def hidden_parts_kernel(h_ref, keep_ref, send_ref, sems):
+    s = lax.axis_index("seq")
+    r = lax.axis_index("dp")
+    y = s // 2
+    copies = []
+    for which, (out, part) in enumerate(((send_ref, 1 - y), (keep_ref, y))):
+        for j in range(N_DP):
+            start = pl.multiple_of((r ^ j) * SHARD + part * (SHARD - WINDOW), 128)
+            copies.append(
+                pltpu.make_async_copy(
+                    h_ref.at[:, pl.ds(start, WINDOW)],
+                    out.at[:, pl.ds(j * WINDOW, WINDOW)],
+                    sems.at[which * N_DP + j],
+                )
+            )
+    for copy in copies:
+        copy.start()
+    for copy in copies:
+        copy.wait()
+
+
+def hidden_parts(h):
+    return pl.pallas_call(
+        hidden_parts_kernel,
+        out_shape=(sds((ROWS, WIDE)), sds((ROWS, WIDE))),
+        in_specs=[ANY],
+        out_specs=(ANY, ANY),
+        scratch_shapes=[pltpu.SemaphoreType.DMA((2 * N_DP,))],
+        compiler_params=params(),
+        cost_estimate=cost(0, 4 * ROWS * WIDE * 2),
+    )(h)
+
+
+def values_kernel(h0, h1, h2, h3, w0, w1, w2, w3, w4, w5, w6, w7, vp_ref, wpad_ref):
+    y = lax.axis_index("seq") // 2
+    for j, w in enumerate((w0, w1, w2, w3, w4, w5, w6, w7)):
+        wpad_ref[pl.ds(pl.multiple_of(j * WINDOW + y * PAD, PAD), HALF), :] = w[...]
+        wpad_ref[pl.ds(pl.multiple_of(j * WINDOW + (1 - y) * HALF, PAD), PAD), :] = jnp.zeros((PAD, CORE_KV), BF)
+    for t, h in enumerate((h0, h1, h2, h3)):
+        vp_ref[t * ROWS : (t + 1) * ROWS, :] = jnp.dot(
+            h[...], wpad_ref[...], preferred_element_type=F32
+        ).astype(BF)
+
+
+def partial_values(hs, ws):
+    return pl.pallas_call(
+        values_kernel,
+        out_shape=(sds((4 * ROWS, CORE_KV)), sds((WIDE, CORE_KV))),
+        in_specs=[VM] * 12,
+        out_specs=(VM, VM),
+        compiler_params=params(),
+        cost_estimate=cost(2 * 512 * WIDE * 256, 6e6),
+    )(*hs, *ws)
+
+
+def dot_tt(a, b):
+    return lax.dot_general(a, b, (((0,), (0,)), ((), ())), preferred_element_type=F32)
+
+
+def dot_nt(a, b):
+    return lax.dot_general(a, b, (((1,), (1,)), ((), ())), preferred_element_type=F32)
+
+
+def attention_kernel(
+    q0, q1, g0, g1, k0, k1, k2, k3, vp, rv,
+    o0, o1, dq0, dq1, dv_ref, dk_ref, dks_ref, bias,
+):
+    s = lax.axis_index("seq")
+    c = s % 2
+    factor = HEAD_SIZE ** (-0.5)
+    log2e = 1.4426950408889634
+    ks = (k0, k1, k2, k3)
+    rows = [k[ROWS : ROWS + 16, 0:ROWS][0:1, :].astype(F32) for k in ks]
+    for t in range(4):
+        key_doc = jnp.transpose(jnp.broadcast_to(rows[t], (ROWS, ROWS)))
+        key_pos = (s ^ t) * ROWS + lax.broadcasted_iota(jnp.int32, (ROWS, ROWS), 0)
+        for u in range(2):
+            query_pos = (s ^ u) * ROWS + lax.broadcasted_iota(jnp.int32, (ROWS, ROWS), 1)
+            allow = (key_pos <= query_pos) & (key_doc == jnp.broadcast_to(rows[u], (ROWS, ROWS)))
+            bias[t * ROWS : (t + 1) * ROWS, u * ROWS : (u + 1) * ROWS] = jnp.where(allow, 0.0, -1e30)
+    for kvh in range(2):
+        cols = pl.ds(pl.multiple_of(c * CORE_KV + kvh * HEAD_SIZE, HEAD_SIZE), HEAD_SIZE)
+        mine = slice(kvh * HEAD_SIZE, (kvh + 1) * HEAD_SIZE)
+        key = jnp.concatenate([k[0:ROWS, cols] for k in ks], axis=0)
+        far = rv[:, mine].astype(F32)
+        far = jnp.concatenate([far[2 * ROWS :], far[: 2 * ROWS]], axis=0)
+        value = (vp[:, mine].astype(F32) + far).astype(BF)
+        dk = jnp.zeros((4 * ROWS, HEAD_SIZE), F32)
+        dv = jnp.zeros((4 * ROWS, HEAD_SIZE), F32)
+        for g in range(QUERY_PER_KV):
+            head = kvh * QUERY_PER_KV + g
+            qcols = pl.ds(pl.multiple_of(c * CORE_Q + head * HEAD_SIZE, HEAD_SIZE), HEAD_SIZE)
+            ocols = slice(head * HEAD_SIZE, (head + 1) * HEAD_SIZE)
+            query = jnp.concatenate([q0[:, qcols], q1[:, qcols]], axis=0)
+            cot = jnp.concatenate([g0[:, qcols], g1[:, qcols]], axis=0)
+            st = dot_nt(key, query) * (factor * log2e) + bias[...]
+            peak = jnp.max(st, axis=0, keepdims=True)
+            e = jnp.exp2(st - peak)
+            inv = 1.0 / jnp.sum(e, axis=0, keepdims=True)
+            out_t = dot_tt(value, e.astype(BF)) * inv
+            out = jnp.transpose(out_t).astype(BF)
+            o0[:, ocols] = out[:ROWS]
+            o1[:, ocols] = out[ROWS:]
+            probs = e * inv
+            dprob = dot_nt(value, cot)
+            term = probs * dprob
+            delta = jnp.sum(term, axis=0, keepdims=True)
+            ds = (term - probs * delta).astype(BF)
+            dq = jnp.transpose(dot_tt(key, ds) * factor).astype(BF)
+            dq0[:, ocols] = dq[:ROWS]
+            dq1[:, ocols] = dq[ROWS:]
+            dk = dk + jnp.dot(ds, query, preferred_element_type=F32)
+            dv = dv + jnp.dot(probs.astype(BF), cot, preferred_element_type=F32)
+        dk = (dk * factor).astype(BF)
+        dk_ref[:, mine] = dk[: 2 * ROWS]
+        dks_ref[:, mine] = dk[2 * ROWS :]
+        dv_ref[:, mine] = dv.astype(BF)
+
+
+def attention(q, qs, g, gs, ks, vp, rv):
+    return pl.pallas_call(
+        attention_kernel,
+        out_shape=(sds((ROWS, CORE_Q)),) * 4
+        + (sds((4 * ROWS, CORE_KV)), sds((2 * ROWS, CORE_KV)), sds((2 * ROWS, CORE_KV))),
+        in_specs=[VM] * 10,
+        out_specs=(VM,) * 7,
+        scratch_shapes=[pltpu.VMEM((4 * ROWS, 2 * ROWS), F32)],
+        compiler_params=params(),
+        cost_estimate=cost(2 * 6 * 10 * 256 * 512 * 128 * 4, 6e6),
+    )(q, qs, g, gs, *ks, vp, rv)
+
+
+def weight_grad_kernel(dv, rdv, h0, h1, h2, h3, own_a, own_b, send_a, send_b, gv_keep, gv_send, gv):
+    for t in range(4):
+        a = dv[t * ROWS : (t + 1) * ROWS, :].astype(F32)
+        b = rdv[(t ^ 2) * ROWS : ((t ^ 2) + 1) * ROWS, :].astype(F32)
+        total = (a + b).astype(BF)
+        gv[t * ROWS : (t + 1) * ROWS, :] = total
+        half = (t // 2) * ROWS
+        if t % 2 == 0:
+            gv_keep[half : half + ROWS, :] = total
+        else:
+            gv_send[half : half + ROWS, :] = total
+    y = lax.axis_index("seq") // 2
+    for j, (out, place) in (
+        (5, (send_a, 0)), (7, (send_a, 1)), (4, (own_a, 0)), (6, (own_a, 1)),
+        (1, (send_b, 0)), (3, (send_b, 1)), (0, (own_b, 0)), (2, (own_b, 1)),
+    ):
+        acc = jnp.zeros((WINDOW, CORE_KV), F32)
+        for t, h in enumerate((h0, h1, h2, h3)):
+            acc = acc + dot_tt(h[:, j * WINDOW : (j + 1) * WINDOW], gv[t * ROWS : (t + 1) * ROWS, :])
+        part = jnp.where(y == 0, acc[:HALF], acc[PAD:])
+        out[place * HALF : (place + 1) * HALF, :] = part.astype(BF)
+
+
+def weight_grad(dv, rdv, hs):
+    return pl.pallas_call(
+        weight_grad_kernel,
+        out_shape=(sds((2 * HALF, CORE_KV)),) * 4 + (sds((2 * ROWS, CORE_KV)),) * 2,
+        in_specs=[VM] * 6,
+        out_specs=(VM,) * 6,
+        scratch_shapes=[pltpu.VMEM((4 * ROWS, CORE_KV), BF)],
+        compiler_params=params(),
+        cost_estimate=cost(2 * 512 * WIDE * 256, 6e6),
+    )(dv, rdv, *hs)
+
+
+def hidden_grad_kernel(gv, gvs, wp, wps, gh0, gh2):
+    full = dot_nt(gv[...], wp[...]) + dot_nt(gvs[...], wps[...])
+    full = full.astype(BF)
+    gh0[...] = full[:ROWS]
+    gh2[...] = full[ROWS:]
+
+
+def hidden_grad(gv, gvs, wp, wps):
+    return pl.pallas_call(
+        hidden_grad_kernel,
+        out_shape=(sds((ROWS, WIDE)),) * 2,
+        in_specs=[VM] * 4,
+        out_specs=(VM,) * 2,
+        compiler_params=params(),
+        cost_estimate=cost(2 * 256 * WIDE * 512, 6e6),
+    )(gv, gvs, wp, wps)
+
+
+def hidden_join_kernel(own_ref, far_ref, o_ref):
+    y = lax.axis_index("seq") // 2
+    r = lax.axis_index("dp")
+    for j in range(N_DP):
+        own = own_ref[:, j * WINDOW : (j + 1) * WINDOW]
+        far = far_ref[:, j * WINDOW : (j + 1) * WINDOW]
+        low = jnp.where(y == 0, own, far)
+        high = jnp.where(y == 0, far, own)
+        base = pl.multiple_of((r ^ j) * SHARD, 128)
+        o_ref[:, pl.ds(base, 256)] = low[:, :256]
+        o_ref[:, pl.ds(pl.multiple_of(base + 256, 128), 128)] = low[:, 256:] + high[:, :128]
+        o_ref[:, pl.ds(pl.multiple_of(base + 384, 128), 256)] = high[:, 128:]
+
+
+def hidden_join(own, far):
+    return pl.pallas_call(
+        hidden_join_kernel,
+        out_shape=sds((ROWS, N_DP * SHARD)),
+        in_specs=[VM] * 2,
+        out_specs=VM,
+        compiler_params=params(),
+        cost_estimate=cost(0, 3e6),
+    )(own, far)
+
+
+def add_pair_kernel(a, b, o0, o1):
+    total = (a[...].astype(F32) + b[...].astype(F32)).astype(BF)
+    o0[...] = total[:HALF]
+    o1[...] = total[HALF:]
+
+
+def add_pair(a, b):
+    return pl.pallas_call(
+        add_pair_kernel,
+        out_shape=(sds((HALF, CORE_KV)),) * 2,
+        in_specs=[VM] * 2,
+        out_specs=(VM,) * 2,
+        compiler_params=params(),
+        cost_estimate=cost(0, 1e6),
+    )(a, b)
+
+
+def add_four_kernel(a, b, c, d, o):
+    o[...] = (
+        (a[...].astype(F32) + b[...].astype(F32)) + (c[...].astype(F32) + d[...].astype(F32))
+    ).astype(BF)
+
+
+def add_four(a, b, c, d):
+    return pl.pallas_call(
+        add_four_kernel,
+        out_shape=sds((HALF, CORE_KV)),
+        in_specs=[VM] * 4,
+        out_specs=VM,
+        compiler_params=params(),
+        cost_estimate=cost(0, 1e6),
+    )(a, b, c, d)
+
+
+def weight_join_kernel(p0, p1, p2, p3, o_ref):
+    s = lax.axis_index("seq")
+    for t, p in enumerate((p0, p1, p2, p3)):
+        owner = s ^ t
+        o_ref[
+            pl.ds(pl.multiple_of((owner // 2) * HALF, HALF), HALF),
+            pl.ds(pl.multiple_of((owner % 2) * CORE_KV, CORE_KV), CORE_KV),
+        ] = p[...].astype(F32)
+
+
+def weight_join(ps):
+    return pl.pallas_call(
+        weight_join_kernel,
+        out_shape=sds((SHARD, 2 * CORE_KV), F32),
+        in_specs=[VM] * 4,
+        out_specs=VM,
+        compiler_params=params(),
+        cost_estimate=cost(0, 2e6),
+    )(*ps)
+
+
+def heads_join_kernel(a0, a1, b0, b1, c0, c1, oa, ob, oc):
+    c = lax.axis_index("seq") % 2
+    for near, far, out in ((a0, a1, oa), (b0, b1, ob), (c0, c1, oc)):
+        width = near.shape[1]
+        out[:, pl.ds(pl.multiple_of(c * width, 128), width)] = near[...]
+        out[:, pl.ds(pl.multiple_of((1 - c) * width, 128), width)] = far[...]
+
+
+def heads_join(*parts):
+    return pl.pallas_call(
+        heads_join_kernel,
+        out_shape=tuple(sds((ROWS, 2 * p.shape[1])) for p in parts[::2]),
+        in_specs=[VM] * 6,
+        out_specs=(VM,) * 3,
+        compiler_params=params(),
+        cost_estimate=cost(0, 4e6),
+    )(*parts)
+
+
+def paired_body(hidden, queries, keys, value_weight, doc_ids, cotangent):
+    h, q, g = hidden[0], queries[0], cotangent[0]
+    w0 = weight_part(value_weight)
+    w2, w4, w6 = swap(w0, "dp", 2), swap(w0, "dp", 4), swap(w0, "dp", 6)
+    w1 = swap(w0, "dp", 1)
+    w3 = swap(w2, "dp", 1)
+    w5, w7 = swap(w4, "dp", 1), swap(w6, "dp", 1)
+    h0, h_send = hidden_parts(h)
+    h2 = swap(h_send, "seq", 2)
+    h1 = swap(h0, "seq", 1)
+    h3 = swap(h2, "seq", 1)
+    doc_row = jnp.pad(doc_ids.astype(BF), ((0, 15), (0, keys.shape[2] - ROWS)))
+    k0 = jnp.concatenate([keys[0], doc_row], axis=0)
+    k2 = swap(k0, "seq", 2)
+    k1, k3 = swap(k0, "seq", 1), swap(k2, "seq", 1)
+    qs, gs = swap(q, "seq", 1), swap(g, "seq", 1)
+
+    vp, wpad = partial_values((h0, h1, h2, h3), (w0, w1, w2, w3, w4, w5, w6, w7))
+    rv = swap(vp, "seq", 2)
+    wpad_s = swap(wpad, "seq", 1)
+    o0, o1, dq0, dq1, dv, dk0, dk_send = attention(q, qs, g, gs, (k0, k1, k2, k3), vp, rv)
+    rdv = swap(dv, "seq", 2)
+    own_a, own_b, send_a, send_b, gv, gv_send = weight_grad(dv, rdv, (h0, h1, h2, h3))
+    far_a = swap(send_a, "dp", 1)
+    far_b = swap(send_b, "dp", 1)
+    gvs = swap(gv_send, "seq", 1)
+    gh0, gh2 = hidden_grad(gv, gvs, wpad, wpad_s)
+    s4, s6 = add_pair(own_a, far_a)
+    t6, t4 = swap(s6, "dp", 6), swap(s4, "dp", 4)
+    s0, s2 = add_pair(own_b, far_b)
+    t2 = swap(s2, "dp", 2)
+    gh_far = swap(gh2, "seq", 2)
+    dk_far = swap(dk_send, "seq", 2)
+    dk_a, dk_b = add_dk(dk0, dk_far)
+    oc, dqc, dkc = swap(o1, "seq", 1), swap(dq1, "seq", 1), swap(dk_b, "seq", 1)
+    attn_out, grad_queries, grad_keys = heads_join(o0, oc, dq0, dqc, dk_a, dkc)
+    grad_hidden = hidden_join(gh0, gh_far)
+    p0 = add_four(s0, t2, t4, t6)
+    p2 = swap(p0, "seq", 2)
+    p1, p3 = swap(p0, "seq", 1), swap(p2, "seq", 1)
+    grad_weight = weight_join((p0, p1, p2, p3))
+    return attn_out[None], grad_queries[None], grad_keys[None], grad_hidden[None], grad_weight
+
+
+def add_dk_kernel(a, b, o0, o1):
+    total = (a[...].astype(F32) + b[...].astype(F32)).astype(BF)
+    o0[...] = total[:ROWS]
+    o1[...] = total[ROWS:]
+
+
+def add_dk(a, b):
+    return pl.pallas_call(
+        add_dk_kernel,
+        out_shape=(sds((ROWS, CORE_KV)),) * 2,
+        in_specs=[VM] * 2,
+        out_specs=(VM,) * 2,
+        compiler_params=params(),
+        cost_estimate=cost(0, 1e6),
+    )(a, b)
+
+
 def solution(mesh):
     in_specs = (
         P("dp", "seq", None),
@@ -157,4 +563,7 @@
         P("dp", "seq", None),
         P("dp", None),
     )
-    return jax.shard_map(body, mesh=mesh, in_specs=in_specs, out_specs=out_specs, check_vma=False)
+    paired = mesh.shape["dp"] == N_DP and mesh.shape["seq"] == 4
+    return jax.shard_map(
+        paired_body if paired else body, mesh=mesh, in_specs=in_specs, out_specs=out_specs, check_vma=False
+    )

time: 362 us -> 134 us (0.37)
  waiting for transfers between devices: 223 us -> 81.6 us
  local copies, waits for them, and re-layouts: 52.1 us -> 3.36 us
  matrix products: 40.6 us -> 0 us
  starting transfers between devices: 0.16 us -> 23.9 us
  Pallas kernels: 0 us -> 23.5 us
  blocking collectives: 21.3 us -> 0 us
  between operations: 13.9 us -> 0.79 us
  other arithmetic: 8.28 us -> 0.02 us
    unnamed x5 -> x0, waiting for transfers between devices: 97.2 us -> none
    ppermute x0 -> x32, waiting for transfers between devices: none -> 81.6 us  [swap(): return lax.ppermute(x, axis, [(i, i ^ k) for i in range(size)])]
    all_gather x1 -> x0, waiting for transfers between devices: 73.9 us -> none  [body(): full_weight = lax.all_gather(value_weight, 'dp', axis=0, tiled=True)]
    dot_general x31 -> x0, matrix products: 40.6 us -> none  [the longest x4 10.7 us: gradient_update(): jnp.einsum('hgqk,khd->qhgd', dscore, key_tile, preferred_element_type=jnp...]
    psum x1 -> x0, waiting for transfers between devices: 28.9 us -> none  [body(): grad_weight = lax.psum(partial_rows, 'seq').astype(jnp.float32)]
    ppermute x0 -> x32, starting transfers between devices: none -> 23.9 us  [swap(): return lax.ppermute(x, axis, [(i, i ^ k) for i in range(size)])]
    pallas_call x0 -> x13, Pallas kernels: none -> 23.5 us  [the longest x1 10.6 us: attention(): pl.pallas_call(attention_kernel, out_shape=(sds((ROWS, CORE_Q)),) * 4 + (...]
    reduce_scatter x1 -> x0, waiting for transfers between devices: 22.9 us -> none  [body(): lax.psum_scatter(grad_buf.astype(jnp.float32).astype(jnp.bfloat16), 'seq'...]
  transfers between devices with their start and end apart: 4 -> 32, of which waited for: 4 -> 16; matrix products, arithmetic and copies ran while one was open for 4% -> 0% of each run, Pallas kernels for 0% -> 16%
where the time goes in v1:
time: 134 us; the launch traced here: 133 us
  waiting for transfers between devices  81.6 us (61%)
  starting transfers between devices  23.9 us (18%)
  Pallas kernels  23.5 us (18%)
  local copies, waits for them, and re-layouts  3.36 us (3%)
    ppermute x32, waiting for transfers between devices, swap(): return lax.ppermute(x, axis, [(i, i ^ k) for i in range(size)])  81.6 us
    ppermute x32, starting transfers between devices, swap(): return lax.ppermute(x, axis, [(i, i ^ k) for i in range(size)])  23.9 us
    pallas_call x1, Pallas kernels, attention(): pl.pallas_call(attention_kernel, out_shape=(sds((ROWS, CORE_Q)),) * 4 + (...  10.6 us
    unnamed x24, local copies, waits for them, and re-layouts  3.36 us
    pallas_call x1, Pallas kernels, weight_grad(): pl.pallas_call(weight_grad_kernel, out_shape=(sds((2 * HALF, CORE_KV)),)...  3.19 us
    pallas_call x1, Pallas kernels, partial_values(): pl.pallas_call(values_kernel, out_shape=(sds((4 * ROWS, CORE_KV)), sds((W...  2.86 us
  transfers between devices with their start and end apart: 32, of which 16 were waited for; matrix products, arithmetic and copies ran while one was open for 0% of the time, Pallas kernels for 16%

profile of v1, /device:TPU:0, one launch (start us, length us, event | category | flops | bytes accessed | tf_op | source)
XLA Modules:
  0.0 133.2 jit_solution(755959662369099539)
XLA Ops:
  0.7 1.3 copy-done.2
  2.4 3.0 %collective-permute-start.6 = (bf16[128,3072]{1,0:T(8,128)(2,1)S(1)}, bf16[128,3072]{1,0:T(8,128)(2,1)S(1)}, u32[]{:S(2)}, u32[]{:S(2)}) collective-permute-start(bf16[128,3072]{1,0:T(8,128)(2,1)S(1)} %get-tuple-element.34), channel_id=1, source_target_pairs={{0,2},{1,3},{2,0},{3,1},{4,6},{5,7},{6,4},{7,5},{8,10},{9,11},{10,... | collective-permute-start | bytes 2359304 | tf_op jit(solution)/shard_map/ppermute | solution.py:178
  5.5 17.5 %collective-permute-done.6.h2 = bf16[128,3072]{1,0:T(8,128)(2,1)S(1)} collective-permute-done((bf16[128,3072]{1,0:T(8,128)(2,1)S(1)}, bf16[128,3072]{1,0:T(8,128)(2,1)S(1)}, u32[]{:S(2)}, u32[]{:S(2)}) %collective-permute-start.6) | collective-permute-done | bytes 786464 | tf_op jit(solution)/shard_map/ppermute | solution.py:178
  23.1 3.9 %collective-permute-start.13 = (bf16[320,256]{1,0:T(8,128)(2,1)S(1)}, bf16[320,256]{1,0:T(8,128)(2,1)S(1)}, u32[]{:S(2)}, u32[]{:S(2)}) collective-permute-start(bf16[320,256]{1,0:T(8,128)(2,1)S(1)} %shard_map.102.w0), channel_id=1, source_target_pairs={{0,24},{4,28},{8,16},{12,20},{16,8},{20,12},{24,0},{28,4},{1,25},{... | collective-permute-start | bytes 491528 | tf_op jit(solution)/shard_map/ppermute | solution.py:178
  27.6 4.6 %collective-permute-done.13.w6 = bf16[320,256]{1,0:T(8,128)(2,1)S(1)} collective-permute-done((bf16[320,256]{1,0:T(8,128)(2,1)S(1)}, bf16[320,256]{1,0:T(8,128)(2,1)S(1)}, u32[]{:S(2)}, u32[]{:S(2)}) %collective-permute-start.13) | collective-permute-done | bytes 163872 | tf_op jit(solution)/shard_map/ppermute | solution.py:178
  32.1 1.6 %collective-permute-start.8 = (bf16[320,256]{1,0:T(8,128)(2,1)S(1)}, bf16[320,256]{1,0:T(8,128)(2,1)S(1)}, u32[]{:S(2)}, u32[]{:S(2)}) collective-permute-start(bf16[320,256]{1,0:T(8,128)(2,1)S(1)} %shard_map.102.w0), channel_id=1, source_target_pairs={{0,4},{4,0},{8,12},{12,8},{16,20},{20,16},{24,28},{28,24},{1,5},{5... | collective-permute-start | bytes 491528 | tf_op jit(solution)/shard_map/ppermute | solution.py:178
  33.8 7.7 %collective-permute-done.11.w4 = bf16[320,256]{1,0:T(8,128)(2,1)S(1)} collective-permute-done((bf16[320,256]{1,0:T(8,128)(2,1)S(1)}, bf16[320,256]{1,0:T(8,128)(2,1)S(1)}, u32[]{:S(2)}, u32[]{:S(2)}) %collective-permute-start.11) | collective-permute-done | bytes 163872 | tf_op jit(solution)/shard_map/ppermute | solution.py:178
  41.5 1.5 %collective-permute-start.14 = (bf16[320,256]{1,0:T(8,128)(2,1)S(1)}, bf16[320,256]{1,0:T(8,128)(2,1)S(1)}, u32[]{:S(2)}, u32[]{:S(2)}) collective-permute-start(bf16[320,256]{1,0:T(8,128)(2,1)S(1)} %collective-permute-done.13.w6), channel_id=1, source_target_pairs={{0,4},{4,0},{8,12},{12,8},{16,20},{20,16},{24,28},{28,24},{1,5},{5... | collective-permute-start | bytes 491528 | tf_op jit(solution)/shard_map/ppermute | solution.py:178
  43.5 5.1 %collective-permute-done.14.w7 = bf16[320,256]{1,0:T(8,128)(2,1)S(1)} collective-permute-done((bf16[320,256]{1,0:T(8,128)(2,1)S(1)}, bf16[320,256]{1,0:T(8,128)(2,1)S(1)}, u32[]{:S(2)}, u32[]{:S(2)}) %collective-permute-start.14) | collective-permute-done | bytes 163872 | tf_op jit(solution)/shard_map/ppermute | solution.py:178
  48.6 2.2 %collective-permute-done.12.w5 = bf16[320,256]{1,0:T(8,128)(2,1)S(1)} collective-permute-done((bf16[320,256]{1,0:T(8,128)(2,1)S(1)}, bf16[320,256]{1,0:T(8,128)(2,1)S(1)}, u32[]{:S(2)}, u32[]{:S(2)}) %collective-permute-start.12) | collective-permute-done | bytes 163872 | tf_op jit(solution)/shard_map/ppermute | solution.py:178
  50.8 1.5 %collective-permute-start.10 = (bf16[320,256]{1,0:T(8,128)(2,1)S(1)}, bf16[320,256]{1,0:T(8,128)(2,1)S(1)}, u32[]{:S(2)}, u32[]{:S(2)}) collective-permute-start(bf16[320,256]{1,0:T(8,128)(2,1)S(1)} %collective-permute-done.9.w2), channel_id=1, source_target_pairs={{0,4},{4,0},{8,12},{12,8},{16,20},{20,16},{24,28},{28,24},{1,5},{5... | collective-permute-start | bytes 491528 | tf_op jit(solution)/shard_map/ppermute | solution.py:178
  52.3 3.8 %collective-permute-done.10.w3 = bf16[320,256]{1,0:T(8,128)(2,1)S(1)} collective-permute-done((bf16[320,256]{1,0:T(8,128)(2,1)S(1)}, bf16[320,256]{1,0:T(8,128)(2,1)S(1)}, u32[]{:S(2)}, u32[]{:S(2)}) %collective-permute-start.10) | collective-permute-done | bytes 163872 | tf_op jit(solution)/shard_map/ppermute | solution.py:178
  56.1 1.5 %collective-permute-start.3 = (bf16[144,512]{1,0:T(8,128)(2,1)S(1)}, bf16[144,512]{1,0:T(8,128)(2,1)S(1)}, u32[]{:S(2)}, u32[]{:S(2)}) collective-permute-start(bf16[144,512]{1,0:T(8,128)(2,1)S(1)} %fusion.1.k0), channel_id=1, source_target_pairs={{0,2},{1,3},{2,0},{3,1},{4,6},{5,7},{6,4},{7,5},{8,10},{9,11},{10,... | collective-permute-start | bytes 442376 | tf_op jit(solution)/shard_map/ppermute | solution.py:178
  58.5 2.9 %shard_map.103 = (bf16[512,256]{1,0:T(8,128)(2,1)S(1)}, bf16[3072,256]{1,0:T(8,128)(2,1)}) custom-call(bf16[128,3072]{1,0:T(8,128)(2,1)S(1)} %get-tuple-element.33.h0, bf16[128,3072]{1,0:T(8,128)(2,1)S(1)} %collective-permute-done.5.h1, bf16[128,3072]{1,0:T(8,128)(2,1)S(1)} %collective-permute-done.6.h2, bf16[128,3072]{1,0:T(8,128)(2,1)} %copy-done.5, ...), custom_call_target="tpu_custom_call" | custom-call | flops 805306368 | bytes 6000000 | tf_op jit(solution)/shard_map/pallas_call | solution.py:250
  62.8 1.9 %collective-permute-done.2.k1 = bf16[144,512]{1,0:T(8,128)(2,1)S(1)} collective-permute-done((bf16[144,512]{1,0:T(8,128)(2,1)S(1)}, bf16[144,512]{1,0:T(8,128)(2,1)S(1)}, u32[]{:S(2)}, u32[]{:S(2)}) %collective-permute-start.2) | collective-permute-done | bytes 147488 | tf_op jit(solution)/shard_map/ppermute | solution.py:178
  66.0 4.1 %collective-permute-done.15.rv = bf16[512,256]{1,0:T(8,128)(2,1)S(1)} collective-permute-done((bf16[512,256]{1,0:T(8,128)(2,1)S(1)}, bf16[512,256]{1,0:T(8,128)(2,1)S(1)}, u32[]{:S(2)}, u32[]{:S(2)}) %collective-permute-start.15) | collective-permute-done | bytes 262176 | tf_op jit(solution)/shard_map/ppermute | solution.py:178
  70.1 10.6 %shard_map.104 = (bf16[128,1280]{1,0:T(8,128)(2,1)S(1)}, bf16[128,1280]{1,0:T(8,128)(2,1)S(1)}, bf16[128,1280]{1,0:T(8,128)(2,1)S(1)}, bf16[128,1280]{1,0:T(8,12...) custom-call(bf16[128,2560]{1,0:T(8,128)(2,1)S(1)} %bitcast.10, ...), custom_call_target="tpu_custom_call" | custom-call | flops 8053063680 | bytes 6000000 | tf_op jit(solution)/shard_map/pallas_call | solution.py:325
  81.4 6.9 %collective-permute-done.20.rdv = bf16[512,256]{1,0:T(8,128)(2,1)S(1)} collective-permute-done((bf16[512,256]{1,0:T(8,128)(2,1)S(1)}, bf16[512,256]{1,0:T(8,128)(2,1)S(1)}, u32[]{:S(2)}, u32[]{:S(2)}) %collective-permute-start.20) | collective-permute-done | bytes 262176 | tf_op jit(solution)/shard_map/ppermute | solution.py:178
  88.2 3.2 %shard_map.107 = (bf16[640,256]{1,0:T(8,128)(2,1)S(1)}, bf16[640,256]{1,0:T(8,128)(2,1)S(1)}, bf16[640,256]{1,0:T(8,128)(2,1)S(1)}, bf16[640,256]{1,0:T(8,128)(2...) custom-call(bf16[512,256]{1,0:T(8,128)(2,1)S(1)} %get-tuple-element.47.dv, ...), custom_call_target="tpu_custom_call" | custom-call | flops 805306368 | bytes 6000000 | tf_op jit(solution)/shard_map/pallas_call | solution.py:361
  91.5 1.6 %collective-permute-start.24 = (bf16[640,256]{1,0:T(8,128)(2,1)S(1)}, bf16[640,256]{1,0:T(8,128)(2,1)S(1)}, u32[]{:S(2)}, u32[]{:S(2)}) collective-permute-start(bf16[640,256]{1,0:T(8,128)(2,1)S(1)} %get-tuple-element.54), channel_id=1, source_target_pairs={{0,4},{4,0},{8,12},{12,8},{16,20},{20,16},{24,28},{28,24},{1,5},{5... | collective-permute-start | bytes 983048 | tf_op jit(solution)/shard_map/ppermute | solution.py:178
  93.6 1.1 copy-done.6
  94.7 2.4 %shard_map.108 = (bf16[128,3072]{1,0:T(8,128)(2,1)S(1)}, bf16[128,3072]{1,0:T(8,128)(2,1)S(1)}) custom-call(bf16[256,256]{1,0:T(8,128)(2,1)S(1)} %get-tuple-element.48.gv, bf16[256,256]{1,0:T(8,128)(2,1)S(1)} %collective-permute-done.21.gvs, bf16[3072,256]{1,0:T(8,128)(2,1)S(1)} %copy-done.1, bf16[3072,256]{1,0:T(8,128)(2,1)} %copy-done.6), custom_call_target="tpu_custom_call" | custom-call | flops 805306368 | bytes 6000000 | tf_op jit(solution)/shard_map/pallas_call | solution.py:380
  97.5 4.6 %collective-permute-done.24.b = bf16[640,256]{1,0:T(8,128)(2,1)S(1)} collective-permute-done((bf16[640,256]{1,0:T(8,128)(2,1)S(1)}, bf16[640,256]{1,0:T(8,128)(2,1)S(1)}, u32[]{:S(2)}, u32[]{:S(2)}) %collective-permute-start.24) | collective-permute-done | bytes 327712 | tf_op jit(solution)/shard_map/ppermute | solution.py:178
  102.8 5.9 %collective-permute-done.26.b = bf16[640,256]{1,0:T(8,128)(2,1)S(1)} collective-permute-done((bf16[640,256]{1,0:T(8,128)(2,1)S(1)}, bf16[640,256]{1,0:T(8,128)(2,1)S(1)}, u32[]{:S(2)}, u32[]{:S(2)}) %collective-permute-start.26) | collective-permute-done | bytes 327712 | tf_op jit(solution)/shard_map/ppermute | solution.py:178
  108.7 1.6 %collective-permute-start.27 = (bf16[320,256]{1,0:T(8,128)(2,1)S(1)}, bf16[320,256]{1,0:T(8,128)(2,1)S(1)}, u32[]{:S(2)}, u32[]{:S(2)}) collective-permute-start(bf16[320,256]{1,0:T(8,128)(2,1)S(1)} %get-tuple-element.59), channel_id=1, source_target_pairs={{0,16},{4,20},{8,24},{12,28},{16,0},{20,4},{24,8},{28,12},{1,17},{... | collective-permute-start | bytes 491528 | tf_op jit(solution)/shard_map/ppermute | solution.py:178
  110.4 1.3 %collective-permute-start.28 = (bf16[320,256]{1,0:T(8,128)(2,1)S(1)}, bf16[320,256]{1,0:T(8,128)(2,1)S(1)}, u32[]{:S(2)}, u32[]{:S(2)}) collective-permute-start(bf16[320,256]{1,0:T(8,128)(2,1)S(1)} %get-tuple-element.60), channel_id=1, source_target_pairs={{0,24},{4,28},{8,16},{12,20},{16,8},{20,12},{24,0},{28,4},{1,25},{... | collective-permute-start | bytes 491528 | tf_op jit(solution)/shard_map/ppermute | solution.py:178
  112.0 10.6 %collective-permute-done.27.c = bf16[320,256]{1,0:T(8,128)(2,1)S(1)} collective-permute-done((bf16[320,256]{1,0:T(8,128)(2,1)S(1)}, bf16[320,256]{1,0:T(8,128)(2,1)S(1)}, u32[]{:S(2)}, u32[]{:S(2)}) %collective-permute-start.27) | collective-permute-done | bytes 163872 | tf_op jit(solution)/shard_map/ppermute | solution.py:178
  123.4 1.0 collective-permute-done.19.c1
  124.6 4.7 %collective-permute-done.30.p2 = bf16[320,256]{1,0:T(8,128)(2,1)S(1)} collective-permute-done((bf16[320,256]{1,0:T(8,128)(2,1)S(1)}, bf16[320,256]{1,0:T(8,128)(2,1)S(1)}, u32[]{:S(2)}, u32[]{:S(2)}) %collective-permute-start.30) | collective-permute-done | bytes 163872 | tf_op jit(solution)/shard_map/ppermute | solution.py:178
  129.4 1.2 shard_map.106
  130.7 1.2 shard_map.113
  131.9 1.3 shard_map.109
  (71 shorter events, 9.2 us)
Async XLA Ops:
  2.4 20.6 %collective-permute-start.6 = (bf16[128,3072]{1,0:T(8,128)(2,1)S(1)}, bf16[128,3072]{1,0:T(8,128)(2,1)S(1)}, u32[]{:S(2)}, u32[]{:S(2)}) collective-permute-start(bf16[128,3072]{1,0:T(8,128)(2,1)S(1)} %get-tuple-element.34), channel_id=1, source_target_pairs={{0,2},{1,3},{2,0},{3,1},{4,6},{5,7},{6,4},{7,5},{8,10},{9,11},{10,... | collective-permute-start | bytes 2359304 | tf_op jit(solution)/shard_map/ppermute | solution.py:178
  5.5 52.2 %collective-permute-start.5 = (bf16[128,3072]{1,0:T(8,128)(2,1)S(1)}, bf16[128,3072]{1,0:T(8,128)(2,1)S(1)}, u32[]{:S(2)}, u32[]{:S(2)}) collective-permute-start(bf16[128,3072]{1,0:T(8,128)(2,1)S(1)} %get-tuple-element.33.h0), channel_id=1, source_target_pairs={{0,1},{1,0},{2,3},{3,2},{4,5},{5,4},{6,7},{7,6},{8,9},{9,8},{10,11... | collective-permute-start | bytes 2359304 | tf_op jit(solution)/shard_map/ppermute | solution.py:178
  23.0 34.6 %collective-permute-start.7 = (bf16[128,3072]{1,0:T(8,128)(2,1)S(1)}, bf16[128,3072]{1,0:T(8,128)(2,1)S(1)}, u32[]{:S(2)}, u32[]{:S(2)}) collective-permute-start(bf16[128,3072]{1,0:T(8,128)(2,1)S(1)} %collective-permute-done.6.h2), channel_id=1, source_target_pairs={{0,1},{1,0},{2,3},{3,2},{4,5},{5,4},{6,7},{7,6},{8,9},{9,8},{10,11... | collective-permute-start | bytes 2359304 | tf_op jit(solution)/shard_map/ppermute | solution.py:178
  23.1 9.1 %collective-permute-start.13 = (bf16[320,256]{1,0:T(8,128)(2,1)S(1)}, bf16[320,256]{1,0:T(8,128)(2,1)S(1)}, u32[]{:S(2)}, u32[]{:S(2)}) collective-permute-start(bf16[320,256]{1,0:T(8,128)(2,1)S(1)} %shard_map.102.w0), channel_id=1, source_target_pairs={{0,24},{4,28},{8,16},{12,20},{16,8},{20,12},{24,0},{28,4},{1,25},{... | collective-permute-start | bytes 491528 | tf_op jit(solution)/shard_map/ppermute | solution.py:178
  26.9 14.5 %collective-permute-start.11 = (bf16[320,256]{1,0:T(8,128)(2,1)S(1)}, bf16[320,256]{1,0:T(8,128)(2,1)S(1)}, u32[]{:S(2)}, u32[]{:S(2)}) collective-permute-start(bf16[320,256]{1,0:T(8,128)(2,1)S(1)} %shard_map.102.w0), channel_id=1, source_target_pairs={{0,16},{4,20},{8,24},{12,28},{16,0},{20,4},{24,8},{28,12},{1,17},{... | collective-permute-start | bytes 491528 | tf_op jit(solution)/shard_map/ppermute | solution.py:178
  27.0 16.0 %collective-permute-start.9 = (bf16[320,256]{1,0:T(8,128)(2,1)S(1)}, bf16[320,256]{1,0:T(8,128)(2,1)S(1)}, u32[]{:S(2)}, u32[]{:S(2)}) collective-permute-start(bf16[320,256]{1,0:T(8,128)(2,1)S(1)} %shard_map.102.w0), channel_id=1, source_target_pairs={{0,8},{4,12},{8,0},{12,4},{16,24},{20,28},{24,16},{28,20},{1,9},{5... | collective-permute-start | bytes 491528 | tf_op jit(solution)/shard_map/ppermute | solution.py:178
  32.1 11.4 %collective-permute-start.8 = (bf16[320,256]{1,0:T(8,128)(2,1)S(1)}, bf16[320,256]{1,0:T(8,128)(2,1)S(1)}, u32[]{:S(2)}, u32[]{:S(2)}) collective-permute-start(bf16[320,256]{1,0:T(8,128)(2,1)S(1)} %shard_map.102.w0), channel_id=1, source_target_pairs={{0,4},{4,0},{8,12},{12,8},{16,20},{20,16},{24,28},{28,24},{1,5},{5... | collective-permute-start | bytes 491528 | tf_op jit(solution)/shard_map/ppermute | solution.py:178
  41.5 7.1 %collective-permute-start.14 = (bf16[320,256]{1,0:T(8,128)(2,1)S(1)}, bf16[320,256]{1,0:T(8,128)(2,1)S(1)}, u32[]{:S(2)}, u32[]{:S(2)}) collective-permute-start(bf16[320,256]{1,0:T(8,128)(2,1)S(1)} %collective-permute-done.13.w6), channel_id=1, source_target_pairs={{0,4},{4,0},{8,12},{12,8},{16,20},{20,16},{24,28},{28,24},{1,5},{5... | collective-permute-start | bytes 491528 | tf_op jit(solution)/shard_map/ppermute | solution.py:178
  43.0 7.8 %collective-permute-start.12 = (bf16[320,256]{1,0:T(8,128)(2,1)S(1)}, bf16[320,256]{1,0:T(8,128)(2,1)S(1)}, u32[]{:S(2)}, u32[]{:S(2)}) collective-permute-start(bf16[320,256]{1,0:T(8,128)(2,1)S(1)} %collective-permute-done.11.w4), channel_id=1, source_target_pairs={{0,4},{4,0},{8,12},{12,8},{16,20},{20,16},{24,28},{28,24},{1,5},{5... | collective-permute-start | bytes 491528 | tf_op jit(solution)/shard_map/ppermute | solution.py:178
  43.5 22.5 %collective-permute-start = (bf16[128,2560]{1,0:T(8,128)(2,1)S(1)}, bf16[128,2560]{1,0:T(8,128)(2,1)S(1)}, u32[]{:S(2)}, u32[]{:S(2)}) collective-permute-start(bf16[128,2560]{1,0:T(8,128)(2,1)S(1)} %bitcast.9), channel_id=1, source_target_pairs={{0,1},{1,0},{2,3},{3,2},{4,5},{5,4},{6,7},{7,6},{8,9},{9,8},{10,11... | collective-permute-start | bytes 1966088 | tf_op jit(solution)/shard_map/ppermute | solution.py:178
  48.6 17.4 %collective-permute-start.1 = (bf16[128,2560]{1,0:T(8,128)(2,1)S(1)}, bf16[128,2560]{1,0:T(8,128)(2,1)S(1)}, u32[]{:S(2)}, u32[]{:S(2)}) collective-permute-start(bf16[128,2560]{1,0:T(8,128)(2,1)S(1)} %bitcast.14), channel_id=1, source_target_pairs={{0,1},{1,0},{2,3},{3,2},{4,5},{5,4},{6,7},{7,6},{8,9},{9,8},{10,11... | collective-permute-start | bytes 1966088 | tf_op jit(solution)/shard_map/ppermute | solution.py:178
  50.8 5.3 %collective-permute-start.10 = (bf16[320,256]{1,0:T(8,128)(2,1)S(1)}, bf16[320,256]{1,0:T(8,128)(2,1)S(1)}, u32[]{:S(2)}, u32[]{:S(2)}) collective-permute-start(bf16[320,256]{1,0:T(8,128)(2,1)S(1)} %collective-permute-done.9.w2), channel_id=1, source_target_pairs={{0,4},{4,0},{8,12},{12,8},{16,20},{20,16},{24,28},{28,24},{1,5},{5... | collective-permute-start | bytes 491528 | tf_op jit(solution)/shard_map/ppermute | solution.py:178
  56.1 5.8 %collective-permute-start.3 = (bf16[144,512]{1,0:T(8,128)(2,1)S(1)}, bf16[144,512]{1,0:T(8,128)(2,1)S(1)}, u32[]{:S(2)}, u32[]{:S(2)}) collective-permute-start(bf16[144,512]{1,0:T(8,128)(2,1)S(1)} %fusion.1.k0), channel_id=1, source_target_pairs={{0,2},{1,3},{2,0},{3,1},{4,6},{5,7},{6,4},{7,5},{8,10},{9,11},{10,... | collective-permute-start | bytes 442376 | tf_op jit(solution)/shard_map/ppermute | solution.py:178
  61.4 32.2 %collective-permute-start.22 = (bf16[3072,256]{1,0:T(8,128)(2,1)}, bf16[3072,256]{1,0:T(8,128)(2,1)S(1)}, u32[]{:S(2)}, u32[]{:S(2)}) collective-permute-start(bf16[3072,256]{1,0:T(8,128)(2,1)} %get-tuple-element.50.wp), channel_id=1, source_target_pairs={{0,1},{1,0},{2,3},{3,2},{4,5},{5,4},{6,7},{7,6},{8,9},{9,8},{10,11... | collective-permute-start | bytes 4718600 | tf_op jit(solution)/shard_map/ppermute | solution.py:178
  61.4 3.2 %collective-permute-start.2 = (bf16[144,512]{1,0:T(8,128)(2,1)S(1)}, bf16[144,512]{1,0:T(8,128)(2,1)S(1)}, u32[]{:S(2)}, u32[]{:S(2)}) collective-permute-start(bf16[144,512]{1,0:T(8,128)(2,1)S(1)} %fusion.1.k0), channel_id=1, source_target_pairs={{0,1},{1,0},{2,3},{3,2},{4,5},{5,4},{6,7},{7,6},{8,9},{9,8},{10,11... | collective-permute-start | bytes 442376 | tf_op jit(solution)/shard_map/ppermute | solution.py:178
  61.9 8.2 %collective-permute-start.15 = (bf16[512,256]{1,0:T(8,128)(2,1)S(1)}, bf16[512,256]{1,0:T(8,128)(2,1)S(1)}, u32[]{:S(2)}, u32[]{:S(2)}) collective-permute-start(bf16[512,256]{1,0:T(8,128)(2,1)S(1)} %get-tuple-element.35.vp), channel_id=1, source_target_pairs={{0,2},{1,3},{2,0},{3,1},{4,6},{5,7},{6,4},{7,5},{8,10},{9,11},{10,... | collective-permute-start | bytes 786440 | tf_op jit(solution)/shard_map/ppermute | solution.py:178
  64.6 1.4 %collective-permute-start.4 = (bf16[144,512]{1,0:T(8,128)(2,1)S(1)}, bf16[144,512]{1,0:T(8,128)(2,1)S(1)}, u32[]{:S(2)}, u32[]{:S(2)}) collective-permute-start(bf16[144,512]{1,0:T(8,128)(2,1)S(1)} %collective-permute-done.3.k2), channel_id=1, source_target_pairs={{0,1},{1,0},{2,3},{3,2},{4,5},{5,4},{6,7},{7,6},{8,9},{9,8},{10,11... | collective-permute-start | bytes 442376 | tf_op jit(solution)/shard_map/ppermute | solution.py:178
  80.8 7.4 %collective-permute-start.20 = (bf16[512,256]{1,0:T(8,128)(2,1)S(1)}, bf16[512,256]{1,0:T(8,128)(2,1)S(1)}, u32[]{:S(2)}, u32[]{:S(2)}) collective-permute-start(bf16[512,256]{1,0:T(8,128)(2,1)S(1)} %get-tuple-element.47.dv), channel_id=1, source_target_pairs={{0,2},{1,3},{2,0},{3,1},{4,6},{5,7},{6,4},{7,5},{8,10},{9,11},{10,... | collective-permute-start | bytes 786440 | tf_op jit(solution)/shard_map/ppermute | solution.py:178
  91.4 2.2 %collective-permute-start.21 = (bf16[256,256]{1,0:T(8,128)(2,1)S(1)}, bf16[256,256]{1,0:T(8,128)(2,1)S(1)}, u32[]{:S(2)}, u32[]{:S(2)}) collective-permute-start(bf16[256,256]{1,0:T(8,128)(2,1)S(1)} %get-tuple-element.49), channel_id=1, source_target_pairs={{0,1},{1,0},{2,3},{3,2},{4,5},{5,4},{6,7},{7,6},{8,9},{9,8},{10,11... | collective-permute-start | bytes 393224 | tf_op jit(solution)/shard_map/ppermute | solution.py:178
  91.5 10.6 %collective-permute-start.24 = (bf16[640,256]{1,0:T(8,128)(2,1)S(1)}, bf16[640,256]{1,0:T(8,128)(2,1)S(1)}, u32[]{:S(2)}, u32[]{:S(2)}) collective-permute-start(bf16[640,256]{1,0:T(8,128)(2,1)S(1)} %get-tuple-element.54), channel_id=1, source_target_pairs={{0,4},{4,0},{8,12},{12,8},{16,20},{20,16},{24,28},{28,24},{1,5},{5... | collective-permute-start | bytes 983048 | tf_op jit(solution)/shard_map/ppermute | solution.py:178
  93.0 15.6 %collective-permute-start.26 = (bf16[640,256]{1,0:T(8,128)(2,1)S(1)}, bf16[640,256]{1,0:T(8,128)(2,1)S(1)}, u32[]{:S(2)}, u32[]{:S(2)}) collective-permute-start(bf16[640,256]{1,0:T(8,128)(2,1)S(1)} %get-tuple-element.58), channel_id=1, source_target_pairs={{0,4},{4,0},{8,12},{12,8},{16,20},{20,16},{24,28},{28,24},{1,5},{5... | collective-permute-start | bytes 983048 | tf_op jit(solution)/shard_map/ppermute | solution.py:178
  97.2 34.8 %collective-permute-start.23 = (bf16[128,3072]{1,0:T(8,128)(2,1)S(1)}, bf16[128,3072]{1,0:T(8,128)(2,1)S(1)}, u32[]{:S(2)}, u32[]{:S(2)}) collective-permute-start(bf16[128,3072]{1,0:T(8,128)(2,1)S(1)} %get-tuple-element.52), channel_id=1, source_target_pairs={{0,2},{1,3},{2,0},{3,1},{4,6},{5,7},{6,4},{7,5},{8,10},{9,11},{10,... | collective-permute-start | bytes 2359304 | tf_op jit(solution)/shard_map/ppermute | solution.py:178
  102.2 9.9 %collective-permute-start.25 = (bf16[320,256]{1,0:T(8,128)(2,1)S(1)}, bf16[320,256]{1,0:T(8,128)(2,1)S(1)}, u32[]{:S(2)}, u32[]{:S(2)}) collective-permute-start(bf16[320,256]{1,0:T(8,128)(2,1)S(1)} %get-tuple-element.56), channel_id=1, source_target_pairs={{0,8},{4,12},{8,0},{12,4},{16,24},{20,28},{24,16},{28,20},{1,9},{5... | collective-permute-start | bytes 491528 | tf_op jit(solution)/shard_map/ppermute | solution.py:178
  108.7 13.8 %collective-permute-start.27 = (bf16[320,256]{1,0:T(8,128)(2,1)S(1)}, bf16[320,256]{1,0:T(8,128)(2,1)S(1)}, u32[]{:S(2)}, u32[]{:S(2)}) collective-permute-start(bf16[320,256]{1,0:T(8,128)(2,1)S(1)} %get-tuple-element.59), channel_id=1, source_target_pairs={{0,16},{4,20},{8,24},{12,28},{16,0},{20,4},{24,8},{28,12},{1,17},{... | collective-permute-start | bytes 491528 | tf_op jit(solution)/shard_map/ppermute | solution.py:178
  110.4 12.2 %collective-permute-start.28 = (bf16[320,256]{1,0:T(8,128)(2,1)S(1)}, bf16[320,256]{1,0:T(8,128)(2,1)S(1)}, u32[]{:S(2)}, u32[]{:S(2)}) collective-permute-start(bf16[320,256]{1,0:T(8,128)(2,1)S(1)} %get-tuple-element.60), channel_id=1, source_target_pairs={{0,24},{4,28},{8,16},{12,20},{16,8},{20,12},{24,0},{28,4},{1,25},{... | collective-permute-start | bytes 491528 | tf_op jit(solution)/shard_map/ppermute | solution.py:178
  111.7 11.3 %collective-permute-start.18 = (bf16[256,256]{1,0:T(8,128)(2,1)S(1)}, bf16[256,256]{1,0:T(8,128)(2,1)S(1)}, u32[]{:S(2)}, u32[]{:S(2)}) collective-permute-start(bf16[256,256]{1,0:T(8,128)(2,1)S(1)} %get-tuple-element.41), channel_id=1, source_target_pairs={{0,2},{1,3},{2,0},{3,1},{4,6},{5,7},{6,4},{7,5},{8,10},{9,11},{10,... | collective-permute-start | bytes 393224 | tf_op jit(solution)/shard_map/ppermute | solution.py:178
  112.0 17.3 %collective-permute-start.16 = (bf16[128,1280]{1,0:T(8,128)(2,1)S(1)}, bf16[128,1280]{1,0:T(8,128)(2,1)S(1)}, u32[]{:S(2)}, u32[]{:S(2)}) collective-permute-start(bf16[128,1280]{1,0:T(8,128)(2,1)S(1)} %get-tuple-element.37), channel_id=1, source_target_pairs={{0,1},{1,0},{2,3},{3,2},{4,5},{5,4},{6,7},{7,6},{8,9},{9,8},{10,11... | collective-permute-start | bytes 983048 | tf_op jit(solution)/shard_map/ppermute | solution.py:178
  122.6 6.8 %collective-permute-start.17 = (bf16[128,1280]{1,0:T(8,128)(2,1)S(1)}, bf16[128,1280]{1,0:T(8,128)(2,1)S(1)}, u32[]{:S(2)}, u32[]{:S(2)}) collective-permute-start(bf16[128,1280]{1,0:T(8,128)(2,1)S(1)} %get-tuple-element.39), channel_id=1, source_target_pairs={{0,1},{1,0},{2,3},{3,2},{4,5},{5,4},{6,7},{7,6},{8,9},{9,8},{10,11... | collective-permute-start | bytes 983048 | tf_op jit(solution)/shard_map/ppermute | solution.py:178
  122.7 6.7 %collective-permute-start.30 = (bf16[320,256]{1,0:T(8,128)(2,1)S(1)}, bf16[320,256]{1,0:T(8,128)(2,1)S(1)}, u32[]{:S(2)}, u32[]{:S(2)}) collective-permute-start(bf16[320,256]{1,0:T(8,128)(2,1)S(1)} %shard_map.112.p0), channel_id=1, source_target_pairs={{0,2},{1,3},{2,0},{3,1},{4,6},{5,7},{6,4},{7,5},{8,10},{9,11},{10,... | collective-permute-start | bytes 491528 | tf_op jit(solution)/shard_map/ppermute | solution.py:178
  123.1 1.3 collective-permute-start.19
  124.4 6.2 %collective-permute-start.29 = (bf16[320,256]{1,0:T(8,128)(2,1)S(1)}, bf16[320,256]{1,0:T(8,128)(2,1)S(1)}, u32[]{:S(2)}, u32[]{:S(2)}) collective-permute-start(bf16[320,256]{1,0:T(8,128)(2,1)S(1)} %shard_map.112.p0), channel_id=1, source_target_pairs={{0,1},{1,0},{2,3},{3,2},{4,5},{5,4},{6,7},{7,6},{8,9},{9,8},{10,11... | collective-permute-start | bytes 491528 | tf_op jit(solution)/shard_map/ppermute | solution.py:178
  129.3 1.4 %collective-permute-start.31 = (bf16[320,256]{1,0:T(8,128)(2,1)S(1)}, bf16[320,256]{1,0:T(8,128)(2,1)S(1)}, u32[]{:S(2)}, u32[]{:S(2)}) collective-permute-start(bf16[320,256]{1,0:T(8,128)(2,1)S(1)} %collective-permute-done.30.p2), channel_id=1, source_target_pairs={{0,1},{1,0},{2,3},{3,2},{4,5},{5,4},{6,7},{7,6},{8,9},{9,8},{10,11... | collective-permute-start | bytes 491528 | tf_op jit(solution)/shard_map/ppermute | solution.py:178
  (12 other events, 275.1 us)

commit v2 on v0

--- a/solution.py
+++ b/solution.py
@@ -1,12 +1,21 @@
+import functools
+
 import jax
 import jax.numpy as jnp
 from jax import lax
+from jax.experimental import pallas as pl
+from jax.experimental.pallas import tpu as pltpu
 from jax.sharding import PartitionSpec as P
 
 QUERY_HEADS = 20
 KEY_VALUE_HEADS = 4
 HEAD_SIZE = 128
 QUERY_PER_KV = 5
+
+BF = jnp.bfloat16
+F32 = jnp.float32
+VM = pl.BlockSpec(memory_space=pltpu.VMEM)
+ANY = pl.BlockSpec(memory_space=pl.ANY)
 
 
 def body(hidden, queries, keys, value_weight, doc_ids, cotangent):
@@ -141,6 +150,491 @@
     )
 
 
+N_DP = 8
+ROWS = 128
+SHARD = 640
+HALF = SHARD // 2
+CHUNK = 128
+WIDE = N_DP * HALF
+CORE_KV = 256
+CORE_Q = 1280
+KEY_AT = WIDE
+DOC_AT = KEY_AT + 512
+QUERY_AT = DOC_AT + ROWS
+COT_AT = QUERY_AT + CORE_Q
+PACK = COT_AT + CORE_Q
+
+
+def params(mib=32):
+    return pltpu.CompilerParams(vmem_limit_bytes=mib * 1024 * 1024)
+
+
+def cost(flops, nbytes):
+    return pl.CostEstimate(flops=int(flops), bytes_accessed=int(nbytes), transcendentals=0)
+
+
+def sds(shape, dtype=BF):
+    return jax.ShapeDtypeStruct(shape, dtype)
+
+
+def swap(x, axis, k):
+    size = lax.axis_size(axis)
+    return lax.ppermute(x, axis, [(i, i ^ k) for i in range(size)])
+
+
+def after(x, *others):
+    return lax.optimization_barrier((x, *others))[0]
+
+
+def dot_tt(a, b):
+    return lax.dot_general(a, b, (((0,), (0,)), ((), ())), preferred_element_type=F32)
+
+
+def dot_nt(a, b):
+    return lax.dot_general(a, b, (((1,), (1,)), ((), ())), preferred_element_type=F32)
+
+
+def turn(x):
+    return pltpu.roll(x.astype(F32), CHUNK // 2, 1).astype(x.dtype)
+
+
+def first_half():
+    return lax.broadcasted_iota(jnp.int32, (ROWS, CHUNK), 1) < CHUNK // 2
+
+
+def pack_kernel(h, k, doc, w, q, g, send, keep, w0):
+    s = lax.axis_index("seq")
+    r = lax.axis_index("dp")
+    y, c = s // 2, s % 2
+    cols = pl.ds(pl.multiple_of(c * CORE_KV, CORE_KV), CORE_KV)
+    w0[0:256, :] = w[pl.ds(pl.multiple_of(y * 384, 128), 256), cols]
+    w0[256:HALF, :] = w[pl.ds(pl.multiple_of(256 + y * 64, 64), 64), cols]
+    low = first_half()
+    for out, part in ((send, 1 - y), (keep, y)):
+        for p in range(N_DP // 2):
+            mids = []
+            for i in range(2):
+                base = (r ^ (2 * p + i)) * SHARD
+                start = pl.multiple_of(base + part * 384, 128)
+                out[:, p * SHARD + i * 256 : p * SHARD + (i + 1) * 256] = h[:, pl.ds(start, 256)]
+                mid = h[:, pl.ds(pl.multiple_of(base + 256, 128), CHUNK)]
+                mids.append(jnp.where(part == i, mid, turn(mid)))
+            out[:, p * SHARD + 512 : (p + 1) * SHARD] = jnp.where(low, mids[0], mids[1])
+        out[:, KEY_AT:DOC_AT] = k[...]
+        out[:, DOC_AT:QUERY_AT] = jnp.broadcast_to(doc[...].astype(F32), (ROWS, ROWS)).astype(BF)
+    other = pl.ds(pl.multiple_of((1 - c) * CORE_Q, CORE_Q), CORE_Q)
+    keep[:, QUERY_AT:COT_AT] = q[:, other]
+    keep[:, COT_AT:PACK] = g[:, other]
+
+
+def pack(h, k, doc, w, q, g):
+    return pl.pallas_call(
+        pack_kernel,
+        out_shape=(sds((ROWS, QUERY_AT)), sds((ROWS, PACK)), sds((HALF, CORE_KV))),
+        in_specs=[VM] * 6,
+        out_specs=(VM,) * 3,
+        compiler_params=params(60),
+        cost_estimate=cost(0, 3e6),
+    )(h, k, doc, w, q, g)
+
+
+def values_kernel(h0, h1, h2, w0, w1, w2, w3, w4, w5, w6, w7, vp_ref, wp_ref):
+    ws = (w0, w1, w2, w3, w4, w5, w6, w7)
+    for p in range(N_DP // 2):
+        a, b = ws[2 * p], ws[2 * p + 1]
+        base = p * SHARD
+        wp_ref[base : base + 256, :] = a[0:256, :]
+        wp_ref[base + 256 : base + 512, :] = b[0:256, :]
+        wp_ref[base + 512 : base + 576, :] = a[256:HALF, :]
+        wp_ref[base + 576 : base + 640, :] = b[256:HALF, :]
+    for t, h in enumerate((h0, h1, h2)):
+        vp_ref[t * ROWS : (t + 1) * ROWS, :] = jnp.dot(
+            h[:, 0:WIDE], wp_ref[...], preferred_element_type=F32
+        ).astype(BF)
+
+
+def partial_values(hs, ws):
+    return pl.pallas_call(
+        values_kernel,
+        out_shape=(sds((3 * ROWS, CORE_KV)), sds((WIDE, CORE_KV))),
+        in_specs=[VM] * 11,
+        out_specs=(VM, VM),
+        compiler_params=params(),
+        cost_estimate=cost(2 * 384 * WIDE * 256, 6e6),
+    )(*hs, *ws)
+
+
+def last_values_kernel(vp, h3, wp, o_ref):
+    o_ref[0 : 3 * ROWS, :] = vp[...]
+    o_ref[3 * ROWS :, :] = jnp.dot(h3[:, 0:WIDE], wp[...], preferred_element_type=F32).astype(BF)
+
+
+def last_values(vp, h3, wp):
+    return pl.pallas_call(
+        last_values_kernel,
+        out_shape=sds((4 * ROWS, CORE_KV)),
+        in_specs=[VM] * 3,
+        out_specs=VM,
+        compiler_params=params(),
+        cost_estimate=cost(2 * 128 * WIDE * 256, 2e6),
+    )(vp, h3, wp)
+
+
+def scores_kernel(q0, p0, p1, p2, p3, e_ref, inv_ref, bias):
+    s = lax.axis_index("seq")
+    c = s % 2
+    factor = HEAD_SIZE ** (-0.5)
+    log2e = 1.4426950408889634
+    ps = (p0, p1, p2, p3)
+    rows = [p[0:16, DOC_AT:QUERY_AT][0:1, :].astype(F32) for p in ps]
+    for t in range(4):
+        key_doc = jnp.transpose(jnp.broadcast_to(rows[t], (ROWS, ROWS)))
+        key_pos = (s ^ t) * ROWS + lax.broadcasted_iota(jnp.int32, (ROWS, ROWS), 0)
+        for u in range(2):
+            query_pos = (s ^ u) * ROWS + lax.broadcasted_iota(jnp.int32, (ROWS, ROWS), 1)
+            allow = (key_pos <= query_pos) & (key_doc == jnp.broadcast_to(rows[u], (ROWS, ROWS)))
+            bias[t * ROWS : (t + 1) * ROWS, u * ROWS : (u + 1) * ROWS] = jnp.where(allow, 0.0, -1e30)
+    for kvh in range(2):
+        cols = pl.ds(pl.multiple_of(KEY_AT + c * CORE_KV + kvh * HEAD_SIZE, HEAD_SIZE), HEAD_SIZE)
+        key = jnp.concatenate([p[:, cols] for p in ps], axis=0)
+        for i in range(QUERY_PER_KV):
+            head = kvh * QUERY_PER_KV + i
+            qcols = pl.ds(pl.multiple_of(c * CORE_Q + head * HEAD_SIZE, HEAD_SIZE), HEAD_SIZE)
+            far = p1[:, QUERY_AT + head * HEAD_SIZE : QUERY_AT + (head + 1) * HEAD_SIZE]
+            query = jnp.concatenate([q0[:, qcols], far], axis=0)
+            st = dot_nt(key, query) * (factor * log2e) + bias[...]
+            e = jnp.exp2(st - jnp.max(st, axis=0, keepdims=True))
+            inv_ref[head * 8 : head * 8 + 8, :] = jnp.broadcast_to(
+                1.0 / jnp.sum(e, axis=0, keepdims=True), (8, 2 * ROWS)
+            )
+            e_ref[head] = e.astype(BF)
+
+
+def scores(q, ps):
+    return pl.pallas_call(
+        scores_kernel,
+        out_shape=(sds((10, 4 * ROWS, 2 * ROWS)), sds((80, 2 * ROWS), F32)),
+        in_specs=[VM] * 5,
+        out_specs=(VM,) * 2,
+        scratch_shapes=[pltpu.VMEM((4 * ROWS, 2 * ROWS), F32)],
+        compiler_params=params(),
+        cost_estimate=cost(2 * 10 * 256 * 512 * 128 * 8, 6e6),
+    )(q, *ps)
+
+
+def attention_kernel(
+    e_ref, inv_ref, q0, g0, p0, p1, p2, p3, vp, rv,
+    o0, dq0, dk0, dk2, swap_ref, dv_ref,
+):
+    c = lax.axis_index("seq") % 2
+    factor = HEAD_SIZE ** (-0.5)
+    ps = (p0, p1, p2, p3)
+    for kvh in range(2):
+        cols = pl.ds(pl.multiple_of(KEY_AT + c * CORE_KV + kvh * HEAD_SIZE, HEAD_SIZE), HEAD_SIZE)
+        mine = slice(kvh * HEAD_SIZE, (kvh + 1) * HEAD_SIZE)
+        key = jnp.concatenate([p[:, cols] for p in ps], axis=0)
+        far = rv[:, mine].astype(F32)
+        far = jnp.concatenate([far[2 * ROWS :], far[: 2 * ROWS]], axis=0)
+        value = (vp[:, mine].astype(F32) + far).astype(BF)
+        dk = jnp.zeros((4 * ROWS, HEAD_SIZE), F32)
+        dv = jnp.zeros((4 * ROWS, HEAD_SIZE), F32)
+        for i in range(QUERY_PER_KV):
+            head = kvh * QUERY_PER_KV + i
+            qcols = pl.ds(pl.multiple_of(c * CORE_Q + head * HEAD_SIZE, HEAD_SIZE), HEAD_SIZE)
+            low, high = head * HEAD_SIZE, (head + 1) * HEAD_SIZE
+            query = jnp.concatenate([q0[:, qcols], p1[:, QUERY_AT + low : QUERY_AT + high]], axis=0)
+            cot = jnp.concatenate([g0[:, qcols], p1[:, COT_AT + low : COT_AT + high]], axis=0)
+            e = e_ref[head]
+            inv = inv_ref[head * 8 : head * 8 + 8, :][0:1, :]
+            out = jnp.transpose(dot_tt(value, e) * inv).astype(BF)
+            o0[:, low:high] = out[:ROWS]
+            swap_ref[:, low:high] = out[ROWS:]
+            probs = e.astype(F32) * inv
+            term = probs * dot_nt(value, cot)
+            delta = jnp.sum(term, axis=0, keepdims=True)
+            ds = (term - probs * delta).astype(BF)
+            dq = jnp.transpose(dot_tt(key, ds) * factor).astype(BF)
+            dq0[:, low:high] = dq[:ROWS]
+            swap_ref[:, CORE_Q + low : CORE_Q + high] = dq[ROWS:]
+            dk = dk + jnp.dot(ds, query, preferred_element_type=F32)
+            dv = dv + jnp.dot(probs.astype(BF), cot, preferred_element_type=F32)
+        dk = (dk * factor).astype(BF)
+        dk0[:, mine] = dk[:ROWS]
+        dk2[:, mine] = dk[2 * ROWS : 3 * ROWS]
+        at = 2 * CORE_Q + kvh * HEAD_SIZE
+        swap_ref[:, at : at + HEAD_SIZE] = dk[ROWS : 2 * ROWS]
+        swap_ref[:, at + CORE_KV : at + CORE_KV + HEAD_SIZE] = dk[3 * ROWS :]
+        dv_ref[:, mine] = dv.astype(BF)
+
+
+def attention(e, inv, q, g, ps, vp, rv):
+    return pl.pallas_call(
+        attention_kernel,
+        out_shape=(sds((ROWS, CORE_Q)),) * 2
+        + (sds((ROWS, CORE_KV)),) * 2
+        + (sds((ROWS, 2 * CORE_Q + 2 * CORE_KV)), sds((4 * ROWS, CORE_KV))),
+        in_specs=[VM] * 10,
+        out_specs=(VM,) * 6,
+        compiler_params=params(),
+        cost_estimate=cost(2 * 5 * 10 * 256 * 512 * 128 * 4, 6e6),
+    )(e, inv, q, g, *ps, vp, rv)
+
+
+def weight_grad_pair(p, hs, gv, even, odd):
+    for (out, at), start in ((even, 0), (odd, 256)):
+        acc = jnp.zeros((256, CORE_KV), F32)
+        for t, h in enumerate(hs):
+            first = p * SHARD + start
+            acc = acc + dot_tt(h[:, first : first + 256], gv[t * ROWS : (t + 1) * ROWS, :])
+        out[at : at + 256, :] = acc.astype(BF)
+    acc = jnp.zeros((CHUNK, CORE_KV), F32)
+    for t, h in enumerate(hs):
+        acc = acc + dot_tt(h[:, p * SHARD + 512 : (p + 1) * SHARD], gv[t * ROWS : (t + 1) * ROWS, :])
+    acc = acc.astype(BF)
+    for (out, at), half in ((even, acc[:64]), (odd, acc[64:])):
+        out[at + 256 : at + HALF, :] = half
+
+
+def weight_grad_far_kernel(dv, rdv, h0, h1, h2, h3, send, own, gv, gv_keep, gv_send):
+    for t in range(4):
+        a = dv[t * ROWS : (t + 1) * ROWS, :].astype(F32)
+        b = rdv[(t ^ 2) * ROWS : ((t ^ 2) + 1) * ROWS, :].astype(F32)
+        total = (a + b).astype(BF)
+        gv[t * ROWS : (t + 1) * ROWS, :] = total
+        half = (t // 2) * ROWS
+        if t % 2 == 0:
+            gv_keep[half : half + ROWS, :] = total
+        else:
+            gv_send[half : half + ROWS, :] = total
+    for place, p in enumerate((2, 3)):
+        weight_grad_pair(p, (h0, h1, h2, h3), gv, (own, place * HALF), (send, place * HALF))
+
+
+def weight_grad_far(dv, rdv, hs):
+    return pl.pallas_call(
+        weight_grad_far_kernel,
+        out_shape=(sds((2 * HALF, CORE_KV)),) * 2 + (sds((4 * ROWS, CORE_KV)),) + (sds((2 * ROWS, CORE_KV)),) * 2,
+        in_specs=[VM] * 6,
+        out_specs=(VM,) * 5,
+        compiler_params=params(),
+        cost_estimate=cost(512 * WIDE * 256, 4e6),
+    )(dv, rdv, *hs)
+
+
+def weight_grad_near_kernel(gv, h0, h1, h2, h3, send, own):
+    for p, out in ((1, send), (0, own)):
+        weight_grad_pair(p, (h0, h1, h2, h3), gv, (out, 0), (out, HALF))
+
+
+def weight_grad_near(gv, hs):
+    return pl.pallas_call(
+        weight_grad_near_kernel,
+        out_shape=(sds((2 * HALF, CORE_KV)),) * 2,
+        in_specs=[VM] * 5,
+        out_specs=(VM,) * 2,
+        compiler_params=params(),
+        cost_estimate=cost(512 * WIDE * 256, 4e6),
+    )(gv, *hs)
+
+
+def hidden_grad_kernel(gv, gvs, wp, wps, dk2, swapped, gh0, send_a, send_b):
+    full = dot_nt(gv[...], wp[...]) + dot_nt(gvs[...], wps[...])
+    full = full.astype(BF)
+    gh0[...] = full[:ROWS]
+    far = full[ROWS:]
+    send_a[...] = far[:, : WIDE // 2]
+    send_b[:, : WIDE // 2] = far[:, WIDE // 2 :]
+    c = lax.axis_index("seq") % 2
+    at = WIDE // 2
+    send_b[:, pl.ds(pl.multiple_of(at + c * CORE_KV, CORE_KV), CORE_KV)] = dk2[...]
+    send_b[:, pl.ds(pl.multiple_of(at + (1 - c) * CORE_KV, CORE_KV), CORE_KV)] = swapped[
+        :, 2 * CORE_Q + CORE_KV :
+    ]
+
+
+def hidden_grad(gv, gvs, wp, wps, dk2, swapped):
+    return pl.pallas_call(
+        hidden_grad_kernel,
+        out_shape=(sds((ROWS, WIDE)), sds((ROWS, WIDE // 2)), sds((ROWS, WIDE // 2 + 2 * CORE_KV))),
+        in_specs=[VM] * 6,
+        out_specs=(VM,) * 3,
+        compiler_params=params(),
+        cost_estimate=cost(2 * 256 * WIDE * 512, 6e6),
+    )(gv, gvs, wp, wps, dk2, swapped)
+
+
+def hidden_join_kernel(own_ref, far_a, far_b, dk0, swapped, o_ref, dk_ref, far_ref):
+    far_ref[:, 0 : WIDE // 2] = far_a[...]
+    far_ref[:, WIDE // 2 :] = far_b[:, : WIDE // 2]
+    s = lax.axis_index("seq")
+    y, c = s // 2, s % 2
+    r = lax.axis_index("dp")
+    low = first_half()
+    for p in range(N_DP // 2):
+        for i in range(2):
+            base = (r ^ (2 * p + i)) * SHARD
+            src = slice(p * SHARD + i * 256, p * SHARD + (i + 1) * 256)
+            o_ref[:, pl.ds(pl.multiple_of(base + y * 384, 128), 256)] = own_ref[:, src]
+            o_ref[:, pl.ds(pl.multiple_of(base + (1 - y) * 384, 128), 256)] = far_ref[:, src]
+        own = own_ref[:, p * SHARD + 512 : (p + 1) * SHARD]
+        far = far_ref[:, p * SHARD + 512 : (p + 1) * SHARD]
+        part0 = jnp.where(y == 0, own, far)
+        part1 = jnp.where(y == 0, far, own)
+        at0 = pl.multiple_of((r ^ (2 * p)) * SHARD + 256, 128)
+        at1 = pl.multiple_of((r ^ (2 * p + 1)) * SHARD + 256, 128)
+        o_ref[:, pl.ds(at0, CHUNK)] = jnp.where(low, part0, turn(part1))
+        o_ref[:, pl.ds(at1, CHUNK)] = jnp.where(low, turn(part0), part1)
+    for place, near in ((c, dk0[...]), (1 - c, swapped[:, 2 * CORE_Q : 2 * CORE_Q + CORE_KV])):
+        far = far_b[:, pl.ds(pl.multiple_of(WIDE // 2 + place * CORE_KV, CORE_KV), CORE_KV)]
+        dk_ref[:, pl.ds(pl.multiple_of(place * CORE_KV, CORE_KV), CORE_KV)] = (
+            near.astype(F32) + far.astype(F32)
+        ).astype(BF)
+
+
+def hidden_join(own, fars, dk0, swapped):
+    return pl.pallas_call(
+        hidden_join_kernel,
+        out_shape=(sds((ROWS, N_DP * SHARD)), sds((ROWS, 2 * CORE_KV))),
+        in_specs=[VM] * 5,
+        out_specs=(VM, VM),
+        scratch_shapes=[pltpu.VMEM((ROWS, WIDE), BF)],
+        compiler_params=params(),
+        cost_estimate=cost(0, 3e6),
+    )(own, *fars, dk0, swapped)
+
+
+def heads_join_kernel(o0, dq0, swapped, o_ref, dq_ref):
+    c = lax.axis_index("seq") % 2
+    near = pl.ds(pl.multiple_of(c * CORE_Q, CORE_Q), CORE_Q)
+    far = pl.ds(pl.multiple_of((1 - c) * CORE_Q, CORE_Q), CORE_Q)
+    o_ref[:, near] = o0[...]
+    o_ref[:, far] = swapped[:, 0:CORE_Q]
+    dq_ref[:, near] = dq0[...]
+    dq_ref[:, far] = swapped[:, CORE_Q : 2 * CORE_Q]
+
+
+def heads_join(o0, dq0, swapped):
+    return pl.pallas_call(
+        heads_join_kernel,
+        out_shape=(sds((ROWS, 2 * CORE_Q)),) * 2,
+        in_specs=[VM] * 3,
+        out_specs=(VM,) * 2,
+        compiler_params=params(),
+        cost_estimate=cost(0, 4e6),
+    )(o0, dq0, swapped)
+
+
+def add_pair_kernel(a, b, o0, o1):
+    total = (a[...].astype(F32) + b[...].astype(F32)).astype(BF)
+    o0[...] = total[:HALF]
+    o1[...] = total[HALF:]
+
+
+def add_pair(a, b):
+    return pl.pallas_call(
+        add_pair_kernel,
+        out_shape=(sds((HALF, CORE_KV)),) * 2,
+        in_specs=[VM] * 2,
+        out_specs=(VM,) * 2,
+        compiler_params=params(),
+        cost_estimate=cost(0, 1e6),
+    )(a, b)
+
+
+def add_two_kernel(a, b, o):
+    o[...] = a[...].astype(F32) + b[...].astype(F32)
+
+
+def add_two(a, b):
+    return pl.pallas_call(
+        add_two_kernel,
+        out_shape=sds((HALF, CORE_KV), F32),
+        in_specs=[VM] * 2,
+        out_specs=VM,
+        compiler_params=params(),
+        cost_estimate=cost(0, 1e6),
+    )(a, b)
+
+
+def add_three_kernel(a, b, c, o):
+    o[...] = (a[...] + (b[...].astype(F32) + c[...].astype(F32))).astype(BF)
+
+
+def add_three(a, b, c):
+    return pl.pallas_call(
+        add_three_kernel,
+        out_shape=sds((HALF, CORE_KV)),
+        in_specs=[VM] * 3,
+        out_specs=VM,
+        compiler_params=params(),
+        cost_estimate=cost(0, 1e6),
+    )(a, b, c)
+
+
+def weight_join_kernel(p0, p1, p2, p3, o_ref):
+    s = lax.axis_index("seq")
+    for t, p in enumerate((p0, p1, p2, p3)):
+        y, c = (s ^ t) // 2, (s ^ t) % 2
+        cols = pl.ds(pl.multiple_of(c * CORE_KV, CORE_KV), CORE_KV)
+        o_ref[pl.ds(pl.multiple_of(y * 384, 128), 256), cols] = p[0:256, :].astype(F32)
+        o_ref[pl.ds(pl.multiple_of(256 + y * 64, 64), 64), cols] = p[256:HALF, :].astype(F32)
+
+
+def weight_join(ps):
+    return pl.pallas_call(
+        weight_join_kernel,
+        out_shape=sds((SHARD, 2 * CORE_KV), F32),
+        in_specs=[VM] * 4,
+        out_specs=VM,
+        compiler_params=params(),
+        cost_estimate=cost(0, 2e6),
+    )(*ps)
+
+
+def paired_body(hidden, queries, keys, value_weight, doc_ids, cotangent):
+    q, g = queries[0], cotangent[0]
+    send, p0, w0 = pack(hidden[0], keys[0], doc_ids, value_weight, q, g)
+    p2 = swap(send, "seq", 2)
+    w6, w4, w2 = swap(w0, "dp", 6), swap(w0, "dp", 4), swap(w0, "dp", 2)
+    w1 = swap(w0, "dp", 1)
+    w3 = swap(w1, "dp", 2)
+    p1 = swap(p0, "seq", 1)
+    w7, w5 = swap(w6, "dp", 1), swap(after(w4, w2), "dp", 1)
+    p3 = swap(after(p2, w1, w3, w5, w7), "seq", 1)
+    ps = (p0, p1, p2, p3)
+    vp3, wp = partial_values((p0, p1, p2), (w0, w1, w2, w3, w4, w5, w6, w7))
+    vp = last_values(vp3, p3, wp)
+    rv = swap(vp, "seq", 2)
+    e, inv = scores(after(q, vp), ps)
+    wps = swap(wp, "seq", 1)
+    o0, dq0, dk0, dk2, swap_out, dv = attention(e, inv, q, g, ps, vp, rv)
+    rdv = swap(dv, "seq", 2)
+    send_a, own_a, gv, gv_keep, gv_send = weight_grad_far(dv, rdv, ps)
+    send_b, own_b = weight_grad_near(gv, ps)
+    far_a = swap(send_a, "dp", 1)
+    far_b = swap(send_b, "dp", 2)
+    gvs = swap(after(gv_send, send_b), "seq", 1)
+    swapped = swap(swap_out, "seq", 1)
+    gh0, gh_a, gh_b = hidden_grad(gv_keep, gvs, wp, wps, dk2, swapped)
+    s4, s6 = add_pair(own_a, far_a)
+    t6, t4 = swap(s6, "dp", 6), swap(s4, "dp", 4)
+    t46 = add_two(t4, t6)
+    s0, s1 = add_pair(own_b, far_b)
+    t1 = swap(s1, "dp", 1)
+    gh_far = swap(gh_a, "seq", 2), swap(gh_b, "seq", 2)
+    attn_out, grad_queries = heads_join(o0, dq0, swapped)
+    d0 = add_three(t46, s0, t1)
+    d2 = swap(d0, "seq", 2)
+    d1 = swap(d0, "seq", 1)
+    grad_hidden, grad_keys = hidden_join(gh0, gh_far, dk0, swapped)
+    d2, grad_hidden, grad_keys, attn_out, grad_queries = lax.optimization_barrier(
+        (d2, grad_hidden, grad_keys, attn_out, grad_queries)
+    )
+    d3 = swap(d2, "seq", 1)
+    grad_weight = weight_join((d0, d1, d2, d3))
+    return attn_out[None], grad_queries[None], grad_keys[None], grad_hidden[None], grad_weight
+
+
 def solution(mesh):
     in_specs = (
         P("dp", "seq", None),
@@ -157,4 +651,7 @@
         P("dp", "seq", None),
         P("dp", None),
     )
-    return jax.shard_map(body, mesh=mesh, in_specs=in_specs, out_specs=out_specs, check_vma=False)
+    paired = mesh.shape["dp"] == N_DP and mesh.shape["seq"] == 4
+    return jax.shard_map(
+        paired_body if paired else body, mesh=mesh, in_specs=in_specs, out_specs=out_specs, check_vma=False
+    )

time: 362 us -> 89.6 us (0.25)
  waiting for transfers between devices: 223 us -> 43.9 us
  local copies, waits for them, and re-layouts: 52.1 us -> 2.78 us
  matrix products: 40.6 us -> 0 us
  starting transfers between devices: 0.16 us -> 24.9 us
  blocking collectives: 21.3 us -> 0 us
  Pallas kernels: 0 us -> 16.4 us
  between operations: 13.9 us -> 0.78 us
  other arithmetic: 8.28 us -> 0 us
    unnamed x5 -> x0, waiting for transfers between devices: 97.2 us -> none
    all_gather x1 -> x0, waiting for transfers between devices: 73.9 us -> none  [body(): full_weight = lax.all_gather(value_weight, 'dp', axis=0, tiled=True)]
    ppermute x0 -> x25, waiting for transfers between devices: none -> 43.9 us  [swap(): return lax.ppermute(x, axis, [(i, i ^ k) for i in range(size)])]
    dot_general x31 -> x0, matrix products: 40.6 us -> none  [the longest x4 10.7 us: gradient_update(): jnp.einsum('hgqk,khd->qhgd', dscore, key_tile, preferred_element_type=jnp...]
    psum x1 -> x0, waiting for transfers between devices: 28.9 us -> none  [body(): grad_weight = lax.psum(partial_rows, 'seq').astype(jnp.float32)]
    ppermute x0 -> x25, starting transfers between devices: none -> 24.9 us  [swap(): return lax.ppermute(x, axis, [(i, i ^ k) for i in range(size)])]
    reduce_scatter x1 -> x0, waiting for transfers between devices: 22.9 us -> none  [body(): lax.psum_scatter(grad_buf.astype(jnp.float32).astype(jnp.bfloat16), 'seq'...]
    all_gather x3 -> x0, blocking collectives: 21.3 us -> none  [the longest x1 8.16 us: body(): lax.all_gather(keys[0], 'seq', axis=0, tiled=True)]
  transfers between devices with their start and end apart: 4 -> 25, of which waited for: 4 -> 12; matrix products, arithmetic and copies ran while one was open for 4% -> 0% of each run, Pallas kernels for 0% -> 12%
where the time goes in v2:
time: 89.6 us; the launch traced here: 88.7 us
  waiting for transfers between devices  43.9 us (49%)
  starting transfers between devices  24.9 us (28%)
  Pallas kernels  16.4 us (18%)
  local copies, waits for them, and re-layouts  2.78 us (3%)
    ppermute x25, waiting for transfers between devices, swap(): return lax.ppermute(x, axis, [(i, i ^ k) for i in range(size)])  43.9 us
    ppermute x25, starting transfers between devices, swap(): return lax.ppermute(x, axis, [(i, i ^ k) for i in range(size)])  24.9 us
    pallas_call x1, Pallas kernels, pack(): pl.pallas_call(pack_kernel, out_shape=(sds((ROWS, QUERY_AT)), sds((ROWS,...  3.83 us
    pallas_call x1, Pallas kernels, attention(): pl.pallas_call(attention_kernel, out_shape=(sds((ROWS, CORE_Q)),) * 2 + (...  3.27 us
    unnamed x10, local copies, waits for them, and re-layouts  2.78 us
  transfers between devices with their start and end apart: 25, of which 12 were waited for; matrix products, arithmetic and copies ran while one was open for 0% of the time, Pallas kernels for 12%

profile of v2, /device:TPU:0, one launch (start us, length us, event | category | flops | bytes accessed | tf_op | source)
XLA Modules:
  0.0 88.7 jit_solution(9175055856669688123)
XLA Ops:
  0.6 3.8 %shard_map.101 = (bf16[128,3200]{1,0:T(8,128)(2,1)}, bf16[128,5760]{1,0:T(8,128)(2,1)}, bf16[320,256]{1,0:T(8,128)(2,1)}) custom-call(bf16[128,5120]{1,0:T(8,128)(2,1)} %bitcast.13, bf16[128,512]{1,0:T(8,128)(2,1)} %bitcast.14, s32[1,128]{1,0:T(1,128)} %doc.1, bf16[640,512]{1,0:T(8,128)(2,1)} %w.1, bf16[128,2560]{1,0:T(8,128)(2,1)} %bitcast.8, ...), custom_call_target="tpu_custom_call" | custom-call | bytes 3000000 | tf_op jit(solution)/shard_map/pallas_call | solution.py:231
  4.5 3.0 %collective-permute-start.1 = (bf16[128,3200]{1,0:T(8,128)(2,1)}, bf16[128,3200]{1,0:T(8,128)(2,1)S(1)}, u32[]{:S(2)}, u32[]{:S(2)}) collective-permute-start(bf16[128,3200]{1,0:T(8,128)(2,1)} %get-tuple-element.46), channel_id=1, source_target_pairs={{0,2},{1,3},{2,0},{3,1},{4,6},{5,7},{6,4},{7,5},{8,10},{9,11},{10,... | collective-permute-start | bytes 2457608 | tf_op jit(solution)/shard_map/ppermute | solution.py:182
  7.4 1.6 %collective-permute-start.3 = (bf16[320,256]{1,0:T(8,128)(2,1)}, bf16[320,256]{1,0:T(8,128)(2,1)S(1)}, u32[]{:S(2)}, u32[]{:S(2)}) collective-permute-start(bf16[320,256]{1,0:T(8,128)(2,1)} %get-tuple-element.47.w0), channel_id=1, source_target_pairs={{0,8},{4,12},{8,0},{12,4},{16,24},{20,28},{24,16},{28,20},{1,9},{5... | collective-permute-start | bytes 491528 | tf_op jit(solution)/shard_map/ppermute | solution.py:182
  9.0 2.6 %collective-permute-start.5 = (bf16[320,256]{1,0:T(8,128)(2,1)}, bf16[320,256]{1,0:T(8,128)(2,1)S(1)}, u32[]{:S(2)}, u32[]{:S(2)}) collective-permute-start(bf16[320,256]{1,0:T(8,128)(2,1)} %get-tuple-element.47.w0), channel_id=1, source_target_pairs={{0,16},{4,20},{8,24},{12,28},{16,0},{20,4},{24,8},{28,12},{1,17},{... | collective-permute-start | bytes 491528 | tf_op jit(solution)/shard_map/ppermute | solution.py:182
  11.6 1.5 %collective-permute-start.2 = (bf16[320,256]{1,0:T(8,128)(2,1)}, bf16[320,256]{1,0:T(8,128)(2,1)S(1)}, u32[]{:S(2)}, u32[]{:S(2)}) collective-permute-start(bf16[320,256]{1,0:T(8,128)(2,1)} %get-tuple-element.47.w0), channel_id=1, source_target_pairs={{0,4},{4,0},{8,12},{12,8},{16,20},{20,16},{24,28},{28,24},{1,5},{5... | collective-permute-start | bytes 491528 | tf_op jit(solution)/shard_map/ppermute | solution.py:182
  13.1 4.5 %collective-permute-done.3.w2 = bf16[320,256]{1,0:T(8,128)(2,1)S(1)} collective-permute-done((bf16[320,256]{1,0:T(8,128)(2,1)}, bf16[320,256]{1,0:T(8,128)(2,1)S(1)}, u32[]{:S(2)}, u32[]{:S(2)}) %collective-permute-start.3) | collective-permute-done | bytes 163872 | tf_op jit(solution)/shard_map/ppermute | solution.py:182
  17.6 2.5 %collective-permute-start.7 = (bf16[320,256]{1,0:T(8,128)(2,1)}, bf16[320,256]{1,0:T(8,128)(2,1)S(1)}, u32[]{:S(2)}, u32[]{:S(2)}) collective-permute-start(bf16[320,256]{1,0:T(8,128)(2,1)} %get-tuple-element.47.w0), channel_id=1, source_target_pairs={{0,24},{4,28},{8,16},{12,20},{16,8},{20,12},{24,0},{28,4},{1,25},{... | collective-permute-start | bytes 491528 | tf_op jit(solution)/shard_map/ppermute | solution.py:182
  20.1 1.5 %collective-permute-start.6 = (bf16[320,256]{1,0:T(8,128)(2,1)S(1)}, bf16[320,256]{1,0:T(8,128)(2,1)S(1)}, u32[]{:S(2)}, u32[]{:S(2)}) collective-permute-start(bf16[320,256]{1,0:T(8,128)(2,1)S(1)} %collective-permute-done.5.w4), channel_id=1, source_target_pairs={{0,4},{4,0},{8,12},{12,8},{16,20},{20,16},{24,28},{28,24},{1,5},{5... | collective-permute-start | bytes 491528 | tf_op jit(solution)/shard_map/ppermute | solution.py:182
  22.0 4.8 %collective-permute-done.7.w6 = bf16[320,256]{1,0:T(8,128)(2,1)S(1)} collective-permute-done((bf16[320,256]{1,0:T(8,128)(2,1)}, bf16[320,256]{1,0:T(8,128)(2,1)S(1)}, u32[]{:S(2)}, u32[]{:S(2)}) %collective-permute-start.7) | collective-permute-done | bytes 163872 | tf_op jit(solution)/shard_map/ppermute | solution.py:182
  26.7 1.5 %collective-permute-start.8 = (bf16[320,256]{1,0:T(8,128)(2,1)S(1)}, bf16[320,256]{1,0:T(8,128)(2,1)S(1)}, u32[]{:S(2)}, u32[]{:S(2)}) collective-permute-start(bf16[320,256]{1,0:T(8,128)(2,1)S(1)} %collective-permute-done.7.w6), channel_id=1, source_target_pairs={{0,4},{4,0},{8,12},{12,8},{16,20},{20,16},{24,28},{28,24},{1,5},{5... | collective-permute-start | bytes 491528 | tf_op jit(solution)/shard_map/ppermute | solution.py:182
  29.1 3.0 %collective-permute-done.8.w7 = bf16[320,256]{1,0:T(8,128)(2,1)S(1)} collective-permute-done((bf16[320,256]{1,0:T(8,128)(2,1)S(1)}, bf16[320,256]{1,0:T(8,128)(2,1)S(1)}, u32[]{:S(2)}, u32[]{:S(2)}) %collective-permute-start.8) | collective-permute-done | bytes 163872 | tf_op jit(solution)/shard_map/ppermute | solution.py:182
  32.1 1.4 %copy-done = bf16[128,5760]{1,0:T(8,128)(2,1)S(1)} copy-done((bf16[128,5760]{1,0:T(8,128)(2,1)S(1)}, bf16[128,5760]{1,0:T(8,128)(2,1)}, u32[]{:S(2)}) %copy-start) | copy-done | bytes 1474584
  33.5 0.9 %copy-done.4 = bf16[320,256]{1,0:T(8,128)(2,1)S(1)} copy-done((bf16[320,256]{1,0:T(8,128)(2,1)S(1)}, bf16[320,256]{1,0:T(8,128)(2,1)}, u32[]{:S(2)}) %copy-start.4) | copy-done | bytes 163864
  36.6 1.7 %shard_map.104 = (bf16[10,512,256]{2,1,0:T(8,128)(2,1)S(1)}, f32[80,256]{1,0:T(8,128)S(1)}) custom-call(bf16[128,2560]{1,0:T(8,128)(2,1)S(1)} %bitcast.9, bf16[128,5760]{1,0:T(8,128)(2,1)S(1)} %copy-done.1, bf16[128,5760]{1,0:T(8,128)(2,1)S(1)} %collective-permute-done.h1.p1, bf16[128,3200]{1,0:T(8,128)(2,1)S(1)} %collective-permute-done.1.h2.p2, ...), custom_call_target="tpu_custom_call" | custom-call | flops 2684354560 | bytes 6000000 | tf_op jit(solution)/shard_map/pallas_call | solution.py:314
  38.3 5.9 %collective-permute-done.10.rv = bf16[512,256]{1,0:T(8,128)(2,1)S(1)} collective-permute-done((bf16[512,256]{1,0:T(8,128)(2,1)S(1)}, bf16[512,256]{1,0:T(8,128)(2,1)S(1)}, u32[]{:S(2)}, u32[]{:S(2)}) %collective-permute-start.10) | collective-permute-done | bytes 262176 | tf_op jit(solution)/shard_map/ppermute | solution.py:182
  44.2 3.3 %shard_map.105 = (bf16[128,1280]{1,0:T(8,128)(2,1)S(1)}, bf16[128,1280]{1,0:T(8,128)(2,1)S(1)}, bf16[128,256]{1,0:T(8,128)(2,1)S(1)}, bf16[128,256]{1,0:T(8,128)...) custom-call(bf16[10,512,256]{2,1,0:T(8,128)(2,1)S(1)} %get-tuple-element.53.e_ref, ...), custom_call_target="tpu_custom_call" | custom-call | flops 6710886400 | bytes 6000000 | tf_op jit(solution)/shard_map/pallas_call | solution.py:371
  48.0 8.3 %collective-permute-done.11.rdv = bf16[512,256]{1,0:T(8,128)(2,1)S(1)} collective-permute-done((bf16[512,256]{1,0:T(8,128)(2,1)S(1)}, bf16[512,256]{1,0:T(8,128)(2,1)S(1)}, u32[]{:S(2)}, u32[]{:S(2)}) %collective-permute-start.11) | collective-permute-done | bytes 262176 | tf_op jit(solution)/shard_map/ppermute | solution.py:182
  57.2 1.6 %collective-permute-start.12 = (bf16[640,256]{1,0:T(8,128)(2,1)S(1)}, bf16[640,256]{1,0:T(8,128)(2,1)S(1)}, u32[]{:S(2)}, u32[]{:S(2)}) collective-permute-start(bf16[640,256]{1,0:T(8,128)(2,1)S(1)} %get-tuple-element.57), channel_id=1, source_target_pairs={{0,4},{4,0},{8,12},{12,8},{16,20},{20,16},{24,28},{28,24},{1,5},{5... | collective-permute-start | bytes 983048 | tf_op jit(solution)/shard_map/ppermute | solution.py:182
  59.6 1.1 %collective-permute-start.15 = (bf16[640,256]{1,0:T(8,128)(2,1)S(1)}, bf16[640,256]{1,0:T(8,128)(2,1)S(1)}, u32[]{:S(2)}, u32[]{:S(2)}) collective-permute-start(bf16[640,256]{1,0:T(8,128)(2,1)S(1)} %get-tuple-element.62), channel_id=1, source_target_pairs={{0,8},{4,12},{8,0},{12,4},{16,24},{20,28},{24,16},{28,20},{1,9},{5... | collective-permute-start | bytes 983048 | tf_op jit(solution)/shard_map/ppermute | solution.py:182
  60.7 1.3 %collective-permute-done.18.gvs = bf16[256,256]{1,0:T(8,128)(2,1)S(1)} collective-permute-done((bf16[256,256]{1,0:T(8,128)(2,1)S(1)}, bf16[256,256]{1,0:T(8,128)(2,1)S(1)}, u32[]{:S(2)}, u32[]{:S(2)}) %collective-permute-start.18) | collective-permute-done | bytes 131104 | tf_op jit(solution)/shard_map/ppermute | solution.py:182
  63.5 3.0 %collective-permute-done.12.b = bf16[640,256]{1,0:T(8,128)(2,1)S(1)} collective-permute-done((bf16[640,256]{1,0:T(8,128)(2,1)S(1)}, bf16[640,256]{1,0:T(8,128)(2,1)S(1)}, u32[]{:S(2)}, u32[]{:S(2)}) %collective-permute-start.12) | collective-permute-done | bytes 327712 | tf_op jit(solution)/shard_map/ppermute | solution.py:182
  66.6 1.9 %collective-permute-start.13 = (bf16[320,256]{1,0:T(8,128)(2,1)S(1)}, bf16[320,256]{1,0:T(8,128)(2,1)S(1)}, u32[]{:S(2)}, u32[]{:S(2)}) collective-permute-start(bf16[320,256]{1,0:T(8,128)(2,1)S(1)} %get-tuple-element.58), channel_id=1, source_target_pairs={{0,16},{4,20},{8,24},{12,28},{16,0},{20,4},{24,8},{28,12},{1,17},{... | collective-permute-start | bytes 491528 | tf_op jit(solution)/shard_map/ppermute | solution.py:182
  68.5 1.5 %collective-permute-start.14 = (bf16[320,256]{1,0:T(8,128)(2,1)S(1)}, bf16[320,256]{1,0:T(8,128)(2,1)S(1)}, u32[]{:S(2)}, u32[]{:S(2)}) collective-permute-start(bf16[320,256]{1,0:T(8,128)(2,1)S(1)} %get-tuple-element.59), channel_id=1, source_target_pairs={{0,24},{4,28},{8,16},{12,20},{16,8},{20,12},{24,0},{28,4},{1,25},{... | collective-permute-start | bytes 491528 | tf_op jit(solution)/shard_map/ppermute | solution.py:182
  70.1 1.0 %collective-permute-start.21 = (bf16[128,1280]{1,0:T(8,128)(2,1)S(1)}, bf16[128,1280]{1,0:T(8,128)(2,1)S(1)}, u32[]{:S(2)}, u32[]{:S(2)}) collective-permute-start(bf16[128,1280]{1,0:T(8,128)(2,1)S(1)} %get-tuple-element.71), channel_id=1, source_target_pairs={{0,2},{1,3},{2,0},{3,1},{4,6},{5,7},{6,4},{7,5},{8,10},{9,11},{10,... | collective-permute-start | bytes 983048 | tf_op jit(solution)/shard_map/ppermute | solution.py:182
  71.2 1.1 %collective-permute-start.16 = (bf16[320,256]{1,0:T(8,128)(2,1)S(1)}, bf16[320,256]{1,0:T(8,128)(2,1)S(1)}, u32[]{:S(2)}, u32[]{:S(2)}) collective-permute-start(bf16[320,256]{1,0:T(8,128)(2,1)S(1)} %get-tuple-element.64), channel_id=1, source_target_pairs={{0,4},{4,0},{8,12},{12,8},{16,20},{20,16},{24,28},{28,24},{1,5},{5... | collective-permute-start | bytes 491528 | tf_op jit(solution)/shard_map/ppermute | solution.py:182
  72.2 8.4 %collective-permute-done.13.a = bf16[320,256]{1,0:T(8,128)(2,1)S(1)} collective-permute-done((bf16[320,256]{1,0:T(8,128)(2,1)S(1)}, bf16[320,256]{1,0:T(8,128)(2,1)S(1)}, u32[]{:S(2)}, u32[]{:S(2)}) %collective-permute-start.13) | collective-permute-done | bytes 163872 | tf_op jit(solution)/shard_map/ppermute | solution.py:182
  81.4 1.2 %shard_map.114 = (bf16[128,2560]{1,0:T(8,128)(2,1)}, bf16[128,2560]{1,0:T(8,128)(2,1)}) custom-call(bf16[128,1280]{1,0:T(8,128)(2,1)S(1)} %get-tuple-element.76.o0, bf16[128,1280]{1,0:T(8,128)(2,1)S(1)} %get-tuple-element.77.dq0, bf16[128,3072]{1,0:T(8,128)(2,1)S(1)} %collective-permute-done.20.swapped), custom_call_target="tpu_custom_call" | custom-call | bytes 4000000 | tf_op jit(solution)/shard_map/pallas_call | solution.py:517
  82.5 0.9 %collective-permute-done.21.far_a = bf16[128,1280]{1,0:T(8,128)(2,1)S(1)} collective-permute-done((bf16[128,1280]{1,0:T(8,128)(2,1)S(1)}, bf16[128,1280]{1,0:T(8,128)(2,1)S(1)}, u32[]{:S(2)}, u32[]{:S(2)}) %collective-permute-start.21) | collective-permute-done | bytes 327712 | tf_op jit(solution)/shard_map/ppermute | solution.py:182
  83.4 1.4 %shard_map.113 = (bf16[128,5120]{1,0:T(8,128)(2,1)}, bf16[128,512]{1,0:T(8,128)(2,1)}) custom-call(bf16[128,2560]{1,0:T(8,128)(2,1)S(1)} %get-tuple-element.70.own_ref, bf16[128,1280]{1,0:T(8,128)(2,1)S(1)} %collective-permute-done.21.far_a, bf16[128,1792]{1,0:T(8,128)(2,1)S(1)} %collective-permute-done.22.far_b, ...), custom_call_target="tpu_custom_call" | custom-call | bytes 3000000 | tf_op jit(solution)/shard_map/pallas_call | solution.py:495
  84.8 1.4 %collective-permute-done.17.p2 = bf16[320,256]{1,0:T(8,128)(2,1)S(1)} collective-permute-done((bf16[320,256]{1,0:T(8,128)(2,1)S(1)}, bf16[320,256]{1,0:T(8,128)(2,1)S(1)}, u32[]{:S(2)}, u32[]{:S(2)}) %collective-permute-start.17) | collective-permute-done | bytes 163872 | tf_op jit(solution)/shard_map/ppermute | solution.py:182
  86.2 1.4 %collective-permute-done.24.p3 = bf16[320,256]{1,0:T(8,128)(2,1)S(1)} collective-permute-done((bf16[320,256]{1,0:T(8,128)(2,1)S(1)}, bf16[320,256]{1,0:T(8,128)(2,1)S(1)}, u32[]{:S(2)}, u32[]{:S(2)}) %collective-permute-start.24) | collective-permute-done | bytes 163872 | tf_op jit(solution)/shard_map/ppermute | solution.py:182
  87.6 1.2 %shard_map.115 = f32[640,512]{1,0:T(8,128)} custom-call(bf16[320,256]{1,0:T(8,128)(2,1)S(1)} %shard_map.111.p0, bf16[320,256]{1,0:T(8,128)(2,1)S(1)} %collective-permute-done.23.p1, bf16[320,256]{1,0:T(8,128)(2,1)S(1)} %collective-permute-done.17.p2, bf16[320,256]{1,0:T(8,128)(2,1)S(1)} %collective-permute-done.24.p3), custom_call_target="tpu_custom_call" | custom-call | bytes 2000000 | tf_op jit(solution)/shard_map/pallas_call | solution.py:584
  (43 shorter events, 7.9 us)
Async XLA Ops:
  4.5 27.6 %collective-permute-start.1 = (bf16[128,3200]{1,0:T(8,128)(2,1)}, bf16[128,3200]{1,0:T(8,128)(2,1)S(1)}, u32[]{:S(2)}, u32[]{:S(2)}) collective-permute-start(bf16[128,3200]{1,0:T(8,128)(2,1)} %get-tuple-element.46), channel_id=1, source_target_pairs={{0,2},{1,3},{2,0},{3,1},{4,6},{5,7},{6,4},{7,5},{8,10},{9,11},{10,... | collective-permute-start | bytes 2457608 | tf_op jit(solution)/shard_map/ppermute | solution.py:182
  7.4 24.6 %collective-permute-start = (bf16[128,5760]{1,0:T(8,128)(2,1)}, bf16[128,5760]{1,0:T(8,128)(2,1)S(1)}, u32[]{:S(2)}, u32[]{:S(2)}) collective-permute-start(bf16[128,5760]{1,0:T(8,128)(2,1)} %get-tuple-element.45.h0.p0), channel_id=1, source_target_pairs={{0,1},{1,0},{2,3},{3,2},{4,5},{5,4},{6,7},{7,6},{8,9},{9,8},{10,11... | collective-permute-start | bytes 4423688 | tf_op jit(solution)/shard_map/ppermute | solution.py:182
  7.4 10.2 %collective-permute-start.3 = (bf16[320,256]{1,0:T(8,128)(2,1)}, bf16[320,256]{1,0:T(8,128)(2,1)S(1)}, u32[]{:S(2)}, u32[]{:S(2)}) collective-permute-start(bf16[320,256]{1,0:T(8,128)(2,1)} %get-tuple-element.47.w0), channel_id=1, source_target_pairs={{0,8},{4,12},{8,0},{12,4},{16,24},{20,28},{24,16},{28,20},{1,9},{5... | collective-permute-start | bytes 491528 | tf_op jit(solution)/shard_map/ppermute | solution.py:182
  9.0 11.1 %collective-permute-start.5 = (bf16[320,256]{1,0:T(8,128)(2,1)}, bf16[320,256]{1,0:T(8,128)(2,1)S(1)}, u32[]{:S(2)}, u32[]{:S(2)}) collective-permute-start(bf16[320,256]{1,0:T(8,128)(2,1)} %get-tuple-element.47.w0), channel_id=1, source_target_pairs={{0,16},{4,20},{8,24},{12,28},{16,0},{20,4},{24,8},{28,12},{1,17},{... | collective-permute-start | bytes 491528 | tf_op jit(solution)/shard_map/ppermute | solution.py:182
  11.6 10.0 %collective-permute-start.2 = (bf16[320,256]{1,0:T(8,128)(2,1)}, bf16[320,256]{1,0:T(8,128)(2,1)S(1)}, u32[]{:S(2)}, u32[]{:S(2)}) collective-permute-start(bf16[320,256]{1,0:T(8,128)(2,1)} %get-tuple-element.47.w0), channel_id=1, source_target_pairs={{0,4},{4,0},{8,12},{12,8},{16,20},{20,16},{24,28},{28,24},{1,5},{5... | collective-permute-start | bytes 491528 | tf_op jit(solution)/shard_map/ppermute | solution.py:182
  17.6 9.1 %collective-permute-start.7 = (bf16[320,256]{1,0:T(8,128)(2,1)}, bf16[320,256]{1,0:T(8,128)(2,1)S(1)}, u32[]{:S(2)}, u32[]{:S(2)}) collective-permute-start(bf16[320,256]{1,0:T(8,128)(2,1)} %get-tuple-element.47.w0), channel_id=1, source_target_pairs={{0,24},{4,28},{8,16},{12,20},{16,8},{20,12},{24,0},{28,4},{1,25},{... | collective-permute-start | bytes 491528 | tf_op jit(solution)/shard_map/ppermute | solution.py:182
  20.1 8.1 %collective-permute-start.6 = (bf16[320,256]{1,0:T(8,128)(2,1)S(1)}, bf16[320,256]{1,0:T(8,128)(2,1)S(1)}, u32[]{:S(2)}, u32[]{:S(2)}) collective-permute-start(bf16[320,256]{1,0:T(8,128)(2,1)S(1)} %collective-permute-done.5.w4), channel_id=1, source_target_pairs={{0,4},{4,0},{8,12},{12,8},{16,20},{20,16},{24,28},{28,24},{1,5},{5... | collective-permute-start | bytes 491528 | tf_op jit(solution)/shard_map/ppermute | solution.py:182
  21.6 7.5 %collective-permute-start.4 = (bf16[320,256]{1,0:T(8,128)(2,1)S(1)}, bf16[320,256]{1,0:T(8,128)(2,1)S(1)}, u32[]{:S(2)}, u32[]{:S(2)}) collective-permute-start(bf16[320,256]{1,0:T(8,128)(2,1)S(1)} %collective-permute-done.2.w1), channel_id=1, source_target_pairs={{0,8},{4,12},{8,0},{12,4},{16,24},{20,28},{24,16},{28,20},{1,9},{5... | collective-permute-start | bytes 491528 | tf_op jit(solution)/shard_map/ppermute | solution.py:182
  26.7 5.3 %collective-permute-start.8 = (bf16[320,256]{1,0:T(8,128)(2,1)S(1)}, bf16[320,256]{1,0:T(8,128)(2,1)S(1)}, u32[]{:S(2)}, u32[]{:S(2)}) collective-permute-start(bf16[320,256]{1,0:T(8,128)(2,1)S(1)} %collective-permute-done.7.w6), channel_id=1, source_target_pairs={{0,4},{4,0},{8,12},{12,8},{16,20},{20,16},{24,28},{28,24},{1,5},{5... | collective-permute-start | bytes 491528 | tf_op jit(solution)/shard_map/ppermute | solution.py:182
  32.1 3.0 %collective-permute-start.9 = (bf16[128,3200]{1,0:T(8,128)(2,1)S(1)}, bf16[128,3200]{1,0:T(8,128)(2,1)S(1)}, u32[]{:S(2)}, u32[]{:S(2)}) collective-permute-start(bf16[128,3200]{1,0:T(8,128)(2,1)S(1)} %collective-permute-done.1.h2.p2), channel_id=1, source_target_pairs={{0,1},{1,0},{2,3},{3,2},{4,5},{5,4},{6,7},{7,6},{8,9},{9,8},{10,11... | collective-permute-start | bytes 2457608 | tf_op jit(solution)/shard_map/ppermute | solution.py:182
  32.1 1.4 %copy-start = (bf16[128,5760]{1,0:T(8,128)(2,1)S(1)}, bf16[128,5760]{1,0:T(8,128)(2,1)}, u32[]{:S(2)}) copy-start(bf16[128,5760]{1,0:T(8,128)(2,1)} %get-tuple-element.45.h0.p0) | copy-start | bytes 4423684
  33.5 0.9 %copy-start.4 = (bf16[320,256]{1,0:T(8,128)(2,1)S(1)}, bf16[320,256]{1,0:T(8,128)(2,1)}, u32[]{:S(2)}) copy-start(bf16[320,256]{1,0:T(8,128)(2,1)} %get-tuple-element.47.w0) | copy-start | bytes 491524
  35.1 1.4 %copy-start.1 = (bf16[128,5760]{1,0:T(8,128)(2,1)S(1)}, bf16[128,5760]{1,0:T(8,128)(2,1)}, u32[]{:S(2)}) copy-start(bf16[128,5760]{1,0:T(8,128)(2,1)} %get-tuple-element.45.h0.p0) | copy-start | bytes 4423684
  35.1 1.5 %copy-start.2 = (bf16[1,128,2560]{2,1,0:T(8,128)(2,1)S(1)}, bf16[1,128,2560]{2,1,0:T(8,128)(2,1)}, u32[]{:S(2)}) copy-start(bf16[1,128,2560]{2,1,0:T(8,128)(2,1)} %param.7) | copy-start | bytes 1966084
  35.4 8.8 %copy-start.3 = (bf16[1,128,2560]{2,1,0:T(8,128)(2,1)S(1)}, bf16[1,128,2560]{2,1,0:T(8,128)(2,1)}, u32[]{:S(2)}) copy-start(bf16[1,128,2560]{2,1,0:T(8,128)(2,1)} %param.11) | copy-start | bytes 1966084
  35.5 8.8 %collective-permute-start.10 = (bf16[512,256]{1,0:T(8,128)(2,1)S(1)}, bf16[512,256]{1,0:T(8,128)(2,1)S(1)}, u32[]{:S(2)}, u32[]{:S(2)}) collective-permute-start(bf16[512,256]{1,0:T(8,128)(2,1)S(1)} %shard_map.103.vp), channel_id=1, source_target_pairs={{0,2},{1,3},{2,0},{3,1},{4,6},{5,7},{6,4},{7,5},{8,10},{9,11},{10,... | collective-permute-start | bytes 786440 | tf_op jit(solution)/shard_map/ppermute | solution.py:182
  35.8 26.3 %collective-permute-start.19 = (bf16[2560,256]{1,0:T(8,128)(2,1)S(1)}, bf16[2560,256]{1,0:T(8,128)(2,1)S(1)}, u32[]{:S(2)}, u32[]{:S(2)}) collective-permute-start(bf16[2560,256]{1,0:T(8,128)(2,1)S(1)} %get-tuple-element.51.wp), channel_id=1, source_target_pairs={{0,1},{1,0},{2,3},{3,2},{4,5},{5,4},{6,7},{7,6},{8,9},{9,8},{10,11... | collective-permute-start | bytes 3932168 | tf_op jit(solution)/shard_map/ppermute | solution.py:182
  47.5 14.6 %collective-permute-start.20 = (bf16[128,3072]{1,0:T(8,128)(2,1)S(1)}, bf16[128,3072]{1,0:T(8,128)(2,1)S(1)}, u32[]{:S(2)}, u32[]{:S(2)}) collective-permute-start(bf16[128,3072]{1,0:T(8,128)(2,1)S(1)} %get-tuple-element.69), channel_id=1, source_target_pairs={{0,1},{1,0},{2,3},{3,2},{4,5},{5,4},{6,7},{7,6},{8,9},{9,8},{10,11... | collective-permute-start | bytes 2359304 | tf_op jit(solution)/shard_map/ppermute | solution.py:182
  47.6 8.7 %collective-permute-start.11 = (bf16[512,256]{1,0:T(8,128)(2,1)S(1)}, bf16[512,256]{1,0:T(8,128)(2,1)S(1)}, u32[]{:S(2)}, u32[]{:S(2)}) collective-permute-start(bf16[512,256]{1,0:T(8,128)(2,1)S(1)} %get-tuple-element.55.dv), channel_id=1, source_target_pairs={{0,2},{1,3},{2,0},{3,1},{4,6},{5,7},{6,4},{7,5},{8,10},{9,11},{10,... | collective-permute-start | bytes 786440 | tf_op jit(solution)/shard_map/ppermute | solution.py:182
  57.2 9.3 %collective-permute-start.12 = (bf16[640,256]{1,0:T(8,128)(2,1)S(1)}, bf16[640,256]{1,0:T(8,128)(2,1)S(1)}, u32[]{:S(2)}, u32[]{:S(2)}) collective-permute-start(bf16[640,256]{1,0:T(8,128)(2,1)S(1)} %get-tuple-element.57), channel_id=1, source_target_pairs={{0,4},{4,0},{8,12},{12,8},{16,20},{20,16},{24,28},{28,24},{1,5},{5... | collective-permute-start | bytes 983048 | tf_op jit(solution)/shard_map/ppermute | solution.py:182
  59.6 10.4 %collective-permute-start.15 = (bf16[640,256]{1,0:T(8,128)(2,1)S(1)}, bf16[640,256]{1,0:T(8,128)(2,1)S(1)}, u32[]{:S(2)}, u32[]{:S(2)}) collective-permute-start(bf16[640,256]{1,0:T(8,128)(2,1)S(1)} %get-tuple-element.62), channel_id=1, source_target_pairs={{0,8},{4,12},{8,0},{12,4},{16,24},{20,28},{24,16},{28,20},{1,9},{5... | collective-permute-start | bytes 983048 | tf_op jit(solution)/shard_map/ppermute | solution.py:182
  60.7 1.3 %collective-permute-start.18 = (bf16[256,256]{1,0:T(8,128)(2,1)S(1)}, bf16[256,256]{1,0:T(8,128)(2,1)S(1)}, u32[]{:S(2)}, u32[]{:S(2)}) collective-permute-start(bf16[256,256]{1,0:T(8,128)(2,1)S(1)} %get-tuple-element.67), channel_id=1, source_target_pairs={{0,1},{1,0},{2,3},{3,2},{4,5},{5,4},{6,7},{7,6},{8,9},{9,8},{10,11... | collective-permute-start | bytes 393224 | tf_op jit(solution)/shard_map/ppermute | solution.py:182
  63.0 20.5 %collective-permute-start.22 = (bf16[128,1792]{1,0:T(8,128)(2,1)S(1)}, bf16[128,1792]{1,0:T(8,128)(2,1)S(1)}, u32[]{:S(2)}, u32[]{:S(2)}) collective-permute-start(bf16[128,1792]{1,0:T(8,128)(2,1)S(1)} %get-tuple-element.72), channel_id=1, source_target_pairs={{0,2},{1,3},{2,0},{3,1},{4,6},{5,7},{6,4},{7,5},{8,10},{9,11},{10,... | collective-permute-start | bytes 1376264 | tf_op jit(solution)/shard_map/ppermute | solution.py:182
  66.6 14.1 %collective-permute-start.13 = (bf16[320,256]{1,0:T(8,128)(2,1)S(1)}, bf16[320,256]{1,0:T(8,128)(2,1)S(1)}, u32[]{:S(2)}, u32[]{:S(2)}) collective-permute-start(bf16[320,256]{1,0:T(8,128)(2,1)S(1)} %get-tuple-element.58), channel_id=1, source_target_pairs={{0,16},{4,20},{8,24},{12,28},{16,0},{20,4},{24,8},{28,12},{1,17},{... | collective-permute-start | bytes 491528 | tf_op jit(solution)/shard_map/ppermute | solution.py:182
  68.5 12.1 %collective-permute-start.14 = (bf16[320,256]{1,0:T(8,128)(2,1)S(1)}, bf16[320,256]{1,0:T(8,128)(2,1)S(1)}, u32[]{:S(2)}, u32[]{:S(2)}) collective-permute-start(bf16[320,256]{1,0:T(8,128)(2,1)S(1)} %get-tuple-element.59), channel_id=1, source_target_pairs={{0,24},{4,28},{8,16},{12,20},{16,8},{20,12},{24,0},{28,4},{1,25},{... | collective-permute-start | bytes 491528 | tf_op jit(solution)/shard_map/ppermute | solution.py:182
  70.1 13.3 %collective-permute-start.21 = (bf16[128,1280]{1,0:T(8,128)(2,1)S(1)}, bf16[128,1280]{1,0:T(8,128)(2,1)S(1)}, u32[]{:S(2)}, u32[]{:S(2)}) collective-permute-start(bf16[128,1280]{1,0:T(8,128)(2,1)S(1)} %get-tuple-element.71), channel_id=1, source_target_pairs={{0,2},{1,3},{2,0},{3,1},{4,6},{5,7},{6,4},{7,5},{8,10},{9,11},{10,... | collective-permute-start | bytes 983048 | tf_op jit(solution)/shard_map/ppermute | solution.py:182
  71.2 9.6 %collective-permute-start.16 = (bf16[320,256]{1,0:T(8,128)(2,1)S(1)}, bf16[320,256]{1,0:T(8,128)(2,1)S(1)}, u32[]{:S(2)}, u32[]{:S(2)}) collective-permute-start(bf16[320,256]{1,0:T(8,128)(2,1)S(1)} %get-tuple-element.64), channel_id=1, source_target_pairs={{0,4},{4,0},{8,12},{12,8},{16,20},{20,16},{24,28},{28,24},{1,5},{5... | collective-permute-start | bytes 491528 | tf_op jit(solution)/shard_map/ppermute | solution.py:182
  80.8 5.4 %collective-permute-start.17 = (bf16[320,256]{1,0:T(8,128)(2,1)S(1)}, bf16[320,256]{1,0:T(8,128)(2,1)S(1)}, u32[]{:S(2)}, u32[]{:S(2)}) collective-permute-start(bf16[320,256]{1,0:T(8,128)(2,1)S(1)} %shard_map.111.p0), channel_id=1, source_target_pairs={{0,2},{1,3},{2,0},{3,1},{4,6},{5,7},{6,4},{7,5},{8,10},{9,11},{10,... | collective-permute-start | bytes 491528 | tf_op jit(solution)/shard_map/ppermute | solution.py:182
  81.4 4.8 %collective-permute-start.23 = (bf16[320,256]{1,0:T(8,128)(2,1)S(1)}, bf16[320,256]{1,0:T(8,128)(2,1)S(1)}, u32[]{:S(2)}, u32[]{:S(2)}) collective-permute-start(bf16[320,256]{1,0:T(8,128)(2,1)S(1)} %shard_map.111.p0), channel_id=1, source_target_pairs={{0,1},{1,0},{2,3},{3,2},{4,5},{5,4},{6,7},{7,6},{8,9},{9,8},{10,11... | collective-permute-start | bytes 491528 | tf_op jit(solution)/shard_map/ppermute | solution.py:182
  86.2 1.4 %collective-permute-start.24 = (bf16[320,256]{1,0:T(8,128)(2,1)S(1)}, bf16[320,256]{1,0:T(8,128)(2,1)S(1)}, u32[]{:S(2)}, u32[]{:S(2)}) collective-permute-start(bf16[320,256]{1,0:T(8,128)(2,1)S(1)} %collective-permute-done.17.p2), channel_id=1, source_target_pairs={{0,1},{1,0},{2,3},{3,2},{4,5},{5,4},{6,7},{7,6},{8,9},{9,8},{10,11... | collective-permute-start | bytes 491528 | tf_op jit(solution)/shard_map/ppermute | solution.py:182

commit v3 on v2

--- a/solution.py
+++ b/solution.py
@@ -157,6 +157,8 @@
 CHUNK = 128
 WIDE = N_DP * HALF
 CORE_KV = 256
+SPARE = 16
+CUT = 768
 CORE_Q = 1280
 KEY_AT = WIDE
 DOC_AT = KEY_AT + 512
@@ -238,6 +240,22 @@
     )(h, k, doc, w, q, g)
 
 
+def relay_kernel(p, w, own, ow):
+    own[...] = p[:, 0:QUERY_AT]
+    ow[...] = w[...]
+
+
+def relay(p, w):
+    return pl.pallas_call(
+        relay_kernel,
+        out_shape=(sds((ROWS, QUERY_AT)), sds((HALF, CORE_KV))),
+        in_specs=[VM] * 2,
+        out_specs=(VM,) * 2,
+        compiler_params=params(),
+        cost_estimate=cost(0, 4e6),
+    )(p, w)
+
+
 def values_kernel(h0, h1, h2, w0, w1, w2, w3, w4, w5, w6, w7, vp_ref, wp_ref):
     ws = (w0, w1, w2, w3, w4, w5, w6, w7)
     for p in range(N_DP // 2):
@@ -264,17 +282,20 @@
     )(*hs, *ws)
 
 
-def last_values_kernel(vp, h3, wp, o_ref):
-    o_ref[0 : 3 * ROWS, :] = vp[...]
-    o_ref[3 * ROWS :, :] = jnp.dot(h3[:, 0:WIDE], wp[...], preferred_element_type=F32).astype(BF)
+def last_values_kernel(vp, h3, wp, o0, o1):
+    last = jnp.dot(h3[:, 0:WIDE], wp[...], preferred_element_type=F32).astype(BF)
+    for i, o in enumerate((o0, o1)):
+        cols = slice(i * HEAD_SIZE, (i + 1) * HEAD_SIZE)
+        o[0 : 3 * ROWS, :] = vp[:, cols]
+        o[3 * ROWS :, :] = last[:, cols]
 
 
 def last_values(vp, h3, wp):
     return pl.pallas_call(
         last_values_kernel,
-        out_shape=sds((4 * ROWS, CORE_KV)),
+        out_shape=(sds((4 * ROWS, HEAD_SIZE)),) * 2,
         in_specs=[VM] * 3,
-        out_specs=VM,
+        out_specs=(VM,) * 2,
         compiler_params=params(),
         cost_estimate=cost(2 * 128 * WIDE * 256, 2e6),
     )(vp, h3, wp)
@@ -322,62 +343,100 @@
     )(q, *ps)
 
 
-def attention_kernel(
-    e_ref, inv_ref, q0, g0, p0, p1, p2, p3, vp, rv,
+def attend_head(kvh, e_ref, inv_ref, q0, g0, ps, vp, rv):
+    c = lax.axis_index("seq") % 2
+    factor = HEAD_SIZE ** (-0.5)
+    p1 = ps[1]
+    cols = pl.ds(pl.multiple_of(KEY_AT + c * CORE_KV + kvh * HEAD_SIZE, HEAD_SIZE), HEAD_SIZE)
+    key = jnp.concatenate([p[:, cols] for p in ps], axis=0)
+    far = rv[...].astype(F32)
+    far = jnp.concatenate([far[2 * ROWS :], far[: 2 * ROWS]], axis=0)
+    value = (vp[...].astype(F32) + far).astype(BF)
+    dk = jnp.zeros((4 * ROWS, HEAD_SIZE), F32)
+    dv = jnp.zeros((4 * ROWS, HEAD_SIZE), F32)
+    outs = []
+    for i in range(QUERY_PER_KV):
+        head = kvh * QUERY_PER_KV + i
+        qcols = pl.ds(pl.multiple_of(c * CORE_Q + head * HEAD_SIZE, HEAD_SIZE), HEAD_SIZE)
+        low, high = head * HEAD_SIZE, (head + 1) * HEAD_SIZE
+        query = jnp.concatenate([q0[:, qcols], p1[:, QUERY_AT + low : QUERY_AT + high]], axis=0)
+        cot = jnp.concatenate([g0[:, qcols], p1[:, COT_AT + low : COT_AT + high]], axis=0)
+        e = e_ref[head]
+        inv = inv_ref[head * 8 : head * 8 + 8, :][0:1, :]
+        out = jnp.transpose(dot_tt(value, e) * inv).astype(BF)
+        probs = e.astype(F32) * inv
+        term = probs * dot_nt(value, cot)
+        delta = jnp.sum(term, axis=0, keepdims=True)
+        ds = (term - probs * delta).astype(BF)
+        dq = jnp.transpose(dot_tt(key, ds) * factor).astype(BF)
+        outs.append((out, dq))
+        dk = dk + jnp.dot(ds, query, preferred_element_type=F32)
+        dv = dv + jnp.dot(probs.astype(BF), cot, preferred_element_type=F32)
+    return outs, (dk * factor).astype(BF), dv.astype(BF)
+
+
+def attention_first_kernel(e_ref, inv_ref, q0, g0, p0, p1, p2, p3, vp, rv, out, dk_ref, dv_ref):
+    outs, dk, dv = attend_head(0, e_ref, inv_ref, q0, g0, (p0, p1, p2, p3), vp, rv)
+    for i, (o, dq) in enumerate(outs):
+        cols = slice(i * HEAD_SIZE, (i + 1) * HEAD_SIZE)
+        out[0 : 2 * ROWS, cols] = o
+        out[2 * ROWS :, cols] = dq
+    dk_ref[...] = dk
+    dv_ref[0 : 4 * ROWS, :] = dv
+    dv_ref[4 * ROWS :, :] = jnp.zeros((SPARE, HEAD_SIZE), BF)
+
+
+def attention_second_kernel(
+    e_ref, inv_ref, q0, g0, p0, p1, p2, p3, vp, rv, first, first_dk,
     o0, dq0, dk0, dk2, swap_ref, dv_ref,
 ):
-    c = lax.axis_index("seq") % 2
-    factor = HEAD_SIZE ** (-0.5)
-    ps = (p0, p1, p2, p3)
-    for kvh in range(2):
-        cols = pl.ds(pl.multiple_of(KEY_AT + c * CORE_KV + kvh * HEAD_SIZE, HEAD_SIZE), HEAD_SIZE)
+    outs, dk, dv = attend_head(1, e_ref, inv_ref, q0, g0, (p0, p1, p2, p3), vp, rv)
+    half = QUERY_PER_KV * HEAD_SIZE
+    o0[:, 0:half] = first[0:ROWS, :]
+    swap_ref[:, 0:half] = first[ROWS : 2 * ROWS, :]
+    dq0[:, 0:half] = first[2 * ROWS : 3 * ROWS, :]
+    swap_ref[:, CORE_Q : CORE_Q + half] = first[3 * ROWS :, :]
+    for i, (o, dq) in enumerate(outs):
+        low, high = half + i * HEAD_SIZE, half + (i + 1) * HEAD_SIZE
+        o0[:, low:high] = o[:ROWS]
+        swap_ref[:, low:high] = o[ROWS:]
+        dq0[:, low:high] = dq[:ROWS]
+        swap_ref[:, CORE_Q + low : CORE_Q + high] = dq[ROWS:]
+    for kvh, d in enumerate((first_dk[...], dk)):
         mine = slice(kvh * HEAD_SIZE, (kvh + 1) * HEAD_SIZE)
-        key = jnp.concatenate([p[:, cols] for p in ps], axis=0)
-        far = rv[:, mine].astype(F32)
-        far = jnp.concatenate([far[2 * ROWS :], far[: 2 * ROWS]], axis=0)
-        value = (vp[:, mine].astype(F32) + far).astype(BF)
-        dk = jnp.zeros((4 * ROWS, HEAD_SIZE), F32)
-        dv = jnp.zeros((4 * ROWS, HEAD_SIZE), F32)
-        for i in range(QUERY_PER_KV):
-            head = kvh * QUERY_PER_KV + i
-            qcols = pl.ds(pl.multiple_of(c * CORE_Q + head * HEAD_SIZE, HEAD_SIZE), HEAD_SIZE)
-            low, high = head * HEAD_SIZE, (head + 1) * HEAD_SIZE
-            query = jnp.concatenate([q0[:, qcols], p1[:, QUERY_AT + low : QUERY_AT + high]], axis=0)
-            cot = jnp.concatenate([g0[:, qcols], p1[:, COT_AT + low : COT_AT + high]], axis=0)
-            e = e_ref[head]
-            inv = inv_ref[head * 8 : head * 8 + 8, :][0:1, :]
-            out = jnp.transpose(dot_tt(value, e) * inv).astype(BF)
-            o0[:, low:high] = out[:ROWS]
-            swap_ref[:, low:high] = out[ROWS:]
-            probs = e.astype(F32) * inv
-            term = probs * dot_nt(value, cot)
-            delta = jnp.sum(term, axis=0, keepdims=True)
-            ds = (term - probs * delta).astype(BF)
-            dq = jnp.transpose(dot_tt(key, ds) * factor).astype(BF)
-            dq0[:, low:high] = dq[:ROWS]
-            swap_ref[:, CORE_Q + low : CORE_Q + high] = dq[ROWS:]
-            dk = dk + jnp.dot(ds, query, preferred_element_type=F32)
-            dv = dv + jnp.dot(probs.astype(BF), cot, preferred_element_type=F32)
-        dk = (dk * factor).astype(BF)
-        dk0[:, mine] = dk[:ROWS]
-        dk2[:, mine] = dk[2 * ROWS : 3 * ROWS]
+        dk0[:, mine] = d[:ROWS]
+        dk2[:, mine] = d[2 * ROWS : 3 * ROWS]
         at = 2 * CORE_Q + kvh * HEAD_SIZE
-        swap_ref[:, at : at + HEAD_SIZE] = dk[ROWS : 2 * ROWS]
-        swap_ref[:, at + CORE_KV : at + CORE_KV + HEAD_SIZE] = dk[3 * ROWS :]
-        dv_ref[:, mine] = dv.astype(BF)
-
-
-def attention(e, inv, q, g, ps, vp, rv):
-    return pl.pallas_call(
-        attention_kernel,
+        swap_ref[:, at : at + HEAD_SIZE] = d[ROWS : 2 * ROWS]
+        swap_ref[:, at + CORE_KV : at + CORE_KV + HEAD_SIZE] = d[3 * ROWS :]
+    dv_ref[...] = dv
+
+
+def attention_first(*args):
+    return pl.pallas_call(
+        attention_first_kernel,
+        out_shape=(
+            sds((4 * ROWS, QUERY_PER_KV * HEAD_SIZE)), sds((4 * ROWS, HEAD_SIZE)),
+            sds((4 * ROWS + SPARE, HEAD_SIZE)),
+        ),
+        in_specs=[VM] * 10,
+        out_specs=(VM,) * 3,
+        compiler_params=params(),
+        cost_estimate=cost(5 * 10 * 256 * 512 * 128 * 4, 3e6),
+    )(*args)
+
+
+def attention_second(*args):
+    return pl.pallas_call(
+        attention_second_kernel,
         out_shape=(sds((ROWS, CORE_Q)),) * 2
         + (sds((ROWS, CORE_KV)),) * 2
-        + (sds((ROWS, 2 * CORE_Q + 2 * CORE_KV)), sds((4 * ROWS, CORE_KV))),
-        in_specs=[VM] * 10,
+        + (sds((ROWS, 2 * CORE_Q + 2 * CORE_KV)), sds((4 * ROWS, HEAD_SIZE))),
+        in_specs=[VM] * 12,
         out_specs=(VM,) * 6,
         compiler_params=params(),
-        cost_estimate=cost(2 * 5 * 10 * 256 * 512 * 128 * 4, 6e6),
-    )(e, inv, q, g, *ps, vp, rv)
+        cost_estimate=cost(5 * 10 * 256 * 512 * 128 * 4, 3e6),
+    )(*args)
 
 
 def weight_grad_pair(p, hs, gv, even, odd):
@@ -395,30 +454,47 @@
         out[at + 256 : at + HALF, :] = half
 
 
-def weight_grad_far_kernel(dv, rdv, h0, h1, h2, h3, send, own, gv, gv_keep, gv_send):
+def value_grad_kernel(dv0, dv1, rdv0, rdv1, gv, gv_keep, gv_send):
     for t in range(4):
-        a = dv[t * ROWS : (t + 1) * ROWS, :].astype(F32)
-        b = rdv[(t ^ 2) * ROWS : ((t ^ 2) + 1) * ROWS, :].astype(F32)
-        total = (a + b).astype(BF)
+        parts = []
+        for dv, rdv in ((dv0, rdv0), (dv1, rdv1)):
+            a = dv[t * ROWS : (t + 1) * ROWS, :].astype(F32)
+            b = rdv[(t ^ 2) * ROWS : ((t ^ 2) + 1) * ROWS, :].astype(F32)
+            parts.append(a + b)
+        total = jnp.concatenate(parts, axis=1).astype(BF)
         gv[t * ROWS : (t + 1) * ROWS, :] = total
         half = (t // 2) * ROWS
         if t % 2 == 0:
             gv_keep[half : half + ROWS, :] = total
         else:
             gv_send[half : half + ROWS, :] = total
+
+
+def value_grad(dvs, rdvs):
+    return pl.pallas_call(
+        value_grad_kernel,
+        out_shape=(sds((4 * ROWS, CORE_KV)),) + (sds((2 * ROWS, CORE_KV)),) * 2,
+        in_specs=[VM] * 4,
+        out_specs=(VM,) * 3,
+        compiler_params=params(),
+        cost_estimate=cost(0, 1e6),
+    )(*dvs, *rdvs)
+
+
+def weight_grad_far_kernel(gv, h0, h1, h2, h3, send, own):
     for place, p in enumerate((2, 3)):
         weight_grad_pair(p, (h0, h1, h2, h3), gv, (own, place * HALF), (send, place * HALF))
 
 
-def weight_grad_far(dv, rdv, hs):
+def weight_grad_far(gv, hs):
     return pl.pallas_call(
         weight_grad_far_kernel,
-        out_shape=(sds((2 * HALF, CORE_KV)),) * 2 + (sds((4 * ROWS, CORE_KV)),) + (sds((2 * ROWS, CORE_KV)),) * 2,
-        in_specs=[VM] * 6,
-        out_specs=(VM,) * 5,
+        out_shape=(sds((2 * HALF, CORE_KV)),) * 2,
+        in_specs=[VM] * 5,
+        out_specs=(VM,) * 2,
         compiler_params=params(),
         cost_estimate=cost(512 * WIDE * 256, 4e6),
-    )(dv, rdv, *hs)
+    )(gv, *hs)
 
 
 def weight_grad_near_kernel(gv, h0, h1, h2, h3, send, own):
@@ -442,10 +518,10 @@
     full = full.astype(BF)
     gh0[...] = full[:ROWS]
     far = full[ROWS:]
-    send_a[...] = far[:, : WIDE // 2]
-    send_b[:, : WIDE // 2] = far[:, WIDE // 2 :]
+    send_a[...] = far[:, : CUT]
+    send_b[:, : WIDE - CUT] = far[:, CUT :]
     c = lax.axis_index("seq") % 2
-    at = WIDE // 2
+    at = WIDE - CUT
     send_b[:, pl.ds(pl.multiple_of(at + c * CORE_KV, CORE_KV), CORE_KV)] = dk2[...]
     send_b[:, pl.ds(pl.multiple_of(at + (1 - c) * CORE_KV, CORE_KV), CORE_KV)] = swapped[
         :, 2 * CORE_Q + CORE_KV :
@@ -455,7 +531,7 @@
 def hidden_grad(gv, gvs, wp, wps, dk2, swapped):
     return pl.pallas_call(
         hidden_grad_kernel,
-        out_shape=(sds((ROWS, WIDE)), sds((ROWS, WIDE // 2)), sds((ROWS, WIDE // 2 + 2 * CORE_KV))),
+        out_shape=(sds((ROWS, WIDE)), sds((ROWS, CUT)), sds((ROWS, WIDE - CUT + 2 * CORE_KV))),
         in_specs=[VM] * 6,
         out_specs=(VM,) * 3,
         compiler_params=params(),
@@ -464,8 +540,8 @@
 
 
 def hidden_join_kernel(own_ref, far_a, far_b, dk0, swapped, o_ref, dk_ref, far_ref):
-    far_ref[:, 0 : WIDE // 2] = far_a[...]
-    far_ref[:, WIDE // 2 :] = far_b[:, : WIDE // 2]
+    far_ref[:, 0:CUT] = far_a[...]
+    far_ref[:, CUT:] = far_b[:, : WIDE - CUT]
     s = lax.axis_index("seq")
     y, c = s // 2, s % 2
     r = lax.axis_index("dp")
@@ -485,7 +561,7 @@
         o_ref[:, pl.ds(at0, CHUNK)] = jnp.where(low, part0, turn(part1))
         o_ref[:, pl.ds(at1, CHUNK)] = jnp.where(low, turn(part0), part1)
     for place, near in ((c, dk0[...]), (1 - c, swapped[:, 2 * CORE_Q : 2 * CORE_Q + CORE_KV])):
-        far = far_b[:, pl.ds(pl.multiple_of(WIDE // 2 + place * CORE_KV, CORE_KV), CORE_KV)]
+        far = far_b[:, pl.ds(pl.multiple_of(WIDE - CUT + place * CORE_KV, CORE_KV), CORE_KV)]
         dk_ref[:, pl.ds(pl.multiple_of(place * CORE_KV, CORE_KV), CORE_KV)] = (
             near.astype(F32) + far.astype(F32)
         ).astype(BF)
@@ -595,41 +671,45 @@
     q, g = queries[0], cotangent[0]
     send, p0, w0 = pack(hidden[0], keys[0], doc_ids, value_weight, q, g)
     p2 = swap(send, "seq", 2)
-    w6, w4, w2 = swap(w0, "dp", 6), swap(w0, "dp", 4), swap(w0, "dp", 2)
-    w1 = swap(w0, "dp", 1)
+    w6, w4 = swap(w0, "dp", 6), swap(w0, "dp", 4)
+    p1 = swap(p0, "seq", 1)
+    later = after(w0, p1)
+    w1, w2 = swap(later, "dp", 1), swap(later, "dp", 2)
     w3 = swap(w1, "dp", 2)
-    p1 = swap(p0, "seq", 1)
-    w7, w5 = swap(w6, "dp", 1), swap(after(w4, w2), "dp", 1)
+    own, w0 = relay(after(p0, p1), w0)
+    w7, w5 = swap(after(w6, own), "dp", 1), swap(after(w4, w2), "dp", 1)
     p3 = swap(after(p2, w1, w3, w5, w7), "seq", 1)
-    ps = (p0, p1, p2, p3)
-    vp3, wp = partial_values((p0, p1, p2), (w0, w1, w2, w3, w4, w5, w6, w7))
-    vp = last_values(vp3, p3, wp)
-    rv = swap(vp, "seq", 2)
-    e, inv = scores(after(q, vp), ps)
+    ps = (own, p1, p2, p3)
+    vp3, wp = partial_values((own, p1, p2), (w0, w1, w2, w3, w4, w5, w6, w7))
+    vp0, vp1 = last_values(vp3, p3, wp)
+    rv0, rv1 = swap(vp0, "seq", 2), swap(vp1, "seq", 2)
+    e, inv = scores(after(q, vp0), ps)
     wps = swap(wp, "seq", 1)
-    o0, dq0, dk0, dk2, swap_out, dv = attention(e, inv, q, g, ps, vp, rv)
-    rdv = swap(dv, "seq", 2)
-    send_a, own_a, gv, gv_keep, gv_send = weight_grad_far(dv, rdv, ps)
+    first, first_dk, dv0 = attention_first(e, inv, q, g, *ps, vp0, rv0)
+    rdv0 = swap(dv0, "seq", 2)
+    o0, dq0, dk0, dk2, swap_out, dv1 = attention_second(e, inv, q, g, *ps, vp1, rv1, first, first_dk)
+    rdv1 = swap(dv1, "seq", 2)
+    gv, gv_keep, gv_send = value_grad((dv0, dv1), (rdv0, rdv1))
+    send_a, own_a = weight_grad_far(gv, ps)
     send_b, own_b = weight_grad_near(gv, ps)
     far_a = swap(send_a, "dp", 1)
     far_b = swap(send_b, "dp", 2)
-    gvs = swap(after(gv_send, send_b), "seq", 1)
-    swapped = swap(swap_out, "seq", 1)
+    gvs = swap(gv_send, "seq", 1)
+    swapped = swap(after(swap_out, gv), "seq", 1)
     gh0, gh_a, gh_b = hidden_grad(gv_keep, gvs, wp, wps, dk2, swapped)
     s4, s6 = add_pair(own_a, far_a)
     t6, t4 = swap(s6, "dp", 6), swap(s4, "dp", 4)
     t46 = add_two(t4, t6)
     s0, s1 = add_pair(own_b, far_b)
-    t1 = swap(s1, "dp", 1)
     gh_far = swap(gh_a, "seq", 2), swap(gh_b, "seq", 2)
     attn_out, grad_queries = heads_join(o0, dq0, swapped)
+    s1, attn_out, grad_queries = lax.optimization_barrier((s1, attn_out, grad_queries))
+    t1 = swap(s1, "dp", 1)
     d0 = add_three(t46, s0, t1)
     d2 = swap(d0, "seq", 2)
     d1 = swap(d0, "seq", 1)
     grad_hidden, grad_keys = hidden_join(gh0, gh_far, dk0, swapped)
-    d2, grad_hidden, grad_keys, attn_out, grad_queries = lax.optimization_barrier(
-        (d2, grad_hidden, grad_keys, attn_out, grad_queries)
-    )
+    d2, grad_hidden, grad_keys = lax.optimization_barrier((d2, grad_hidden, grad_keys))
     d3 = swap(d2, "seq", 1)
     grad_weight = weight_join((d0, d1, d2, d3))
     return attn_out[None], grad_queries[None], grad_keys[None], grad_hidden[None], grad_weight

time: 89.6 us -> 84.4 us (0.942)
  waiting for transfers between devices: 43.9 us -> 34.5 us
  starting transfers between devices: 24.9 us -> 29.7 us
    ppermute x25 -> x27, waiting for transfers between devices: 43.9 us -> 34.5 us  [swap(): return lax.ppermute(x, axis, [(i, i ^ k) for i in range(size)])]
    ppermute x25 -> x27, starting transfers between devices: 24.9 us -> 29.7 us  [swap(): return lax.ppermute(x, axis, [(i, i ^ k) for i in range(size)])]
    pallas_call x2 -> x5, Pallas kernels: 3.61 us -> 4.12 us  [the longest x1 1.83 us: attention_second(): pl.pallas_call(attention_second_kernel, out_shape=(sds((ROWS, CORE_Q)),)...]
    unnamed x10 -> x8, local copies, waits for them, and re-layouts: 2.78 us -> 2.3 us
  transfers between devices with their start and end apart: 25 -> 27, of which waited for: 12 -> 11; matrix products, arithmetic and copies ran while one was open for 0% -> 0% of each run, Pallas kernels for 12% -> 14%
where the time goes in v3:
time: 84.4 us; the launch traced here: 84.3 us
  waiting for transfers between devices  34.5 us (41%)
  starting transfers between devices  29.7 us (35%)
  Pallas kernels  16.9 us (20%)
  local copies, waits for them, and re-layouts  2.3 us (3%)
    ppermute x27, waiting for transfers between devices, swap(): return lax.ppermute(x, axis, [(i, i ^ k) for i in range(size)])  34.5 us
    ppermute x27, starting transfers between devices, swap(): return lax.ppermute(x, axis, [(i, i ^ k) for i in range(size)])  29.7 us
    pallas_call x1, Pallas kernels, pack(): pl.pallas_call(pack_kernel, out_shape=(sds((ROWS, QUERY_AT)), sds((ROWS,...  3.84 us
    unnamed x8, local copies, waits for them, and re-layouts  2.3 us
    pallas_call x1, Pallas kernels, attention_second(): pl.pallas_call(attention_second_kernel, out_shape=(sds((ROWS, CORE_Q)),)...  1.83 us
    pallas_call x1, Pallas kernels, attention_first(): pl.pallas_call(attention_first_kernel, out_shape=(sds((4 * ROWS, QUERY_PE...  1.82 us
    pallas_call x1, Pallas kernels, scores(): pl.pallas_call(scores_kernel, out_shape=(sds((10, 4 * ROWS, 2 * ROWS)), s...  1.71 us
  transfers between devices with their start and end apart: 27, of which 11 were waited for; matrix products, arithmetic and copies ran while one was open for 0% of the time, Pallas kernels for 14%

profile of v3, /device:TPU:0, one launch (start us, length us, event | category | flops | bytes accessed | tf_op | source)
XLA Modules:
  0.0 84.3 jit_solution(8182232803185500885)
XLA Ops:
  0.6 3.8 %shard_map.101 = (bf16[128,3200]{1,0:T(8,128)(2,1)}, bf16[128,5760]{1,0:T(8,128)(2,1)}, bf16[320,256]{1,0:T(8,128)(2,1)}) custom-call(bf16[128,5120]{1,0:T(8,128)(2,1)} %bitcast.15, bf16[128,512]{1,0:T(8,128)(2,1)} %bitcast.16, s32[1,128]{1,0:T(1,128)} %doc.1, bf16[640,512]{1,0:T(8,128)(2,1)} %w.1, bf16[128,2560]{1,0:T(8,128)(2,1)} %bitcast.8, ...), custom_call_target="tpu_custom_call" | custom-call | bytes 3000000 | tf_op jit(solution)/shard_map/pallas_call | solution.py:233
  4.9 2.5 %collective-permute-start.1 = (bf16[128,3200]{1,0:T(8,128)(2,1)}, bf16[128,3200]{1,0:T(8,128)(2,1)S(1)}, u32[]{:S(2)}, u32[]{:S(2)}) collective-permute-start(bf16[128,3200]{1,0:T(8,128)(2,1)} %get-tuple-element.60), channel_id=1, source_target_pairs={{0,2},{1,3},{2,0},{3,1},{4,6},{5,7},{6,4},{7,5},{8,10},{9,11},{10,... | collective-permute-start | bytes 2457608 | tf_op jit(solution)/shard_map/ppermute | solution.py:184
  7.4 3.6 %collective-permute-start.7 = (bf16[320,256]{1,0:T(8,128)(2,1)}, bf16[320,256]{1,0:T(8,128)(2,1)S(1)}, u32[]{:S(2)}, u32[]{:S(2)}) collective-permute-start(bf16[320,256]{1,0:T(8,128)(2,1)} %get-tuple-element.62.w), channel_id=1, source_target_pairs={{0,24},{4,28},{8,16},{12,20},{16,8},{20,12},{24,0},{28,4},{1,25},{... | collective-permute-start | bytes 491528 | tf_op jit(solution)/shard_map/ppermute | solution.py:184
  11.8 1.5 %collective-permute-start.2 = (bf16[320,256]{1,0:T(8,128)(2,1)}, bf16[320,256]{1,0:T(8,128)(2,1)S(1)}, u32[]{:S(2)}, u32[]{:S(2)}) collective-permute-start(bf16[320,256]{1,0:T(8,128)(2,1)} %get-tuple-element.62.w), channel_id=1, source_target_pairs={{0,4},{4,0},{8,12},{12,8},{16,20},{20,16},{24,28},{28,24},{1,5},{5... | collective-permute-start | bytes 491528 | tf_op jit(solution)/shard_map/ppermute | solution.py:184
  13.3 1.4 %copy-done = bf16[128,5760]{1,0:T(8,128)(2,1)S(1)} copy-done((bf16[128,5760]{1,0:T(8,128)(2,1)S(1)}, bf16[128,5760]{1,0:T(8,128)(2,1)}, u32[]{:S(2)}) %copy-start) | copy-done | bytes 1474584
  16.6 1.5 %collective-permute-start.8 = (bf16[320,256]{1,0:T(8,128)(2,1)S(1)}, bf16[320,256]{1,0:T(8,128)(2,1)S(1)}, u32[]{:S(2)}, u32[]{:S(2)}) collective-permute-start(bf16[320,256]{1,0:T(8,128)(2,1)S(1)} %collective-permute-done.7.w6), channel_id=1, source_target_pairs={{0,4},{4,0},{8,12},{12,8},{16,20},{20,16},{24,28},{28,24},{1,5},{5... | collective-permute-start | bytes 491528 | tf_op jit(solution)/shard_map/ppermute | solution.py:184
  18.1 7.5 %collective-permute-done.5.w4 = bf16[320,256]{1,0:T(8,128)(2,1)S(1)} collective-permute-done((bf16[320,256]{1,0:T(8,128)(2,1)}, bf16[320,256]{1,0:T(8,128)(2,1)S(1)}, u32[]{:S(2)}, u32[]{:S(2)}) %collective-permute-start.5) | collective-permute-done | bytes 163872 | tf_op jit(solution)/shard_map/ppermute | solution.py:184
  25.6 1.6 %collective-permute-start.6 = (bf16[320,256]{1,0:T(8,128)(2,1)S(1)}, bf16[320,256]{1,0:T(8,128)(2,1)S(1)}, u32[]{:S(2)}, u32[]{:S(2)}) collective-permute-start(bf16[320,256]{1,0:T(8,128)(2,1)S(1)} %collective-permute-done.5.w4), channel_id=1, source_target_pairs={{0,4},{4,0},{8,12},{12,8},{16,20},{20,16},{24,28},{28,24},{1,5},{5... | collective-permute-start | bytes 491528 | tf_op jit(solution)/shard_map/ppermute | solution.py:184
  27.1 3.9 %collective-permute-done.4.w3 = bf16[320,256]{1,0:T(8,128)(2,1)S(1)} collective-permute-done((bf16[320,256]{1,0:T(8,128)(2,1)S(1)}, bf16[320,256]{1,0:T(8,128)(2,1)S(1)}, u32[]{:S(2)}, u32[]{:S(2)}) %collective-permute-start.4) | collective-permute-done | bytes 163872 | tf_op jit(solution)/shard_map/ppermute | solution.py:184
  32.4 1.1 %collective-permute-done.9.h3.p3 = bf16[128,3200]{1,0:T(8,128)(2,1)S(1)} collective-permute-done((bf16[128,3200]{1,0:T(8,128)(2,1)S(1)}, bf16[128,3200]{1,0:T(8,128)(2,1)S(1)}, u32[]{:S(2)}, u32[]{:S(2)}) %collective-permute-start.9) | collective-permute-done | bytes 819232 | tf_op jit(solution)/shard_map/ppermute | solution.py:184
  34.4 1.5 %collective-permute-start.11 = (bf16[512,128]{1,0:T(8,128)(2,1)S(1)}, bf16[512,128]{1,0:T(8,128)(2,1)S(1)}, u32[]{:S(2)}, u32[]{:S(2)}) collective-permute-start(bf16[512,128]{1,0:T(8,128)(2,1)S(1)} %get-tuple-element.73.vp), channel_id=1, source_target_pairs={{0,2},{1,3},{2,0},{3,1},{4,6},{5,7},{6,4},{7,5},{8,10},{9,11},{10,... | collective-permute-start | bytes 393224 | tf_op jit(solution)/shard_map/ppermute | solution.py:184
  35.9 1.7 %shard_map.105 = (bf16[10,512,256]{2,1,0:T(8,128)(2,1)S(1)}, f32[80,256]{1,0:T(8,128)S(1)}) custom-call(bf16[128,2560]{1,0:T(8,128)(2,1)S(1)} %bitcast.9, bf16[128,3200]{1,0:T(8,128)(2,1)S(1)} %get-tuple-element.59.h0.p0, bf16[128,5760]{1,0:T(8,128)(2,1)S(1)} %collective-permute-done.h1.p1, bf16[128,3200]{1,0:T(8,128)(2,1)S(1)} %collective-permute-done.1.h2.p2, ...), custom_call_target="tpu_custom_call" | custom-call | flops 2684354560 | bytes 6000000 | tf_op jit(solution)/shard_map/pallas_call | solution.py:335
  37.6 2.6 %collective-permute-done.10.rv = bf16[512,128]{1,0:T(8,128)(2,1)S(1)} collective-permute-done((bf16[512,128]{1,0:T(8,128)(2,1)S(1)}, bf16[512,128]{1,0:T(8,128)(2,1)S(1)}, u32[]{:S(2)}, u32[]{:S(2)}) %collective-permute-start.10) | collective-permute-done | bytes 131104 | tf_op jit(solution)/shard_map/ppermute | solution.py:184
  40.2 1.8 %shard_map.106 = (bf16[512,640]{1,0:T(8,128)(2,1)S(1)}, bf16[512,128]{1,0:T(8,128)(2,1)S(1)}, bf16[528,128]{1,0:T(8,128)(2,1)S(1)}) custom-call(bf16[10,512,256]{2,1,0:T(8,128)(2,1)S(1)} %get-tuple-element.70.e_ref, f32[80,256]{1,0:T(8,128)S(1)} %get-tuple-element.71.inv_ref, bf16[128,2560]{1,0:T(8,128)(2,1)S(1)} %bitcast.10, ...), custom_call_target="tpu_custom_call" | custom-call | flops 3355443200 | bytes 3000000 | tf_op jit(solution)/shard_map/pallas_call | solution.py:416
  42.6 1.8 %shard_map.107 = (bf16[128,1280]{1,0:T(8,128)(2,1)S(1)}, bf16[128,1280]{1,0:T(8,128)(2,1)S(1)}, bf16[128,256]{1,0:T(8,128)(2,1)S(1)}, bf16[128,256]{1,0:T(8,128)...) custom-call(bf16[10,512,256]{2,1,0:T(8,128)(2,1)S(1)} %get-tuple-element.70.e_ref, ...), custom_call_target="tpu_custom_call" | custom-call | flops 3355443200 | bytes 3000000 | tf_op jit(solution)/shard_map/pallas_call | solution.py:430
  44.5 1.6 %collective-permute-start.13 = (bf16[512,128]{1,0:T(8,128)(2,1)S(1)}, bf16[512,128]{1,0:T(8,128)(2,1)S(1)}, u32[]{:S(2)}, u32[]{:S(2)}) collective-permute-start(bf16[512,128]{1,0:T(8,128)(2,1)S(1)} %get-tuple-element.76.dv1), channel_id=1, source_target_pairs={{0,2},{1,3},{2,0},{3,1},{4,6},{5,7},{6,4},{7,5},{8,10},{9,11},{10,... | collective-permute-start | bytes 393224 | tf_op jit(solution)/shard_map/ppermute | solution.py:184
  46.1 3.9 %collective-permute-done.13.rdv1 = bf16[512,128]{1,0:T(8,128)(2,1)S(1)} collective-permute-done((bf16[512,128]{1,0:T(8,128)(2,1)S(1)}, bf16[512,128]{1,0:T(8,128)(2,1)S(1)}, u32[]{:S(2)}, u32[]{:S(2)}) %collective-permute-start.13) | collective-permute-done | bytes 131104 | tf_op jit(solution)/shard_map/ppermute | solution.py:184
  51.5 1.6 %collective-permute-start.16 = (bf16[640,256]{1,0:T(8,128)(2,1)S(1)}, bf16[640,256]{1,0:T(8,128)(2,1)S(1)}, u32[]{:S(2)}, u32[]{:S(2)}) collective-permute-start(bf16[640,256]{1,0:T(8,128)(2,1)S(1)} %get-tuple-element.90), channel_id=1, source_target_pairs={{0,4},{4,0},{8,12},{12,8},{16,20},{20,16},{24,28},{28,24},{1,5},{5... | collective-permute-start | bytes 983048 | tf_op jit(solution)/shard_map/ppermute | solution.py:184
  53.9 1.8 %collective-permute-start.14 = (bf16[640,256]{1,0:T(8,128)(2,1)S(1)}, bf16[640,256]{1,0:T(8,128)(2,1)S(1)}, u32[]{:S(2)}, u32[]{:S(2)}) collective-permute-start(bf16[640,256]{1,0:T(8,128)(2,1)S(1)} %get-tuple-element.79), channel_id=1, source_target_pairs={{0,8},{4,12},{8,0},{12,4},{16,24},{20,28},{24,16},{28,20},{1,9},{5... | collective-permute-start | bytes 983048 | tf_op jit(solution)/shard_map/ppermute | solution.py:184
  56.7 1.1 %collective-permute-start.24 = (bf16[128,2304]{1,0:T(8,128)(2,1)S(1)}, bf16[128,2304]{1,0:T(8,128)(2,1)S(1)}, u32[]{:S(2)}, u32[]{:S(2)}) collective-permute-start(bf16[128,2304]{1,0:T(8,128)(2,1)S(1)} %get-tuple-element.100), channel_id=1, source_target_pairs={{0,2},{1,3},{2,0},{3,1},{4,6},{5,7},{6,4},{7,5},{8,10},{9,11},{10,... | collective-permute-start | bytes 1769480 | tf_op jit(solution)/shard_map/ppermute | solution.py:184
  57.8 3.4 %collective-permute-done.16.b = bf16[640,256]{1,0:T(8,128)(2,1)S(1)} collective-permute-done((bf16[640,256]{1,0:T(8,128)(2,1)S(1)}, bf16[640,256]{1,0:T(8,128)(2,1)S(1)}, u32[]{:S(2)}, u32[]{:S(2)}) %collective-permute-start.16) | collective-permute-done | bytes 327712 | tf_op jit(solution)/shard_map/ppermute | solution.py:184
  61.3 2.8 %collective-permute-start.17 = (bf16[320,256]{1,0:T(8,128)(2,1)S(1)}, bf16[320,256]{1,0:T(8,128)(2,1)S(1)}, u32[]{:S(2)}, u32[]{:S(2)}) collective-permute-start(bf16[320,256]{1,0:T(8,128)(2,1)S(1)} %get-tuple-element.91), channel_id=1, source_target_pairs={{0,16},{4,20},{8,24},{12,28},{16,0},{20,4},{24,8},{28,12},{1,17},{... | collective-permute-start | bytes 491528 | tf_op jit(solution)/shard_map/ppermute | solution.py:184
  64.2 1.4 %collective-permute-start.18 = (bf16[320,256]{1,0:T(8,128)(2,1)S(1)}, bf16[320,256]{1,0:T(8,128)(2,1)S(1)}, u32[]{:S(2)}, u32[]{:S(2)}) collective-permute-start(bf16[320,256]{1,0:T(8,128)(2,1)S(1)} %get-tuple-element.92), channel_id=1, source_target_pairs={{0,24},{4,28},{8,16},{12,20},{16,8},{20,12},{24,0},{28,4},{1,25},{... | collective-permute-start | bytes 491528 | tf_op jit(solution)/shard_map/ppermute | solution.py:184
  65.6 1.2 %shard_map.111 = (bf16[128,2560]{1,0:T(8,128)(2,1)}, bf16[128,2560]{1,0:T(8,128)(2,1)}) custom-call(bf16[128,1280]{1,0:T(8,128)(2,1)S(1)} %get-tuple-element.81.o0, bf16[128,1280]{1,0:T(8,128)(2,1)S(1)} %get-tuple-element.82.dq0, bf16[128,3072]{1,0:T(8,128)(2,1)S(1)} %collective-permute-done.15.swapped), custom_call_target="tpu_custom_call" | custom-call | bytes 4000000 | tf_op jit(solution)/shard_map/pallas_call | solution.py:593
  66.8 1.5 %collective-permute-start.19 = (bf16[320,256]{1,0:T(8,128)(2,1)S(1)}, bf16[320,256]{1,0:T(8,128)(2,1)S(1)}, u32[]{:S(2)}, u32[]{:S(2)}) collective-permute-start(bf16[320,256]{1,0:T(8,128)(2,1)S(1)} %get-tuple-element.94), channel_id=1, source_target_pairs={{0,4},{4,0},{8,12},{12,8},{16,20},{20,16},{24,28},{28,24},{1,5},{5... | collective-permute-start | bytes 491528 | tf_op jit(solution)/shard_map/ppermute | solution.py:184
  68.2 1.1 %collective-permute-start.23 = (bf16[128,768]{1,0:T(8,128)(2,1)S(1)}, bf16[128,768]{1,0:T(8,128)(2,1)S(1)}, u32[]{:S(2)}, u32[]{:S(2)}) collective-permute-start(bf16[128,768]{1,0:T(8,128)(2,1)S(1)} %get-tuple-element.99), channel_id=1, source_target_pairs={{0,2},{1,3},{2,0},{3,1},{4,6},{5,7},{6,4},{7,5},{8,10},{9,11},{10,... | collective-permute-start | bytes 589832 | tf_op jit(solution)/shard_map/ppermute | solution.py:184
  69.3 6.9 %collective-permute-done.17.a = bf16[320,256]{1,0:T(8,128)(2,1)S(1)} collective-permute-done((bf16[320,256]{1,0:T(8,128)(2,1)S(1)}, bf16[320,256]{1,0:T(8,128)(2,1)S(1)}, u32[]{:S(2)}, u32[]{:S(2)}) %collective-permute-start.17) | collective-permute-done | bytes 163872 | tf_op jit(solution)/shard_map/ppermute | solution.py:184
  76.3 1.2 %collective-permute-start.20 = (bf16[320,256]{1,0:T(8,128)(2,1)S(1)}, bf16[320,256]{1,0:T(8,128)(2,1)S(1)}, u32[]{:S(2)}, u32[]{:S(2)}) collective-permute-start(bf16[320,256]{1,0:T(8,128)(2,1)S(1)} %shard_map.115.p0), channel_id=1, source_target_pairs={{0,2},{1,3},{2,0},{3,1},{4,6},{5,7},{6,4},{7,5},{8,10},{9,11},{10,... | collective-permute-start | bytes 491528 | tf_op jit(solution)/shard_map/ppermute | solution.py:184
  77.5 1.4 %shard_map.117 = (bf16[128,5120]{1,0:T(8,128)(2,1)}, bf16[128,512]{1,0:T(8,128)(2,1)}) custom-call(bf16[128,2560]{1,0:T(8,128)(2,1)S(1)} %get-tuple-element.98.own_ref, bf16[128,768]{1,0:T(8,128)(2,1)S(1)} %collective-permute-done.23.far_a, bf16[128,2304]{1,0:T(8,128)(2,1)S(1)} %collective-permute-done.24.far_b, ...), custom_call_target="tpu_custom_call" | custom-call | bytes 3000000 | tf_op jit(solution)/shard_map/pallas_call | solution.py:571
  78.9 2.8 %collective-permute-done.20.p2 = bf16[320,256]{1,0:T(8,128)(2,1)S(1)} collective-permute-done((bf16[320,256]{1,0:T(8,128)(2,1)S(1)}, bf16[320,256]{1,0:T(8,128)(2,1)S(1)}, u32[]{:S(2)}, u32[]{:S(2)}) %collective-permute-start.20) | collective-permute-done | bytes 163872 | tf_op jit(solution)/shard_map/ppermute | solution.py:184
  81.7 1.4 %collective-permute-done.26.p3 = bf16[320,256]{1,0:T(8,128)(2,1)S(1)} collective-permute-done((bf16[320,256]{1,0:T(8,128)(2,1)S(1)}, bf16[320,256]{1,0:T(8,128)(2,1)S(1)}, u32[]{:S(2)}, u32[]{:S(2)}) %collective-permute-start.26) | collective-permute-done | bytes 163872 | tf_op jit(solution)/shard_map/ppermute | solution.py:184
  83.1 1.2 %shard_map.118 = f32[640,512]{1,0:T(8,128)} custom-call(bf16[320,256]{1,0:T(8,128)(2,1)S(1)} %shard_map.115.p0, bf16[320,256]{1,0:T(8,128)(2,1)S(1)} %collective-permute-done.25.p1, bf16[320,256]{1,0:T(8,128)(2,1)S(1)} %collective-permute-done.20.p2, bf16[320,256]{1,0:T(8,128)(2,1)S(1)} %collective-permute-done.26.p3), custom_call_target="tpu_custom_call" | custom-call | bytes 2000000 | tf_op jit(solution)/shard_map/pallas_call | solution.py:660
  (48 shorter events, 9.5 us)
Async XLA Ops:
  4.5 6.6 %collective-permute-start = (bf16[128,5760]{1,0:T(8,128)(2,1)}, bf16[128,5760]{1,0:T(8,128)(2,1)S(1)}, u32[]{:S(2)}, u32[]{:S(2)}) collective-permute-start(bf16[128,5760]{1,0:T(8,128)(2,1)} %get-tuple-element.57.p), channel_id=1, source_target_pairs={{0,1},{1,0},{2,3},{3,2},{4,5},{5,4},{6,7},{7,6},{8,9},{9,8},{10,11... | collective-permute-start | bytes 4423688 | tf_op jit(solution)/shard_map/ppermute | solution.py:184
  4.9 22.2 %collective-permute-start.1 = (bf16[128,3200]{1,0:T(8,128)(2,1)}, bf16[128,3200]{1,0:T(8,128)(2,1)S(1)}, u32[]{:S(2)}, u32[]{:S(2)}) collective-permute-start(bf16[128,3200]{1,0:T(8,128)(2,1)} %get-tuple-element.60), channel_id=1, source_target_pairs={{0,2},{1,3},{2,0},{3,1},{4,6},{5,7},{6,4},{7,5},{8,10},{9,11},{10,... | collective-permute-start | bytes 2457608 | tf_op jit(solution)/shard_map/ppermute | solution.py:184
  7.4 9.1 %collective-permute-start.7 = (bf16[320,256]{1,0:T(8,128)(2,1)}, bf16[320,256]{1,0:T(8,128)(2,1)S(1)}, u32[]{:S(2)}, u32[]{:S(2)}) collective-permute-start(bf16[320,256]{1,0:T(8,128)(2,1)} %get-tuple-element.62.w), channel_id=1, source_target_pairs={{0,24},{4,28},{8,16},{12,20},{16,8},{20,12},{24,0},{28,4},{1,25},{... | collective-permute-start | bytes 491528 | tf_op jit(solution)/shard_map/ppermute | solution.py:184
  11.0 14.5 %collective-permute-start.5 = (bf16[320,256]{1,0:T(8,128)(2,1)}, bf16[320,256]{1,0:T(8,128)(2,1)S(1)}, u32[]{:S(2)}, u32[]{:S(2)}) collective-permute-start(bf16[320,256]{1,0:T(8,128)(2,1)} %get-tuple-element.62.w), channel_id=1, source_target_pairs={{0,16},{4,20},{8,24},{12,28},{16,0},{20,4},{24,8},{28,12},{1,17},{... | collective-permute-start | bytes 491528 | tf_op jit(solution)/shard_map/ppermute | solution.py:184
  11.1 14.5 %collective-permute-start.3 = (bf16[320,256]{1,0:T(8,128)(2,1)}, bf16[320,256]{1,0:T(8,128)(2,1)S(1)}, u32[]{:S(2)}, u32[]{:S(2)}) collective-permute-start(bf16[320,256]{1,0:T(8,128)(2,1)} %get-tuple-element.62.w), channel_id=1, source_target_pairs={{0,8},{4,12},{8,0},{12,4},{16,24},{20,28},{24,16},{28,20},{1,9},{5... | collective-permute-start | bytes 491528 | tf_op jit(solution)/shard_map/ppermute | solution.py:184
  11.8 13.7 %collective-permute-start.2 = (bf16[320,256]{1,0:T(8,128)(2,1)}, bf16[320,256]{1,0:T(8,128)(2,1)S(1)}, u32[]{:S(2)}, u32[]{:S(2)}) collective-permute-start(bf16[320,256]{1,0:T(8,128)(2,1)} %get-tuple-element.62.w), channel_id=1, source_target_pairs={{0,4},{4,0},{8,12},{12,8},{16,20},{20,16},{24,28},{28,24},{1,5},{5... | collective-permute-start | bytes 491528 | tf_op jit(solution)/shard_map/ppermute | solution.py:184
  13.3 1.4 %copy-start = (bf16[128,5760]{1,0:T(8,128)(2,1)S(1)}, bf16[128,5760]{1,0:T(8,128)(2,1)}, u32[]{:S(2)}) copy-start(bf16[128,5760]{1,0:T(8,128)(2,1)} %get-tuple-element.57.p) | copy-start | bytes 4423684
  14.7 0.9 %copy-start.3 = (bf16[320,256]{1,0:T(8,128)(2,1)S(1)}, bf16[320,256]{1,0:T(8,128)(2,1)}, u32[]{:S(2)}) copy-start(bf16[320,256]{1,0:T(8,128)(2,1)} %get-tuple-element.62.w) | copy-start | bytes 491524
  16.6 10.5 %collective-permute-start.8 = (bf16[320,256]{1,0:T(8,128)(2,1)S(1)}, bf16[320,256]{1,0:T(8,128)(2,1)S(1)}, u32[]{:S(2)}, u32[]{:S(2)}) collective-permute-start(bf16[320,256]{1,0:T(8,128)(2,1)S(1)} %collective-permute-done.7.w6), channel_id=1, source_target_pairs={{0,4},{4,0},{8,12},{12,8},{16,20},{20,16},{24,28},{28,24},{1,5},{5... | collective-permute-start | bytes 491528 | tf_op jit(solution)/shard_map/ppermute | solution.py:184
  25.5 5.5 %collective-permute-start.4 = (bf16[320,256]{1,0:T(8,128)(2,1)S(1)}, bf16[320,256]{1,0:T(8,128)(2,1)S(1)}, u32[]{:S(2)}, u32[]{:S(2)}) collective-permute-start(bf16[320,256]{1,0:T(8,128)(2,1)S(1)} %collective-permute-done.2.w1), channel_id=1, source_target_pairs={{0,8},{4,12},{8,0},{12,4},{16,24},{20,28},{24,16},{28,20},{1,9},{5... | collective-permute-start | bytes 491528 | tf_op jit(solution)/shard_map/ppermute | solution.py:184
  25.6 5.6 %collective-permute-start.6 = (bf16[320,256]{1,0:T(8,128)(2,1)S(1)}, bf16[320,256]{1,0:T(8,128)(2,1)S(1)}, u32[]{:S(2)}, u32[]{:S(2)}) collective-permute-start(bf16[320,256]{1,0:T(8,128)(2,1)S(1)} %collective-permute-done.5.w4), channel_id=1, source_target_pairs={{0,4},{4,0},{8,12},{12,8},{16,20},{20,16},{24,28},{28,24},{1,5},{5... | collective-permute-start | bytes 491528 | tf_op jit(solution)/shard_map/ppermute | solution.py:184
  31.1 2.3 %collective-permute-start.9 = (bf16[128,3200]{1,0:T(8,128)(2,1)S(1)}, bf16[128,3200]{1,0:T(8,128)(2,1)S(1)}, u32[]{:S(2)}, u32[]{:S(2)}) collective-permute-start(bf16[128,3200]{1,0:T(8,128)(2,1)S(1)} %collective-permute-done.1.h2.p2), channel_id=1, source_target_pairs={{0,1},{1,0},{2,3},{3,2},{4,5},{5,4},{6,7},{7,6},{8,9},{9,8},{10,11... | collective-permute-start | bytes 2457608 | tf_op jit(solution)/shard_map/ppermute | solution.py:184
  31.8 4.1 %copy-start.1 = (bf16[1,128,2560]{2,1,0:T(8,128)(2,1)S(1)}, bf16[1,128,2560]{2,1,0:T(8,128)(2,1)}, u32[]{:S(2)}) copy-start(bf16[1,128,2560]{2,1,0:T(8,128)(2,1)} %param.7) | copy-start | bytes 1966084
  31.8 23.9 %collective-permute-start.22 = (bf16[2560,256]{1,0:T(8,128)(2,1)S(1)}, bf16[2560,256]{1,0:T(8,128)(2,1)S(1)}, u32[]{:S(2)}, u32[]{:S(2)}) collective-permute-start(bf16[2560,256]{1,0:T(8,128)(2,1)S(1)} %get-tuple-element.67.wp), channel_id=1, source_target_pairs={{0,1},{1,0},{2,3},{3,2},{4,5},{5,4},{6,7},{7,6},{8,9},{9,8},{10,11... | collective-permute-start | bytes 3932168 | tf_op jit(solution)/shard_map/ppermute | solution.py:184
  33.8 6.4 %collective-permute-start.10 = (bf16[512,128]{1,0:T(8,128)(2,1)S(1)}, bf16[512,128]{1,0:T(8,128)(2,1)S(1)}, u32[]{:S(2)}, u32[]{:S(2)}) collective-permute-start(bf16[512,128]{1,0:T(8,128)(2,1)S(1)} %get-tuple-element.68.vp), channel_id=1, source_target_pairs={{0,2},{1,3},{2,0},{3,1},{4,6},{5,7},{6,4},{7,5},{8,10},{9,11},{10,... | collective-permute-start | bytes 393224 | tf_op jit(solution)/shard_map/ppermute | solution.py:184
  34.4 5.9 %copy-start.2 = (bf16[1,128,2560]{2,1,0:T(8,128)(2,1)S(1)}, bf16[1,128,2560]{2,1,0:T(8,128)(2,1)}, u32[]{:S(2)}) copy-start(bf16[1,128,2560]{2,1,0:T(8,128)(2,1)} %param.11) | copy-start | bytes 1966084
  34.4 8.2 %collective-permute-start.11 = (bf16[512,128]{1,0:T(8,128)(2,1)S(1)}, bf16[512,128]{1,0:T(8,128)(2,1)S(1)}, u32[]{:S(2)}, u32[]{:S(2)}) collective-permute-start(bf16[512,128]{1,0:T(8,128)(2,1)S(1)} %get-tuple-element.73.vp), channel_id=1, source_target_pairs={{0,2},{1,3},{2,0},{3,1},{4,6},{5,7},{6,4},{7,5},{8,10},{9,11},{10,... | collective-permute-start | bytes 393224 | tf_op jit(solution)/shard_map/ppermute | solution.py:184
  42.1 7.9 %collective-permute-start.12 = (bf16[528,128]{1,0:T(8,128)(2,1)S(1)}, bf16[528,128]{1,0:T(8,128)(2,1)S(1)}, u32[]{:S(2)}, u32[]{:S(2)}) collective-permute-start(bf16[528,128]{1,0:T(8,128)(2,1)S(1)} %get-tuple-element.72.dv0), channel_id=1, source_target_pairs={{0,2},{1,3},{2,0},{3,1},{4,6},{5,7},{6,4},{7,5},{8,10},{9,11},{10,... | collective-permute-start | bytes 405512 | tf_op jit(solution)/shard_map/ppermute | solution.py:184
  44.5 5.5 %collective-permute-start.13 = (bf16[512,128]{1,0:T(8,128)(2,1)S(1)}, bf16[512,128]{1,0:T(8,128)(2,1)S(1)}, u32[]{:S(2)}, u32[]{:S(2)}) collective-permute-start(bf16[512,128]{1,0:T(8,128)(2,1)S(1)} %get-tuple-element.76.dv1), channel_id=1, source_target_pairs={{0,2},{1,3},{2,0},{3,1},{4,6},{5,7},{6,4},{7,5},{8,10},{9,11},{10,... | collective-permute-start | bytes 393224 | tf_op jit(solution)/shard_map/ppermute | solution.py:184
  50.0 5.7 %collective-permute-start.15 = (bf16[128,3072]{1,0:T(8,128)(2,1)S(1)}, bf16[128,3072]{1,0:T(8,128)(2,1)S(1)}, u32[]{:S(2)}, u32[]{:S(2)}) collective-permute-start(bf16[128,3072]{1,0:T(8,128)(2,1)S(1)} %get-tuple-element.84), channel_id=1, source_target_pairs={{0,1},{1,0},{2,3},{3,2},{4,5},{5,4},{6,7},{7,6},{8,9},{9,8},{10,11... | collective-permute-start | bytes 2359304 | tf_op jit(solution)/shard_map/ppermute | solution.py:184
  50.1 5.6 %collective-permute-start.21 = (bf16[256,256]{1,0:T(8,128)(2,1)S(1)}, bf16[256,256]{1,0:T(8,128)(2,1)S(1)}, u32[]{:S(2)}, u32[]{:S(2)}) collective-permute-start(bf16[256,256]{1,0:T(8,128)(2,1)S(1)} %get-tuple-element.96), channel_id=1, source_target_pairs={{0,1},{1,0},{2,3},{3,2},{4,5},{5,4},{6,7},{7,6},{8,9},{9,8},{10,11... | collective-permute-start | bytes 393224 | tf_op jit(solution)/shard_map/ppermute | solution.py:184
  51.5 9.8 %collective-permute-start.16 = (bf16[640,256]{1,0:T(8,128)(2,1)S(1)}, bf16[640,256]{1,0:T(8,128)(2,1)S(1)}, u32[]{:S(2)}, u32[]{:S(2)}) collective-permute-start(bf16[640,256]{1,0:T(8,128)(2,1)S(1)} %get-tuple-element.90), channel_id=1, source_target_pairs={{0,4},{4,0},{8,12},{12,8},{16,20},{20,16},{24,28},{28,24},{1,5},{5... | collective-permute-start | bytes 983048 | tf_op jit(solution)/shard_map/ppermute | solution.py:184
  53.9 11.6 %collective-permute-start.14 = (bf16[640,256]{1,0:T(8,128)(2,1)S(1)}, bf16[640,256]{1,0:T(8,128)(2,1)S(1)}, u32[]{:S(2)}, u32[]{:S(2)}) collective-permute-start(bf16[640,256]{1,0:T(8,128)(2,1)S(1)} %get-tuple-element.79), channel_id=1, source_target_pairs={{0,8},{4,12},{8,0},{12,4},{16,24},{20,28},{24,16},{28,20},{1,9},{5... | collective-permute-start | bytes 983048 | tf_op jit(solution)/shard_map/ppermute | solution.py:184
  56.7 20.8 %collective-permute-start.24 = (bf16[128,2304]{1,0:T(8,128)(2,1)S(1)}, bf16[128,2304]{1,0:T(8,128)(2,1)S(1)}, u32[]{:S(2)}, u32[]{:S(2)}) collective-permute-start(bf16[128,2304]{1,0:T(8,128)(2,1)S(1)} %get-tuple-element.100), channel_id=1, source_target_pairs={{0,2},{1,3},{2,0},{3,1},{4,6},{5,7},{6,4},{7,5},{8,10},{9,11},{10,... | collective-permute-start | bytes 1769480 | tf_op jit(solution)/shard_map/ppermute | solution.py:184
  61.3 14.9 %collective-permute-start.17 = (bf16[320,256]{1,0:T(8,128)(2,1)S(1)}, bf16[320,256]{1,0:T(8,128)(2,1)S(1)}, u32[]{:S(2)}, u32[]{:S(2)}) collective-permute-start(bf16[320,256]{1,0:T(8,128)(2,1)S(1)} %get-tuple-element.91), channel_id=1, source_target_pairs={{0,16},{4,20},{8,24},{12,28},{16,0},{20,4},{24,8},{28,12},{1,17},{... | collective-permute-start | bytes 491528 | tf_op jit(solution)/shard_map/ppermute | solution.py:184
  64.2 12.1 %collective-permute-start.18 = (bf16[320,256]{1,0:T(8,128)(2,1)S(1)}, bf16[320,256]{1,0:T(8,128)(2,1)S(1)}, u32[]{:S(2)}, u32[]{:S(2)}) collective-permute-start(bf16[320,256]{1,0:T(8,128)(2,1)S(1)} %get-tuple-element.92), channel_id=1, source_target_pairs={{0,24},{4,28},{8,16},{12,20},{16,8},{20,12},{24,0},{28,4},{1,25},{... | collective-permute-start | bytes 491528 | tf_op jit(solution)/shard_map/ppermute | solution.py:184
  66.8 9.5 %collective-permute-start.19 = (bf16[320,256]{1,0:T(8,128)(2,1)S(1)}, bf16[320,256]{1,0:T(8,128)(2,1)S(1)}, u32[]{:S(2)}, u32[]{:S(2)}) collective-permute-start(bf16[320,256]{1,0:T(8,128)(2,1)S(1)} %get-tuple-element.94), channel_id=1, source_target_pairs={{0,4},{4,0},{8,12},{12,8},{16,20},{20,16},{24,28},{28,24},{1,5},{5... | collective-permute-start | bytes 491528 | tf_op jit(solution)/shard_map/ppermute | solution.py:184
  68.2 9.2 %collective-permute-start.23 = (bf16[128,768]{1,0:T(8,128)(2,1)S(1)}, bf16[128,768]{1,0:T(8,128)(2,1)S(1)}, u32[]{:S(2)}, u32[]{:S(2)}) collective-permute-start(bf16[128,768]{1,0:T(8,128)(2,1)S(1)} %get-tuple-element.99), channel_id=1, source_target_pairs={{0,2},{1,3},{2,0},{3,1},{4,6},{5,7},{6,4},{7,5},{8,10},{9,11},{10,... | collective-permute-start | bytes 589832 | tf_op jit(solution)/shard_map/ppermute | solution.py:184
  76.3 5.4 %collective-permute-start.20 = (bf16[320,256]{1,0:T(8,128)(2,1)S(1)}, bf16[320,256]{1,0:T(8,128)(2,1)S(1)}, u32[]{:S(2)}, u32[]{:S(2)}) collective-permute-start(bf16[320,256]{1,0:T(8,128)(2,1)S(1)} %shard_map.115.p0), channel_id=1, source_target_pairs={{0,2},{1,3},{2,0},{3,1},{4,6},{5,7},{6,4},{7,5},{8,10},{9,11},{10,... | collective-permute-start | bytes 491528 | tf_op jit(solution)/shard_map/ppermute | solution.py:184
  77.5 4.2 %collective-permute-start.25 = (bf16[320,256]{1,0:T(8,128)(2,1)S(1)}, bf16[320,256]{1,0:T(8,128)(2,1)S(1)}, u32[]{:S(2)}, u32[]{:S(2)}) collective-permute-start(bf16[320,256]{1,0:T(8,128)(2,1)S(1)} %shard_map.115.p0), channel_id=1, source_target_pairs={{0,1},{1,0},{2,3},{3,2},{4,5},{5,4},{6,7},{7,6},{8,9},{9,8},{10,11... | collective-permute-start | bytes 491528 | tf_op jit(solution)/shard_map/ppermute | solution.py:184
  81.7 1.4 %collective-permute-start.26 = (bf16[320,256]{1,0:T(8,128)(2,1)S(1)}, bf16[320,256]{1,0:T(8,128)(2,1)S(1)}, u32[]{:S(2)}, u32[]{:S(2)}) collective-permute-start(bf16[320,256]{1,0:T(8,128)(2,1)S(1)} %collective-permute-done.20.p2), channel_id=1, source_target_pairs={{0,1},{1,0},{2,3},{3,2},{4,5},{5,4},{6,7},{7,6},{8,9},{9,8},{10,11... | collective-permute-start | bytes 491528 | tf_op jit(solution)/shard_map/ppermute | solution.py:184

commit v4 on v3

--- a/solution.py
+++ b/solution.py
@@ -158,7 +158,7 @@
 WIDE = N_DP * HALF
 CORE_KV = 256
 SPARE = 16
-CUT = 768
+CUT = 1536
 CORE_Q = 1280
 KEY_AT = WIDE
 DOC_AT = KEY_AT + 512
@@ -204,38 +204,80 @@
     return lax.broadcasted_iota(jnp.int32, (ROWS, CHUNK), 1) < CHUNK // 2
 
 
-def pack_kernel(h, k, doc, w, q, g, send, keep, w0):
+def pack_kernel(h, k, doc, w, q, g, send, keep, w0, h_in, k_in, doc_in, w_in, send_out, keep_out, sems):
     s = lax.axis_index("seq")
     r = lax.axis_index("dp")
     y, c = s // 2, s % 2
     cols = pl.ds(pl.multiple_of(c * CORE_KV, CORE_KV), CORE_KV)
-    w0[0:256, :] = w[pl.ds(pl.multiple_of(y * 384, 128), 256), cols]
-    w0[256:HALF, :] = w[pl.ds(pl.multiple_of(256 + y * 64, 64), 64), cols]
+    other = pl.ds(pl.multiple_of((1 - c) * CORE_Q, CORE_Q), CORE_Q)
+
+    def copy(i, src, dst):
+        made = pltpu.make_async_copy(src, dst, sems.at[i])
+        made.start()
+        return made
+
+    w_copies = (
+        copy(0, w.at[pl.ds(pl.multiple_of(y * 384, 128), 256), cols], w_in.at[pl.ds(0, 256)]),
+        copy(1, w.at[pl.ds(pl.multiple_of(256 + y * 64, 64), 64), cols], w_in.at[pl.ds(256, 64)]),
+    )
+    blocks = [
+        copy(10 + j, h.at[:, pl.ds(pl.multiple_of((r ^ j) * SHARD, 128), SHARD)], h_in.at[:, pl.ds(j * SHARD, SHARD)])
+        for j in range(N_DP)
+    ]
+    small = copy(3, k, k_in), copy(4, doc, doc_in)
+    heads = (
+        copy(5, q.at[:, other], keep_out.at[:, pl.ds(QUERY_AT, CORE_Q)]),
+        copy(6, g.at[:, other], keep_out.at[:, pl.ds(COT_AT, CORE_Q)]),
+    )
+    for made in w_copies:
+        made.wait()
+    outs = [copy(7, w_in, w0)]
     low = first_half()
-    for out, part in ((send, 1 - y), (keep, y)):
-        for p in range(N_DP // 2):
+    for p in range(N_DP // 2):
+        blocks[2 * p].wait()
+        blocks[2 * p + 1].wait()
+        for which, (out, dst, part) in enumerate(((send_out, send, 1 - y), (keep_out, keep, y))):
             mids = []
             for i in range(2):
-                base = (r ^ (2 * p + i)) * SHARD
+                base = (2 * p + i) * SHARD
                 start = pl.multiple_of(base + part * 384, 128)
-                out[:, p * SHARD + i * 256 : p * SHARD + (i + 1) * 256] = h[:, pl.ds(start, 256)]
-                mid = h[:, pl.ds(pl.multiple_of(base + 256, 128), CHUNK)]
+                out[:, p * SHARD + i * 256 : p * SHARD + (i + 1) * 256] = h_in[:, pl.ds(start, 256)]
+                mid = h_in[:, base + 256 : base + 384]
                 mids.append(jnp.where(part == i, mid, turn(mid)))
             out[:, p * SHARD + 512 : (p + 1) * SHARD] = jnp.where(low, mids[0], mids[1])
-        out[:, KEY_AT:DOC_AT] = k[...]
-        out[:, DOC_AT:QUERY_AT] = jnp.broadcast_to(doc[...].astype(F32), (ROWS, ROWS)).astype(BF)
-    other = pl.ds(pl.multiple_of((1 - c) * CORE_Q, CORE_Q), CORE_Q)
-    keep[:, QUERY_AT:COT_AT] = q[:, other]
-    keep[:, COT_AT:PACK] = g[:, other]
+            span = pl.ds(p * SHARD, SHARD)
+            outs.append(copy(18 + 4 * which + p, out.at[:, span], dst.at[:, span]))
+    for made in small:
+        made.wait()
+    for out in (send_out, keep_out):
+        out[:, KEY_AT:DOC_AT] = k_in[...]
+        out[:, DOC_AT:QUERY_AT] = jnp.broadcast_to(doc_in[...].astype(F32), (ROWS, ROWS)).astype(BF)
+    rest = pl.ds(KEY_AT, QUERY_AT - KEY_AT)
+    outs.append(copy(8, send_out.at[:, rest], send.at[:, rest]))
+    for made in heads:
+        made.wait()
+    rest = pl.ds(KEY_AT, PACK - KEY_AT)
+    outs.append(copy(9, keep_out.at[:, rest], keep.at[:, rest]))
+    for made in outs:
+        made.wait()
 
 
 def pack(h, k, doc, w, q, g):
     return pl.pallas_call(
         pack_kernel,
         out_shape=(sds((ROWS, QUERY_AT)), sds((ROWS, PACK)), sds((HALF, CORE_KV))),
-        in_specs=[VM] * 6,
-        out_specs=(VM,) * 3,
-        compiler_params=params(60),
+        in_specs=[ANY] * 6,
+        out_specs=(ANY,) * 3,
+        scratch_shapes=[
+            pltpu.VMEM((ROWS, N_DP * SHARD), BF),
+            pltpu.VMEM((ROWS, 2 * CORE_KV), BF),
+            pltpu.VMEM((1, ROWS), jnp.int32),
+            pltpu.VMEM((HALF, CORE_KV), BF),
+            pltpu.VMEM((ROWS, QUERY_AT), BF),
+            pltpu.VMEM((ROWS, PACK), BF),
+            pltpu.SemaphoreType.DMA((26,)),
+        ],
+        compiler_params=params(62),
         cost_estimate=cost(0, 3e6),
     )(h, k, doc, w, q, g)
 
@@ -439,19 +481,18 @@
     )(*args)
 
 
-def weight_grad_pair(p, hs, gv, even, odd):
-    for (out, at), start in ((even, 0), (odd, 256)):
-        acc = jnp.zeros((256, CORE_KV), F32)
-        for t, h in enumerate(hs):
-            first = p * SHARD + start
-            acc = acc + dot_tt(h[:, first : first + 256], gv[t * ROWS : (t + 1) * ROWS, :])
-        out[at : at + 256, :] = acc.astype(BF)
+def weight_grad_pair(p, hs, gv, *outs):
     acc = jnp.zeros((CHUNK, CORE_KV), F32)
     for t, h in enumerate(hs):
         acc = acc + dot_tt(h[:, p * SHARD + 512 : (p + 1) * SHARD], gv[t * ROWS : (t + 1) * ROWS, :])
-    acc = acc.astype(BF)
-    for (out, at), half in ((even, acc[:64]), (odd, acc[64:])):
-        out[at + 256 : at + HALF, :] = half
+    middle = acc.astype(BF)
+    for which, out, at in outs:
+        acc = jnp.zeros((256, CORE_KV), F32)
+        for t, h in enumerate(hs):
+            first = p * SHARD + which * 256
+            acc = acc + dot_tt(h[:, first : first + 256], gv[t * ROWS : (t + 1) * ROWS, :])
+        out[at : at + 256, :] = acc.astype(BF)
+        out[at + 256 : at + HALF, :] = middle[which * 64 : (which + 1) * 64]
 
 
 def value_grad_kernel(dv0, dv1, rdv0, rdv1, gv, gv_keep, gv_send):
@@ -481,25 +522,25 @@
     )(*dvs, *rdvs)
 
 
-def weight_grad_far_kernel(gv, h0, h1, h2, h3, send, own):
+def weight_grad_far_kernel(which, gv, h0, h1, h2, h3, out):
     for place, p in enumerate((2, 3)):
-        weight_grad_pair(p, (h0, h1, h2, h3), gv, (own, place * HALF), (send, place * HALF))
-
-
-def weight_grad_far(gv, hs):
-    return pl.pallas_call(
-        weight_grad_far_kernel,
-        out_shape=(sds((2 * HALF, CORE_KV)),) * 2,
+        weight_grad_pair(p, (h0, h1, h2, h3), gv, (which, out, place * HALF))
+
+
+def weight_grad_far(which, gv, hs):
+    return pl.pallas_call(
+        functools.partial(weight_grad_far_kernel, which),
+        out_shape=sds((2 * HALF, CORE_KV)),
         in_specs=[VM] * 5,
-        out_specs=(VM,) * 2,
-        compiler_params=params(),
-        cost_estimate=cost(512 * WIDE * 256, 4e6),
+        out_specs=VM,
+        compiler_params=params(),
+        cost_estimate=cost(256 * WIDE * 256, 2e6),
     )(gv, *hs)
 
 
 def weight_grad_near_kernel(gv, h0, h1, h2, h3, send, own):
     for p, out in ((1, send), (0, own)):
-        weight_grad_pair(p, (h0, h1, h2, h3), gv, (out, 0), (out, HALF))
+        weight_grad_pair(p, (h0, h1, h2, h3), gv, (0, out, 0), (1, out, HALF))
 
 
 def weight_grad_near(gv, hs):
@@ -690,13 +731,14 @@
     o0, dq0, dk0, dk2, swap_out, dv1 = attention_second(e, inv, q, g, *ps, vp1, rv1, first, first_dk)
     rdv1 = swap(dv1, "seq", 2)
     gv, gv_keep, gv_send = value_grad((dv0, dv1), (rdv0, rdv1))
-    send_a, own_a = weight_grad_far(gv, ps)
-    send_b, own_b = weight_grad_near(gv, ps)
+    send_a = weight_grad_far(1, gv, ps)
     far_a = swap(send_a, "dp", 1)
-    far_b = swap(send_b, "dp", 2)
+    own_a = weight_grad_far(0, after(gv, send_a), ps)
     gvs = swap(gv_send, "seq", 1)
     swapped = swap(after(swap_out, gv), "seq", 1)
     gh0, gh_a, gh_b = hidden_grad(gv_keep, gvs, wp, wps, dk2, swapped)
+    send_b, own_b = weight_grad_near(after(gv, gh0), ps)
+    far_b = swap(send_b, "dp", 2)
     s4, s6 = add_pair(own_a, far_a)
     t6, t4 = swap(s6, "dp", 6), swap(s4, "dp", 4)
     t46 = add_two(t4, t6)

time: 84.4 us -> 83.4 us (0.988)
    pallas_call x1, Pallas kernels: 3.84 us -> 2.91 us  [pack(): pl.pallas_call(pack_kernel, out_shape=(sds((ROWS, QUERY_AT)), sds((ROWS,...]
  transfers between devices with their start and end apart: 27 -> 27, of which waited for: 11 -> 11; matrix products, arithmetic and copies ran while one was open for 0% -> 0% of each run, Pallas kernels for 14% -> 15%
where the time goes in v4:
time: 83.4 us; the launch traced here: 83.2 us
  waiting for transfers between devices  33.9 us (41%)
  starting transfers between devices  29.9 us (36%)
  Pallas kernels  16.3 us (20%)
  local copies, waits for them, and re-layouts  2.3 us (3%)
    ppermute x27, waiting for transfers between devices, swap(): return lax.ppermute(x, axis, [(i, i ^ k) for i in range(size)])  33.9 us
    ppermute x27, starting transfers between devices, swap(): return lax.ppermute(x, axis, [(i, i ^ k) for i in range(size)])  29.9 us
    pallas_call x1, Pallas kernels, pack(): pl.pallas_call(pack_kernel, out_shape=(sds((ROWS, QUERY_AT)), sds((ROWS,...  2.91 us
    unnamed x8, local copies, waits for them, and re-layouts  2.3 us
    pallas_call x1, Pallas kernels, attention_second(): pl.pallas_call(attention_second_kernel, out_shape=(sds((ROWS, CORE_Q)),)...  1.83 us
    pallas_call x1, Pallas kernels, attention_first(): pl.pallas_call(attention_first_kernel, out_shape=(sds((4 * ROWS, QUERY_PE...  1.82 us
    pallas_call x1, Pallas kernels, scores(): pl.pallas_call(scores_kernel, out_shape=(sds((10, 4 * ROWS, 2 * ROWS)), s...  1.71 us
  transfers between devices with their start and end apart: 27, of which 11 were waited for; matrix products, arithmetic and copies ran while one was open for 0% of the time, Pallas kernels for 15%

profile of v4, /device:TPU:0, one launch (start us, length us, event | category | flops | bytes accessed | tf_op | source)
XLA Modules:
  0.0 83.2 jit_solution(18323865748938766406)
XLA Ops:
  0.6 2.9 %shard_map.101 = (bf16[128,3200]{1,0:T(8,128)(2,1)}, bf16[128,5760]{1,0:T(8,128)(2,1)}, bf16[320,256]{1,0:T(8,128)(2,1)}) custom-call(bf16[128,5120]{1,0:T(8,128)(2,1)} %bitcast.15, bf16[128,512]{1,0:T(8,128)(2,1)} %bitcast.16, s32[1,128]{1,0:T(1,128)} %doc.1, bf16[640,512]{1,0:T(8,128)(2,1)} %w.1, bf16[128,2560]{1,0:T(8,128)(2,1)} %bitcast.8, ...), custom_call_target="tpu_custom_call" | custom-call | bytes 3000000 | tf_op jit(solution)/shard_map/pallas_call | solution.py:266
  4.1 2.6 %collective-permute-start.1 = (bf16[128,3200]{1,0:T(8,128)(2,1)}, bf16[128,3200]{1,0:T(8,128)(2,1)S(1)}, u32[]{:S(2)}, u32[]{:S(2)}) collective-permute-start(bf16[128,3200]{1,0:T(8,128)(2,1)} %get-tuple-element.60), channel_id=1, source_target_pairs={{0,2},{1,3},{2,0},{3,1},{4,6},{5,7},{6,4},{7,5},{8,10},{9,11},{10,... | collective-permute-start | bytes 2457608 | tf_op jit(solution)/shard_map/ppermute | solution.py:184
  6.7 3.6 %collective-permute-start.7 = (bf16[320,256]{1,0:T(8,128)(2,1)}, bf16[320,256]{1,0:T(8,128)(2,1)S(1)}, u32[]{:S(2)}, u32[]{:S(2)}) collective-permute-start(bf16[320,256]{1,0:T(8,128)(2,1)} %get-tuple-element.62.w), channel_id=1, source_target_pairs={{0,24},{4,28},{8,16},{12,20},{16,8},{20,12},{24,0},{28,4},{1,25},{... | collective-permute-start | bytes 491528 | tf_op jit(solution)/shard_map/ppermute | solution.py:184
  11.1 1.5 %collective-permute-start.2 = (bf16[320,256]{1,0:T(8,128)(2,1)}, bf16[320,256]{1,0:T(8,128)(2,1)S(1)}, u32[]{:S(2)}, u32[]{:S(2)}) collective-permute-start(bf16[320,256]{1,0:T(8,128)(2,1)} %get-tuple-element.62.w), channel_id=1, source_target_pairs={{0,4},{4,0},{8,12},{12,8},{16,20},{20,16},{24,28},{28,24},{1,5},{5... | collective-permute-start | bytes 491528 | tf_op jit(solution)/shard_map/ppermute | solution.py:184
  12.5 1.4 %copy-done = bf16[128,5760]{1,0:T(8,128)(2,1)S(1)} copy-done((bf16[128,5760]{1,0:T(8,128)(2,1)S(1)}, bf16[128,5760]{1,0:T(8,128)(2,1)}, u32[]{:S(2)}) %copy-start) | copy-done | bytes 1474584
  15.8 1.5 %collective-permute-start.8 = (bf16[320,256]{1,0:T(8,128)(2,1)S(1)}, bf16[320,256]{1,0:T(8,128)(2,1)S(1)}, u32[]{:S(2)}, u32[]{:S(2)}) collective-permute-start(bf16[320,256]{1,0:T(8,128)(2,1)S(1)} %collective-permute-done.7.w6), channel_id=1, source_target_pairs={{0,4},{4,0},{8,12},{12,8},{16,20},{20,16},{24,28},{28,24},{1,5},{5... | collective-permute-start | bytes 491528 | tf_op jit(solution)/shard_map/ppermute | solution.py:184
  17.3 7.4 %collective-permute-done.5.w4 = bf16[320,256]{1,0:T(8,128)(2,1)S(1)} collective-permute-done((bf16[320,256]{1,0:T(8,128)(2,1)}, bf16[320,256]{1,0:T(8,128)(2,1)S(1)}, u32[]{:S(2)}, u32[]{:S(2)}) %collective-permute-start.5) | collective-permute-done | bytes 163872 | tf_op jit(solution)/shard_map/ppermute | solution.py:184
  24.7 1.6 %collective-permute-start.6 = (bf16[320,256]{1,0:T(8,128)(2,1)S(1)}, bf16[320,256]{1,0:T(8,128)(2,1)S(1)}, u32[]{:S(2)}, u32[]{:S(2)}) collective-permute-start(bf16[320,256]{1,0:T(8,128)(2,1)S(1)} %collective-permute-done.5.w4), channel_id=1, source_target_pairs={{0,4},{4,0},{8,12},{12,8},{16,20},{20,16},{24,28},{28,24},{1,5},{5... | collective-permute-start | bytes 491528 | tf_op jit(solution)/shard_map/ppermute | solution.py:184
  26.3 3.9 %collective-permute-done.4.w3 = bf16[320,256]{1,0:T(8,128)(2,1)S(1)} collective-permute-done((bf16[320,256]{1,0:T(8,128)(2,1)S(1)}, bf16[320,256]{1,0:T(8,128)(2,1)S(1)}, u32[]{:S(2)}, u32[]{:S(2)}) %collective-permute-start.4) | collective-permute-done | bytes 163872 | tf_op jit(solution)/shard_map/ppermute | solution.py:184
  31.5 1.1 %collective-permute-done.9.h3.p3 = bf16[128,3200]{1,0:T(8,128)(2,1)S(1)} collective-permute-done((bf16[128,3200]{1,0:T(8,128)(2,1)S(1)}, bf16[128,3200]{1,0:T(8,128)(2,1)S(1)}, u32[]{:S(2)}, u32[]{:S(2)}) %collective-permute-start.9) | collective-permute-done | bytes 819232 | tf_op jit(solution)/shard_map/ppermute | solution.py:184
  33.5 1.5 %collective-permute-start.11 = (bf16[512,128]{1,0:T(8,128)(2,1)S(1)}, bf16[512,128]{1,0:T(8,128)(2,1)S(1)}, u32[]{:S(2)}, u32[]{:S(2)}) collective-permute-start(bf16[512,128]{1,0:T(8,128)(2,1)S(1)} %get-tuple-element.73.vp), channel_id=1, source_target_pairs={{0,2},{1,3},{2,0},{3,1},{4,6},{5,7},{6,4},{7,5},{8,10},{9,11},{10,... | collective-permute-start | bytes 393224 | tf_op jit(solution)/shard_map/ppermute | solution.py:184
  35.0 1.7 %shard_map.105 = (bf16[10,512,256]{2,1,0:T(8,128)(2,1)S(1)}, f32[80,256]{1,0:T(8,128)S(1)}) custom-call(bf16[128,2560]{1,0:T(8,128)(2,1)S(1)} %bitcast.9, bf16[128,3200]{1,0:T(8,128)(2,1)S(1)} %get-tuple-element.59.h0.p0, bf16[128,5760]{1,0:T(8,128)(2,1)S(1)} %collective-permute-done.h1.p1, bf16[128,3200]{1,0:T(8,128)(2,1)S(1)} %collective-permute-done.1.h2.p2, ...), custom_call_target="tpu_custom_call" | custom-call | flops 2684354560 | bytes 6000000 | tf_op jit(solution)/shard_map/pallas_call | solution.py:377
  36.7 2.6 %collective-permute-done.10.rv = bf16[512,128]{1,0:T(8,128)(2,1)S(1)} collective-permute-done((bf16[512,128]{1,0:T(8,128)(2,1)S(1)}, bf16[512,128]{1,0:T(8,128)(2,1)S(1)}, u32[]{:S(2)}, u32[]{:S(2)}) %collective-permute-start.10) | collective-permute-done | bytes 131104 | tf_op jit(solution)/shard_map/ppermute | solution.py:184
  39.3 1.8 %shard_map.106 = (bf16[512,640]{1,0:T(8,128)(2,1)S(1)}, bf16[512,128]{1,0:T(8,128)(2,1)S(1)}, bf16[528,128]{1,0:T(8,128)(2,1)S(1)}) custom-call(bf16[10,512,256]{2,1,0:T(8,128)(2,1)S(1)} %get-tuple-element.70.e_ref, f32[80,256]{1,0:T(8,128)S(1)} %get-tuple-element.71.inv_ref, bf16[128,2560]{1,0:T(8,128)(2,1)S(1)} %bitcast.10, ...), custom_call_target="tpu_custom_call" | custom-call | flops 3355443200 | bytes 3000000 | tf_op jit(solution)/shard_map/pallas_call | solution.py:458
  41.7 1.8 %shard_map.107 = (bf16[128,1280]{1,0:T(8,128)(2,1)S(1)}, bf16[128,1280]{1,0:T(8,128)(2,1)S(1)}, bf16[128,256]{1,0:T(8,128)(2,1)S(1)}, bf16[128,256]{1,0:T(8,128)...) custom-call(bf16[10,512,256]{2,1,0:T(8,128)(2,1)S(1)} %get-tuple-element.70.e_ref, ...), custom_call_target="tpu_custom_call" | custom-call | flops 3355443200 | bytes 3000000 | tf_op jit(solution)/shard_map/pallas_call | solution.py:472
  43.5 1.6 %collective-permute-start.13 = (bf16[512,128]{1,0:T(8,128)(2,1)S(1)}, bf16[512,128]{1,0:T(8,128)(2,1)S(1)}, u32[]{:S(2)}, u32[]{:S(2)}) collective-permute-start(bf16[512,128]{1,0:T(8,128)(2,1)S(1)} %get-tuple-element.76.dv1), channel_id=1, source_target_pairs={{0,2},{1,3},{2,0},{3,1},{4,6},{5,7},{6,4},{7,5},{8,10},{9,11},{10,... | collective-permute-start | bytes 393224 | tf_op jit(solution)/shard_map/ppermute | solution.py:184
  45.1 3.9 %collective-permute-done.13.rdv1 = bf16[512,128]{1,0:T(8,128)(2,1)S(1)} collective-permute-done((bf16[512,128]{1,0:T(8,128)(2,1)S(1)}, bf16[512,128]{1,0:T(8,128)(2,1)S(1)}, u32[]{:S(2)}, u32[]{:S(2)}) %collective-permute-start.13) | collective-permute-done | bytes 131104 | tf_op jit(solution)/shard_map/ppermute | solution.py:184
  50.3 1.6 %collective-permute-start.18 = (bf16[640,256]{1,0:T(8,128)(2,1)S(1)}, bf16[640,256]{1,0:T(8,128)(2,1)S(1)}, u32[]{:S(2)}, u32[]{:S(2)}) collective-permute-start(bf16[640,256]{1,0:T(8,128)(2,1)S(1)} %shard_map.113), channel_id=1, source_target_pairs={{0,4},{4,0},{8,12},{12,8},{16,20},{20,16},{24,28},{28,24},{1,5},{5... | collective-permute-start | bytes 983048 | tf_op jit(solution)/shard_map/ppermute | solution.py:184
  53.6 1.9 %collective-permute-start.17 = (bf16[640,256]{1,0:T(8,128)(2,1)S(1)}, bf16[640,256]{1,0:T(8,128)(2,1)S(1)}, u32[]{:S(2)}, u32[]{:S(2)}) collective-permute-start(bf16[640,256]{1,0:T(8,128)(2,1)S(1)} %get-tuple-element.86), channel_id=1, source_target_pairs={{0,8},{4,12},{8,0},{12,4},{16,24},{20,28},{24,16},{28,20},{1,9},{5... | collective-permute-start | bytes 983048 | tf_op jit(solution)/shard_map/ppermute | solution.py:184
  55.5 1.1 %collective-permute-start.23 = (bf16[128,1536]{1,0:T(8,128)(2,1)S(1)}, bf16[128,1536]{1,0:T(8,128)(2,1)S(1)}, u32[]{:S(2)}, u32[]{:S(2)}) collective-permute-start(bf16[128,1536]{1,0:T(8,128)(2,1)S(1)} %get-tuple-element.99), channel_id=1, source_target_pairs={{0,2},{1,3},{2,0},{3,1},{4,6},{5,7},{6,4},{7,5},{8,10},{9,11},{10,... | collective-permute-start | bytes 1179656 | tf_op jit(solution)/shard_map/ppermute | solution.py:184
  56.6 0.9 %collective-permute-start.24 = (bf16[128,1536]{1,0:T(8,128)(2,1)S(1)}, bf16[128,1536]{1,0:T(8,128)(2,1)S(1)}, u32[]{:S(2)}, u32[]{:S(2)}) collective-permute-start(bf16[128,1536]{1,0:T(8,128)(2,1)S(1)} %get-tuple-element.100), channel_id=1, source_target_pairs={{0,2},{1,3},{2,0},{3,1},{4,6},{5,7},{6,4},{7,5},{8,10},{9,11},{10,... | collective-permute-start | bytes 1179656 | tf_op jit(solution)/shard_map/ppermute | solution.py:184
  58.2 1.9 %collective-permute-done.18.b = bf16[640,256]{1,0:T(8,128)(2,1)S(1)} collective-permute-done((bf16[640,256]{1,0:T(8,128)(2,1)S(1)}, bf16[640,256]{1,0:T(8,128)(2,1)S(1)}, u32[]{:S(2)}, u32[]{:S(2)}) %collective-permute-start.18) | collective-permute-done | bytes 327712 | tf_op jit(solution)/shard_map/ppermute | solution.py:184
  60.1 2.9 %collective-permute-start.19 = (bf16[320,256]{1,0:T(8,128)(2,1)S(1)}, bf16[320,256]{1,0:T(8,128)(2,1)S(1)}, u32[]{:S(2)}, u32[]{:S(2)}) collective-permute-start(bf16[320,256]{1,0:T(8,128)(2,1)S(1)} %get-tuple-element.95), channel_id=1, source_target_pairs={{0,16},{4,20},{8,24},{12,28},{16,0},{20,4},{24,8},{28,12},{1,17},{... | collective-permute-start | bytes 491528 | tf_op jit(solution)/shard_map/ppermute | solution.py:184
  63.0 1.3 %collective-permute-start.20 = (bf16[320,256]{1,0:T(8,128)(2,1)S(1)}, bf16[320,256]{1,0:T(8,128)(2,1)S(1)}, u32[]{:S(2)}, u32[]{:S(2)}) collective-permute-start(bf16[320,256]{1,0:T(8,128)(2,1)S(1)} %get-tuple-element.96), channel_id=1, source_target_pairs={{0,24},{4,28},{8,16},{12,20},{16,8},{20,12},{24,0},{28,4},{1,25},{... | collective-permute-start | bytes 491528 | tf_op jit(solution)/shard_map/ppermute | solution.py:184
  64.4 1.2 %shard_map.112 = (bf16[128,2560]{1,0:T(8,128)(2,1)}, bf16[128,2560]{1,0:T(8,128)(2,1)}) custom-call(bf16[128,1280]{1,0:T(8,128)(2,1)S(1)} %get-tuple-element.88.o0, bf16[128,1280]{1,0:T(8,128)(2,1)S(1)} %get-tuple-element.89.dq0, bf16[128,3072]{1,0:T(8,128)(2,1)S(1)} %collective-permute-done.16.swapped), custom_call_target="tpu_custom_call" | custom-call | bytes 4000000 | tf_op jit(solution)/shard_map/pallas_call | solution.py:634
  65.6 1.6 %collective-permute-start.21 = (bf16[320,256]{1,0:T(8,128)(2,1)S(1)}, bf16[320,256]{1,0:T(8,128)(2,1)S(1)}, u32[]{:S(2)}, u32[]{:S(2)}) collective-permute-start(bf16[320,256]{1,0:T(8,128)(2,1)S(1)} %get-tuple-element.98), channel_id=1, source_target_pairs={{0,4},{4,0},{8,12},{12,8},{16,20},{20,16},{24,28},{28,24},{1,5},{5... | collective-permute-start | bytes 491528 | tf_op jit(solution)/shard_map/ppermute | solution.py:184
  67.2 8.0 %collective-permute-done.19.a = bf16[320,256]{1,0:T(8,128)(2,1)S(1)} collective-permute-done((bf16[320,256]{1,0:T(8,128)(2,1)S(1)}, bf16[320,256]{1,0:T(8,128)(2,1)S(1)}, u32[]{:S(2)}, u32[]{:S(2)}) %collective-permute-start.19) | collective-permute-done | bytes 163872 | tf_op jit(solution)/shard_map/ppermute | solution.py:184
  75.3 1.1 %collective-permute-start.22 = (bf16[320,256]{1,0:T(8,128)(2,1)S(1)}, bf16[320,256]{1,0:T(8,128)(2,1)S(1)}, u32[]{:S(2)}, u32[]{:S(2)}) collective-permute-start(bf16[320,256]{1,0:T(8,128)(2,1)S(1)} %shard_map.117.p0), channel_id=1, source_target_pairs={{0,2},{1,3},{2,0},{3,1},{4,6},{5,7},{6,4},{7,5},{8,10},{9,11},{10,... | collective-permute-start | bytes 491528 | tf_op jit(solution)/shard_map/ppermute | solution.py:184
  76.4 1.4 %shard_map.118 = (bf16[128,5120]{1,0:T(8,128)(2,1)}, bf16[128,512]{1,0:T(8,128)(2,1)}) custom-call(bf16[128,2560]{1,0:T(8,128)(2,1)S(1)} %get-tuple-element.83.own_ref, bf16[128,1536]{1,0:T(8,128)(2,1)S(1)} %collective-permute-done.23.far_a, bf16[128,1536]{1,0:T(8,128)(2,1)S(1)} %collective-permute-done.24.far_b, ...), custom_call_target="tpu_custom_call" | custom-call | bytes 3000000 | tf_op jit(solution)/shard_map/pallas_call | solution.py:612
  77.8 2.8 %collective-permute-done.22.p2 = bf16[320,256]{1,0:T(8,128)(2,1)S(1)} collective-permute-done((bf16[320,256]{1,0:T(8,128)(2,1)S(1)}, bf16[320,256]{1,0:T(8,128)(2,1)S(1)}, u32[]{:S(2)}, u32[]{:S(2)}) %collective-permute-start.22) | collective-permute-done | bytes 163872 | tf_op jit(solution)/shard_map/ppermute | solution.py:184
  80.7 1.4 %collective-permute-done.26.p3 = bf16[320,256]{1,0:T(8,128)(2,1)S(1)} collective-permute-done((bf16[320,256]{1,0:T(8,128)(2,1)S(1)}, bf16[320,256]{1,0:T(8,128)(2,1)S(1)}, u32[]{:S(2)}, u32[]{:S(2)}) %collective-permute-start.26) | collective-permute-done | bytes 163872 | tf_op jit(solution)/shard_map/ppermute | solution.py:184
  82.0 1.2 %shard_map.119 = f32[640,512]{1,0:T(8,128)} custom-call(bf16[320,256]{1,0:T(8,128)(2,1)S(1)} %shard_map.117.p0, bf16[320,256]{1,0:T(8,128)(2,1)S(1)} %collective-permute-done.25.p1, bf16[320,256]{1,0:T(8,128)(2,1)S(1)} %collective-permute-done.22.p2, bf16[320,256]{1,0:T(8,128)(2,1)S(1)} %collective-permute-done.26.p3), custom_call_target="tpu_custom_call" | custom-call | bytes 2000000 | tf_op jit(solution)/shard_map/pallas_call | solution.py:701
  (49 shorter events, 9.9 us)
Async XLA Ops:
  3.5 6.7 %collective-permute-start = (bf16[128,5760]{1,0:T(8,128)(2,1)}, bf16[128,5760]{1,0:T(8,128)(2,1)S(1)}, u32[]{:S(2)}, u32[]{:S(2)}) collective-permute-start(bf16[128,5760]{1,0:T(8,128)(2,1)} %get-tuple-element.57.p), channel_id=1, source_target_pairs={{0,1},{1,0},{2,3},{3,2},{4,5},{5,4},{6,7},{7,6},{8,9},{9,8},{10,11... | collective-permute-start | bytes 4423688 | tf_op jit(solution)/shard_map/ppermute | solution.py:184
  4.1 22.2 %collective-permute-start.1 = (bf16[128,3200]{1,0:T(8,128)(2,1)}, bf16[128,3200]{1,0:T(8,128)(2,1)S(1)}, u32[]{:S(2)}, u32[]{:S(2)}) collective-permute-start(bf16[128,3200]{1,0:T(8,128)(2,1)} %get-tuple-element.60), channel_id=1, source_target_pairs={{0,2},{1,3},{2,0},{3,1},{4,6},{5,7},{6,4},{7,5},{8,10},{9,11},{10,... | collective-permute-start | bytes 2457608 | tf_op jit(solution)/shard_map/ppermute | solution.py:184
  6.7 9.1 %collective-permute-start.7 = (bf16[320,256]{1,0:T(8,128)(2,1)}, bf16[320,256]{1,0:T(8,128)(2,1)S(1)}, u32[]{:S(2)}, u32[]{:S(2)}) collective-permute-start(bf16[320,256]{1,0:T(8,128)(2,1)} %get-tuple-element.62.w), channel_id=1, source_target_pairs={{0,24},{4,28},{8,16},{12,20},{16,8},{20,12},{24,0},{28,4},{1,25},{... | collective-permute-start | bytes 491528 | tf_op jit(solution)/shard_map/ppermute | solution.py:184
  10.3 14.4 %collective-permute-start.5 = (bf16[320,256]{1,0:T(8,128)(2,1)}, bf16[320,256]{1,0:T(8,128)(2,1)S(1)}, u32[]{:S(2)}, u32[]{:S(2)}) collective-permute-start(bf16[320,256]{1,0:T(8,128)(2,1)} %get-tuple-element.62.w), channel_id=1, source_target_pairs={{0,16},{4,20},{8,24},{12,28},{16,0},{20,4},{24,8},{28,12},{1,17},{... | collective-permute-start | bytes 491528 | tf_op jit(solution)/shard_map/ppermute | solution.py:184
  10.3 14.4 %collective-permute-start.3 = (bf16[320,256]{1,0:T(8,128)(2,1)}, bf16[320,256]{1,0:T(8,128)(2,1)S(1)}, u32[]{:S(2)}, u32[]{:S(2)}) collective-permute-start(bf16[320,256]{1,0:T(8,128)(2,1)} %get-tuple-element.62.w), channel_id=1, source_target_pairs={{0,8},{4,12},{8,0},{12,4},{16,24},{20,28},{24,16},{28,20},{1,9},{5... | collective-permute-start | bytes 491528 | tf_op jit(solution)/shard_map/ppermute | solution.py:184
  11.1 13.6 %collective-permute-start.2 = (bf16[320,256]{1,0:T(8,128)(2,1)}, bf16[320,256]{1,0:T(8,128)(2,1)S(1)}, u32[]{:S(2)}, u32[]{:S(2)}) collective-permute-start(bf16[320,256]{1,0:T(8,128)(2,1)} %get-tuple-element.62.w), channel_id=1, source_target_pairs={{0,4},{4,0},{8,12},{12,8},{16,20},{20,16},{24,28},{28,24},{1,5},{5... | collective-permute-start | bytes 491528 | tf_op jit(solution)/shard_map/ppermute | solution.py:184
  12.5 1.4 %copy-start = (bf16[128,5760]{1,0:T(8,128)(2,1)S(1)}, bf16[128,5760]{1,0:T(8,128)(2,1)}, u32[]{:S(2)}) copy-start(bf16[128,5760]{1,0:T(8,128)(2,1)} %get-tuple-element.57.p) | copy-start | bytes 4423684
  13.9 0.9 %copy-start.3 = (bf16[320,256]{1,0:T(8,128)(2,1)S(1)}, bf16[320,256]{1,0:T(8,128)(2,1)}, u32[]{:S(2)}) copy-start(bf16[320,256]{1,0:T(8,128)(2,1)} %get-tuple-element.62.w) | copy-start | bytes 491524
  15.8 10.5 %collective-permute-start.8 = (bf16[320,256]{1,0:T(8,128)(2,1)S(1)}, bf16[320,256]{1,0:T(8,128)(2,1)S(1)}, u32[]{:S(2)}, u32[]{:S(2)}) collective-permute-start(bf16[320,256]{1,0:T(8,128)(2,1)S(1)} %collective-permute-done.7.w6), channel_id=1, source_target_pairs={{0,4},{4,0},{8,12},{12,8},{16,20},{20,16},{24,28},{28,24},{1,5},{5... | collective-permute-start | bytes 491528 | tf_op jit(solution)/shard_map/ppermute | solution.py:184
  24.7 5.4 %collective-permute-start.4 = (bf16[320,256]{1,0:T(8,128)(2,1)S(1)}, bf16[320,256]{1,0:T(8,128)(2,1)S(1)}, u32[]{:S(2)}, u32[]{:S(2)}) collective-permute-start(bf16[320,256]{1,0:T(8,128)(2,1)S(1)} %collective-permute-done.2.w1), channel_id=1, source_target_pairs={{0,8},{4,12},{8,0},{12,4},{16,24},{20,28},{24,16},{28,20},{1,9},{5... | collective-permute-start | bytes 491528 | tf_op jit(solution)/shard_map/ppermute | solution.py:184
  24.7 5.5 %collective-permute-start.6 = (bf16[320,256]{1,0:T(8,128)(2,1)S(1)}, bf16[320,256]{1,0:T(8,128)(2,1)S(1)}, u32[]{:S(2)}, u32[]{:S(2)}) collective-permute-start(bf16[320,256]{1,0:T(8,128)(2,1)S(1)} %collective-permute-done.5.w4), channel_id=1, source_target_pairs={{0,4},{4,0},{8,12},{12,8},{16,20},{20,16},{24,28},{28,24},{1,5},{5... | collective-permute-start | bytes 491528 | tf_op jit(solution)/shard_map/ppermute | solution.py:184
  30.2 2.3 %collective-permute-start.9 = (bf16[128,3200]{1,0:T(8,128)(2,1)S(1)}, bf16[128,3200]{1,0:T(8,128)(2,1)S(1)}, u32[]{:S(2)}, u32[]{:S(2)}) collective-permute-start(bf16[128,3200]{1,0:T(8,128)(2,1)S(1)} %collective-permute-done.1.h2.p2), channel_id=1, source_target_pairs={{0,1},{1,0},{2,3},{3,2},{4,5},{5,4},{6,7},{7,6},{8,9},{9,8},{10,11... | collective-permute-start | bytes 2457608 | tf_op jit(solution)/shard_map/ppermute | solution.py:184
  30.9 4.1 %copy-start.1 = (bf16[1,128,2560]{2,1,0:T(8,128)(2,1)S(1)}, bf16[1,128,2560]{2,1,0:T(8,128)(2,1)}, u32[]{:S(2)}) copy-start(bf16[1,128,2560]{2,1,0:T(8,128)(2,1)} %param.7) | copy-start | bytes 1966084
  30.9 20.9 %collective-permute-start.15 = (bf16[2560,256]{1,0:T(8,128)(2,1)S(1)}, bf16[2560,256]{1,0:T(8,128)(2,1)S(1)}, u32[]{:S(2)}, u32[]{:S(2)}) collective-permute-start(bf16[2560,256]{1,0:T(8,128)(2,1)S(1)} %get-tuple-element.67.wp), channel_id=1, source_target_pairs={{0,1},{1,0},{2,3},{3,2},{4,5},{5,4},{6,7},{7,6},{8,9},{9,8},{10,11... | collective-permute-start | bytes 3932168 | tf_op jit(solution)/shard_map/ppermute | solution.py:184
  32.9 6.4 %collective-permute-start.10 = (bf16[512,128]{1,0:T(8,128)(2,1)S(1)}, bf16[512,128]{1,0:T(8,128)(2,1)S(1)}, u32[]{:S(2)}, u32[]{:S(2)}) collective-permute-start(bf16[512,128]{1,0:T(8,128)(2,1)S(1)} %get-tuple-element.68.vp), channel_id=1, source_target_pairs={{0,2},{1,3},{2,0},{3,1},{4,6},{5,7},{6,4},{7,5},{8,10},{9,11},{10,... | collective-permute-start | bytes 393224 | tf_op jit(solution)/shard_map/ppermute | solution.py:184
  33.5 5.9 %copy-start.2 = (bf16[1,128,2560]{2,1,0:T(8,128)(2,1)S(1)}, bf16[1,128,2560]{2,1,0:T(8,128)(2,1)}, u32[]{:S(2)}) copy-start(bf16[1,128,2560]{2,1,0:T(8,128)(2,1)} %param.11) | copy-start | bytes 1966084
  33.5 8.2 %collective-permute-start.11 = (bf16[512,128]{1,0:T(8,128)(2,1)S(1)}, bf16[512,128]{1,0:T(8,128)(2,1)S(1)}, u32[]{:S(2)}, u32[]{:S(2)}) collective-permute-start(bf16[512,128]{1,0:T(8,128)(2,1)S(1)} %get-tuple-element.73.vp), channel_id=1, source_target_pairs={{0,2},{1,3},{2,0},{3,1},{4,6},{5,7},{6,4},{7,5},{8,10},{9,11},{10,... | collective-permute-start | bytes 393224 | tf_op jit(solution)/shard_map/ppermute | solution.py:184
  41.1 7.9 %collective-permute-start.12 = (bf16[528,128]{1,0:T(8,128)(2,1)S(1)}, bf16[528,128]{1,0:T(8,128)(2,1)S(1)}, u32[]{:S(2)}, u32[]{:S(2)}) collective-permute-start(bf16[528,128]{1,0:T(8,128)(2,1)S(1)} %get-tuple-element.72.dv0), channel_id=1, source_target_pairs={{0,2},{1,3},{2,0},{3,1},{4,6},{5,7},{6,4},{7,5},{8,10},{9,11},{10,... | collective-permute-start | bytes 405512 | tf_op jit(solution)/shard_map/ppermute | solution.py:184
  43.5 5.5 %collective-permute-start.13 = (bf16[512,128]{1,0:T(8,128)(2,1)S(1)}, bf16[512,128]{1,0:T(8,128)(2,1)S(1)}, u32[]{:S(2)}, u32[]{:S(2)}) collective-permute-start(bf16[512,128]{1,0:T(8,128)(2,1)S(1)} %get-tuple-element.76.dv1), channel_id=1, source_target_pairs={{0,2},{1,3},{2,0},{3,1},{4,6},{5,7},{6,4},{7,5},{8,10},{9,11},{10,... | collective-permute-start | bytes 393224 | tf_op jit(solution)/shard_map/ppermute | solution.py:184
  49.1 2.8 %collective-permute-start.16 = (bf16[128,3072]{1,0:T(8,128)(2,1)S(1)}, bf16[128,3072]{1,0:T(8,128)(2,1)S(1)}, u32[]{:S(2)}, u32[]{:S(2)}) collective-permute-start(bf16[128,3072]{1,0:T(8,128)(2,1)S(1)} %get-tuple-element.82), channel_id=1, source_target_pairs={{0,1},{1,0},{2,3},{3,2},{4,5},{5,4},{6,7},{7,6},{8,9},{9,8},{10,11... | collective-permute-start | bytes 2359304 | tf_op jit(solution)/shard_map/ppermute | solution.py:184
  49.2 2.7 %collective-permute-start.14 = (bf16[256,256]{1,0:T(8,128)(2,1)S(1)}, bf16[256,256]{1,0:T(8,128)(2,1)S(1)}, u32[]{:S(2)}, u32[]{:S(2)}) collective-permute-start(bf16[256,256]{1,0:T(8,128)(2,1)S(1)} %get-tuple-element.79), channel_id=1, source_target_pairs={{0,1},{1,0},{2,3},{3,2},{4,5},{5,4},{6,7},{7,6},{8,9},{9,8},{10,11... | collective-permute-start | bytes 393224 | tf_op jit(solution)/shard_map/ppermute | solution.py:184
  50.3 9.8 %collective-permute-start.18 = (bf16[640,256]{1,0:T(8,128)(2,1)S(1)}, bf16[640,256]{1,0:T(8,128)(2,1)S(1)}, u32[]{:S(2)}, u32[]{:S(2)}) collective-permute-start(bf16[640,256]{1,0:T(8,128)(2,1)S(1)} %shard_map.113), channel_id=1, source_target_pairs={{0,4},{4,0},{8,12},{12,8},{16,20},{20,16},{24,28},{28,24},{1,5},{5... | collective-permute-start | bytes 983048 | tf_op jit(solution)/shard_map/ppermute | solution.py:184
  53.6 11.9 %collective-permute-start.17 = (bf16[640,256]{1,0:T(8,128)(2,1)S(1)}, bf16[640,256]{1,0:T(8,128)(2,1)S(1)}, u32[]{:S(2)}, u32[]{:S(2)}) collective-permute-start(bf16[640,256]{1,0:T(8,128)(2,1)S(1)} %get-tuple-element.86), channel_id=1, source_target_pairs={{0,8},{4,12},{8,0},{12,4},{16,24},{20,28},{24,16},{28,20},{1,9},{5... | collective-permute-start | bytes 983048 | tf_op jit(solution)/shard_map/ppermute | solution.py:184
  55.5 20.9 %collective-permute-start.23 = (bf16[128,1536]{1,0:T(8,128)(2,1)S(1)}, bf16[128,1536]{1,0:T(8,128)(2,1)S(1)}, u32[]{:S(2)}, u32[]{:S(2)}) collective-permute-start(bf16[128,1536]{1,0:T(8,128)(2,1)S(1)} %get-tuple-element.99), channel_id=1, source_target_pairs={{0,2},{1,3},{2,0},{3,1},{4,6},{5,7},{6,4},{7,5},{8,10},{9,11},{10,... | collective-permute-start | bytes 1179656 | tf_op jit(solution)/shard_map/ppermute | solution.py:184
  56.6 19.8 %collective-permute-start.24 = (bf16[128,1536]{1,0:T(8,128)(2,1)S(1)}, bf16[128,1536]{1,0:T(8,128)(2,1)S(1)}, u32[]{:S(2)}, u32[]{:S(2)}) collective-permute-start(bf16[128,1536]{1,0:T(8,128)(2,1)S(1)} %get-tuple-element.100), channel_id=1, source_target_pairs={{0,2},{1,3},{2,0},{3,1},{4,6},{5,7},{6,4},{7,5},{8,10},{9,11},{10,... | collective-permute-start | bytes 1179656 | tf_op jit(solution)/shard_map/ppermute | solution.py:184
  60.1 15.0 %collective-permute-start.19 = (bf16[320,256]{1,0:T(8,128)(2,1)S(1)}, bf16[320,256]{1,0:T(8,128)(2,1)S(1)}, u32[]{:S(2)}, u32[]{:S(2)}) collective-permute-start(bf16[320,256]{1,0:T(8,128)(2,1)S(1)} %get-tuple-element.95), channel_id=1, source_target_pairs={{0,16},{4,20},{8,24},{12,28},{16,0},{20,4},{24,8},{28,12},{1,17},{... | collective-permute-start | bytes 491528 | tf_op jit(solution)/shard_map/ppermute | solution.py:184
  63.0 12.1 %collective-permute-start.20 = (bf16[320,256]{1,0:T(8,128)(2,1)S(1)}, bf16[320,256]{1,0:T(8,128)(2,1)S(1)}, u32[]{:S(2)}, u32[]{:S(2)}) collective-permute-start(bf16[320,256]{1,0:T(8,128)(2,1)S(1)} %get-tuple-element.96), channel_id=1, source_target_pairs={{0,24},{4,28},{8,16},{12,20},{16,8},{20,12},{24,0},{28,4},{1,25},{... | collective-permute-start | bytes 491528 | tf_op jit(solution)/shard_map/ppermute | solution.py:184
  65.6 9.6 %collective-permute-start.21 = (bf16[320,256]{1,0:T(8,128)(2,1)S(1)}, bf16[320,256]{1,0:T(8,128)(2,1)S(1)}, u32[]{:S(2)}, u32[]{:S(2)}) collective-permute-start(bf16[320,256]{1,0:T(8,128)(2,1)S(1)} %get-tuple-element.98), channel_id=1, source_target_pairs={{0,4},{4,0},{8,12},{12,8},{16,20},{20,16},{24,28},{28,24},{1,5},{5... | collective-permute-start | bytes 491528 | tf_op jit(solution)/shard_map/ppermute | solution.py:184
  75.3 5.4 %collective-permute-start.22 = (bf16[320,256]{1,0:T(8,128)(2,1)S(1)}, bf16[320,256]{1,0:T(8,128)(2,1)S(1)}, u32[]{:S(2)}, u32[]{:S(2)}) collective-permute-start(bf16[320,256]{1,0:T(8,128)(2,1)S(1)} %shard_map.117.p0), channel_id=1, source_target_pairs={{0,2},{1,3},{2,0},{3,1},{4,6},{5,7},{6,4},{7,5},{8,10},{9,11},{10,... | collective-permute-start | bytes 491528 | tf_op jit(solution)/shard_map/ppermute | solution.py:184
  77.8 2.9 %collective-permute-start.25 = (bf16[320,256]{1,0:T(8,128)(2,1)S(1)}, bf16[320,256]{1,0:T(8,128)(2,1)S(1)}, u32[]{:S(2)}, u32[]{:S(2)}) collective-permute-start(bf16[320,256]{1,0:T(8,128)(2,1)S(1)} %shard_map.117.p0), channel_id=1, source_target_pairs={{0,1},{1,0},{2,3},{3,2},{4,5},{5,4},{6,7},{7,6},{8,9},{9,8},{10,11... | collective-permute-start | bytes 491528 | tf_op jit(solution)/shard_map/ppermute | solution.py:184
  80.7 1.4 %collective-permute-start.26 = (bf16[320,256]{1,0:T(8,128)(2,1)S(1)}, bf16[320,256]{1,0:T(8,128)(2,1)S(1)}, u32[]{:S(2)}, u32[]{:S(2)}) collective-permute-start(bf16[320,256]{1,0:T(8,128)(2,1)S(1)} %collective-permute-done.22.p2), channel_id=1, source_target_pairs={{0,1},{1,0},{2,3},{3,2},{4,5},{5,4},{6,7},{7,6},{8,9},{9,8},{10,11... | collective-permute-start | bytes 491528 | tf_op jit(solution)/shard_map/ppermute | solution.py:184

commit v5 on v4

--- a/solution.py
+++ b/solution.py
@@ -158,7 +158,6 @@
 WIDE = N_DP * HALF
 CORE_KV = 256
 SPARE = 16
-CUT = 1536
 CORE_Q = 1280
 KEY_AT = WIDE
 DOC_AT = KEY_AT + 512
@@ -522,17 +521,34 @@
     )(*dvs, *rdvs)
 
 
-def weight_grad_far_kernel(which, gv, h0, h1, h2, h3, out):
-    for place, p in enumerate((2, 3)):
-        weight_grad_pair(p, (h0, h1, h2, h3), gv, (which, out, place * HALF))
-
-
-def weight_grad_far(which, gv, hs):
-    return pl.pallas_call(
-        functools.partial(weight_grad_far_kernel, which),
-        out_shape=sds((2 * HALF, CORE_KV)),
+def weight_grad_sent_kernel(gv, h0, h1, h2, h3, first, second):
+    weight_grad_pair(2, (h0, h1, h2, h3), gv, (1, first, 0))
+    first[HALF:, :] = jnp.zeros((SPARE, CORE_KV), BF)
+    weight_grad_pair(3, (h0, h1, h2, h3), gv, (1, second, 0))
+
+
+def weight_grad_sent(gv, hs):
+    return pl.pallas_call(
+        weight_grad_sent_kernel,
+        out_shape=(sds((HALF + SPARE, CORE_KV)), sds((HALF, CORE_KV))),
         in_specs=[VM] * 5,
-        out_specs=VM,
+        out_specs=(VM,) * 2,
+        compiler_params=params(),
+        cost_estimate=cost(256 * WIDE * 256, 2e6),
+    )(gv, *hs)
+
+
+def weight_grad_kept_kernel(gv, h0, h1, h2, h3, first, second):
+    weight_grad_pair(2, (h0, h1, h2, h3), gv, (0, first, 0))
+    weight_grad_pair(3, (h0, h1, h2, h3), gv, (0, second, 0))
+
+
+def weight_grad_kept(gv, hs):
+    return pl.pallas_call(
+        weight_grad_kept_kernel,
+        out_shape=(sds((HALF, CORE_KV)),) * 2,
+        in_specs=[VM] * 5,
+        out_specs=(VM,) * 2,
         compiler_params=params(),
         cost_estimate=cost(256 * WIDE * 256, 2e6),
     )(gv, *hs)
@@ -554,15 +570,14 @@
     )(gv, *hs)
 
 
-def hidden_grad_kernel(gv, gvs, wp, wps, dk2, swapped, gh0, send_a, send_b):
+def hidden_grad_kernel(gv, gvs, wp, wps, dk2, swapped, gh0, send_b):
     full = dot_nt(gv[...], wp[...]) + dot_nt(gvs[...], wps[...])
     full = full.astype(BF)
     gh0[...] = full[:ROWS]
     far = full[ROWS:]
-    send_a[...] = far[:, : CUT]
-    send_b[:, : WIDE - CUT] = far[:, CUT :]
+    send_b[:, :WIDE] = far
     c = lax.axis_index("seq") % 2
-    at = WIDE - CUT
+    at = WIDE
     send_b[:, pl.ds(pl.multiple_of(at + c * CORE_KV, CORE_KV), CORE_KV)] = dk2[...]
     send_b[:, pl.ds(pl.multiple_of(at + (1 - c) * CORE_KV, CORE_KV), CORE_KV)] = swapped[
         :, 2 * CORE_Q + CORE_KV :
@@ -572,17 +587,15 @@
 def hidden_grad(gv, gvs, wp, wps, dk2, swapped):
     return pl.pallas_call(
         hidden_grad_kernel,
-        out_shape=(sds((ROWS, WIDE)), sds((ROWS, CUT)), sds((ROWS, WIDE - CUT + 2 * CORE_KV))),
+        out_shape=(sds((ROWS, WIDE)), sds((ROWS, WIDE + 2 * CORE_KV))),
         in_specs=[VM] * 6,
-        out_specs=(VM,) * 3,
+        out_specs=(VM,) * 2,
         compiler_params=params(),
         cost_estimate=cost(2 * 256 * WIDE * 512, 6e6),
     )(gv, gvs, wp, wps, dk2, swapped)
 
 
-def hidden_join_kernel(own_ref, far_a, far_b, dk0, swapped, o_ref, dk_ref, far_ref):
-    far_ref[:, 0:CUT] = far_a[...]
-    far_ref[:, CUT:] = far_b[:, : WIDE - CUT]
+def hidden_join_kernel(own_ref, far_ref, dk0, swapped, o_ref, dk_ref):
     s = lax.axis_index("seq")
     y, c = s // 2, s % 2
     r = lax.axis_index("dp")
@@ -602,22 +615,21 @@
         o_ref[:, pl.ds(at0, CHUNK)] = jnp.where(low, part0, turn(part1))
         o_ref[:, pl.ds(at1, CHUNK)] = jnp.where(low, turn(part0), part1)
     for place, near in ((c, dk0[...]), (1 - c, swapped[:, 2 * CORE_Q : 2 * CORE_Q + CORE_KV])):
-        far = far_b[:, pl.ds(pl.multiple_of(WIDE - CUT + place * CORE_KV, CORE_KV), CORE_KV)]
+        far = far_ref[:, pl.ds(pl.multiple_of(WIDE + place * CORE_KV, CORE_KV), CORE_KV)]
         dk_ref[:, pl.ds(pl.multiple_of(place * CORE_KV, CORE_KV), CORE_KV)] = (
             near.astype(F32) + far.astype(F32)
         ).astype(BF)
 
 
-def hidden_join(own, fars, dk0, swapped):
+def hidden_join(own, far, dk0, swapped):
     return pl.pallas_call(
         hidden_join_kernel,
         out_shape=(sds((ROWS, N_DP * SHARD)), sds((ROWS, 2 * CORE_KV))),
-        in_specs=[VM] * 5,
+        in_specs=[VM] * 4,
         out_specs=(VM, VM),
-        scratch_shapes=[pltpu.VMEM((ROWS, WIDE), BF)],
         compiler_params=params(),
         cost_estimate=cost(0, 3e6),
-    )(own, *fars, dk0, swapped)
+    )(own, far, dk0, swapped)
 
 
 def heads_join_kernel(o0, dq0, swapped, o_ref, dq_ref):
@@ -658,8 +670,25 @@
     )(a, b)
 
 
+def add_one_kernel(a, b, o):
+    o[0:HALF, :] = (a[...].astype(F32) + b[0:HALF, :].astype(F32)).astype(BF)
+    if o.shape[0] > HALF:
+        o[HALF:, :] = jnp.zeros((o.shape[0] - HALF, CORE_KV), BF)
+
+
+def add_one(a, b, spare):
+    return pl.pallas_call(
+        add_one_kernel,
+        out_shape=sds((HALF + spare, CORE_KV)),
+        in_specs=[VM] * 2,
+        out_specs=VM,
+        compiler_params=params(),
+        cost_estimate=cost(0 if spare else 1e9, 1e3),
+    )(a, b)
+
+
 def add_two_kernel(a, b, o):
-    o[...] = a[...].astype(F32) + b[...].astype(F32)
+    o[...] = a[0:HALF, :].astype(F32) + b[...].astype(F32)
 
 
 def add_two(a, b):
@@ -669,7 +698,7 @@
         in_specs=[VM] * 2,
         out_specs=VM,
         compiler_params=params(),
-        cost_estimate=cost(0, 1e6),
+        cost_estimate=cost(3e9, 1e6),
     )(a, b)
 
 
@@ -731,19 +760,21 @@
     o0, dq0, dk0, dk2, swap_out, dv1 = attention_second(e, inv, q, g, *ps, vp1, rv1, first, first_dk)
     rdv1 = swap(dv1, "seq", 2)
     gv, gv_keep, gv_send = value_grad((dv0, dv1), (rdv0, rdv1))
-    send_a = weight_grad_far(1, gv, ps)
-    far_a = swap(send_a, "dp", 1)
-    own_a = weight_grad_far(0, after(gv, send_a), ps)
+    send5, send7 = weight_grad_sent(gv, ps)
+    far5, far7 = swap(send5, "dp", 1), swap(send7, "dp", 1)
+    own4, own6 = weight_grad_kept(after(gv, send5), ps)
     gvs = swap(gv_send, "seq", 1)
     swapped = swap(after(swap_out, gv), "seq", 1)
-    gh0, gh_a, gh_b = hidden_grad(gv_keep, gvs, wp, wps, dk2, swapped)
+    gh0, gh_send = hidden_grad(gv_keep, gvs, wp, wps, dk2, swapped)
     send_b, own_b = weight_grad_near(after(gv, gh0), ps)
     far_b = swap(send_b, "dp", 2)
-    s4, s6 = add_pair(own_a, far_a)
-    t6, t4 = swap(s6, "dp", 6), swap(s4, "dp", 4)
+    s4 = add_one(own4, far5, SPARE)
+    t4 = swap(s4, "dp", 4)
+    s6 = add_one(own6, after(far7, s4), 0)
+    t6 = swap(s6, "dp", 6)
     t46 = add_two(t4, t6)
     s0, s1 = add_pair(own_b, far_b)
-    gh_far = swap(gh_a, "seq", 2), swap(gh_b, "seq", 2)
+    gh_far = swap(gh_send, "seq", 2)
     attn_out, grad_queries = heads_join(o0, dq0, swapped)
     s1, attn_out, grad_queries = lax.optimization_barrier((s1, attn_out, grad_queries))
     t1 = swap(s1, "dp", 1)

time: 83.4 us -> 82.1 us (0.984)
  waiting for transfers between devices: 33.9 us -> 32.4 us
    ppermute x27, waiting for transfers between devices: 33.9 us -> 32.4 us  [swap(): return lax.ppermute(x, axis, [(i, i ^ k) for i in range(size)])]
where the time goes in v5:
time: 82.1 us; the launch traced here: 81.9 us
  waiting for transfers between devices  32.4 us (39%)
  starting transfers between devices  30 us (37%)
  Pallas kernels  16.3 us (20%)
  local copies, waits for them, and re-layouts  2.3 us (3%)
    ppermute x27, waiting for transfers between devices, swap(): return lax.ppermute(x, axis, [(i, i ^ k) for i in range(size)])  32.4 us
    ppermute x27, starting transfers between devices, swap(): return lax.ppermute(x, axis, [(i, i ^ k) for i in range(size)])  30 us
    pallas_call x1, Pallas kernels, pack(): pl.pallas_call(pack_kernel, out_shape=(sds((ROWS, QUERY_AT)), sds((ROWS,...  2.89 us
    unnamed x8, local copies, waits for them, and re-layouts  2.3 us
    pallas_call x1, Pallas kernels, attention_second(): pl.pallas_call(attention_second_kernel, out_shape=(sds((ROWS, CORE_Q)),)...  1.85 us
    pallas_call x1, Pallas kernels, attention_first(): pl.pallas_call(attention_first_kernel, out_shape=(sds((4 * ROWS, QUERY_PE...  1.83 us
    pallas_call x1, Pallas kernels, scores(): pl.pallas_call(scores_kernel, out_shape=(sds((10, 4 * ROWS, 2 * ROWS)), s...  1.71 us
  transfers between devices with their start and end apart: 27, of which 11 were waited for; matrix products, arithmetic and copies ran while one was open for 0% of the time, Pallas kernels for 15%

profile of v5, /device:TPU:0, one launch (start us, length us, event | category | flops | bytes accessed | tf_op | source)
XLA Modules:
  0.0 81.9 jit_solution(16214463180563201699)
XLA Ops:
  0.6 2.9 %shard_map.101 = (bf16[128,3200]{1,0:T(8,128)(2,1)}, bf16[128,5760]{1,0:T(8,128)(2,1)}, bf16[320,256]{1,0:T(8,128)(2,1)}) custom-call(bf16[128,5120]{1,0:T(8,128)(2,1)} %bitcast.15, bf16[128,512]{1,0:T(8,128)(2,1)} %bitcast.16, s32[1,128]{1,0:T(1,128)} %doc.1, bf16[640,512]{1,0:T(8,128)(2,1)} %w.1, bf16[128,2560]{1,0:T(8,128)(2,1)} %bitcast.8, ...), custom_call_target="tpu_custom_call" | custom-call | bytes 3000000 | tf_op jit(solution)/shard_map/pallas_call | solution.py:265
  4.0 2.6 %collective-permute-start.1 = (bf16[128,3200]{1,0:T(8,128)(2,1)}, bf16[128,3200]{1,0:T(8,128)(2,1)S(1)}, u32[]{:S(2)}, u32[]{:S(2)}) collective-permute-start(bf16[128,3200]{1,0:T(8,128)(2,1)} %get-tuple-element.62), channel_id=1, source_target_pairs={{0,2},{1,3},{2,0},{3,1},{4,6},{5,7},{6,4},{7,5},{8,10},{9,11},{10,... | collective-permute-start | bytes 2457608 | tf_op jit(solution)/shard_map/ppermute | solution.py:183
  6.6 3.6 %collective-permute-start.7 = (bf16[320,256]{1,0:T(8,128)(2,1)}, bf16[320,256]{1,0:T(8,128)(2,1)S(1)}, u32[]{:S(2)}, u32[]{:S(2)}) collective-permute-start(bf16[320,256]{1,0:T(8,128)(2,1)} %get-tuple-element.64.w), channel_id=1, source_target_pairs={{0,24},{4,28},{8,16},{12,20},{16,8},{20,12},{24,0},{28,4},{1,25},{... | collective-permute-start | bytes 491528 | tf_op jit(solution)/shard_map/ppermute | solution.py:183
  11.0 1.5 %collective-permute-start.2 = (bf16[320,256]{1,0:T(8,128)(2,1)}, bf16[320,256]{1,0:T(8,128)(2,1)S(1)}, u32[]{:S(2)}, u32[]{:S(2)}) collective-permute-start(bf16[320,256]{1,0:T(8,128)(2,1)} %get-tuple-element.64.w), channel_id=1, source_target_pairs={{0,4},{4,0},{8,12},{12,8},{16,20},{20,16},{24,28},{28,24},{1,5},{5... | collective-permute-start | bytes 491528 | tf_op jit(solution)/shard_map/ppermute | solution.py:183
  12.5 1.4 %copy-done = bf16[128,5760]{1,0:T(8,128)(2,1)S(1)} copy-done((bf16[128,5760]{1,0:T(8,128)(2,1)S(1)}, bf16[128,5760]{1,0:T(8,128)(2,1)}, u32[]{:S(2)}) %copy-start) | copy-done | bytes 1474584
  13.9 0.9 %copy-done.3 = bf16[320,256]{1,0:T(8,128)(2,1)S(1)} copy-done((bf16[320,256]{1,0:T(8,128)(2,1)S(1)}, bf16[320,256]{1,0:T(8,128)(2,1)}, u32[]{:S(2)}) %copy-start.3) | copy-done | bytes 163864
  15.8 1.5 %collective-permute-start.8 = (bf16[320,256]{1,0:T(8,128)(2,1)S(1)}, bf16[320,256]{1,0:T(8,128)(2,1)S(1)}, u32[]{:S(2)}, u32[]{:S(2)}) collective-permute-start(bf16[320,256]{1,0:T(8,128)(2,1)S(1)} %collective-permute-done.7.w6), channel_id=1, source_target_pairs={{0,4},{4,0},{8,12},{12,8},{16,20},{20,16},{24,28},{28,24},{1,5},{5... | collective-permute-start | bytes 491528 | tf_op jit(solution)/shard_map/ppermute | solution.py:183
  17.3 7.4 %collective-permute-done.5.w4 = bf16[320,256]{1,0:T(8,128)(2,1)S(1)} collective-permute-done((bf16[320,256]{1,0:T(8,128)(2,1)}, bf16[320,256]{1,0:T(8,128)(2,1)S(1)}, u32[]{:S(2)}, u32[]{:S(2)}) %collective-permute-start.5) | collective-permute-done | bytes 163872 | tf_op jit(solution)/shard_map/ppermute | solution.py:183
  24.7 1.6 %collective-permute-start.6 = (bf16[320,256]{1,0:T(8,128)(2,1)S(1)}, bf16[320,256]{1,0:T(8,128)(2,1)S(1)}, u32[]{:S(2)}, u32[]{:S(2)}) collective-permute-start(bf16[320,256]{1,0:T(8,128)(2,1)S(1)} %collective-permute-done.5.w4), channel_id=1, source_target_pairs={{0,4},{4,0},{8,12},{12,8},{16,20},{20,16},{24,28},{28,24},{1,5},{5... | collective-permute-start | bytes 491528 | tf_op jit(solution)/shard_map/ppermute | solution.py:183
  26.2 3.9 %collective-permute-done.4.w3 = bf16[320,256]{1,0:T(8,128)(2,1)S(1)} collective-permute-done((bf16[320,256]{1,0:T(8,128)(2,1)S(1)}, bf16[320,256]{1,0:T(8,128)(2,1)S(1)}, u32[]{:S(2)}, u32[]{:S(2)}) %collective-permute-start.4) | collective-permute-done | bytes 163872 | tf_op jit(solution)/shard_map/ppermute | solution.py:183
  31.5 1.0 %collective-permute-done.9.h3.p3 = bf16[128,3200]{1,0:T(8,128)(2,1)S(1)} collective-permute-done((bf16[128,3200]{1,0:T(8,128)(2,1)S(1)}, bf16[128,3200]{1,0:T(8,128)(2,1)S(1)}, u32[]{:S(2)}, u32[]{:S(2)}) %collective-permute-start.9) | collective-permute-done | bytes 819232 | tf_op jit(solution)/shard_map/ppermute | solution.py:183
  33.4 1.5 %collective-permute-start.11 = (bf16[512,128]{1,0:T(8,128)(2,1)S(1)}, bf16[512,128]{1,0:T(8,128)(2,1)S(1)}, u32[]{:S(2)}, u32[]{:S(2)}) collective-permute-start(bf16[512,128]{1,0:T(8,128)(2,1)S(1)} %get-tuple-element.75.vp), channel_id=1, source_target_pairs={{0,2},{1,3},{2,0},{3,1},{4,6},{5,7},{6,4},{7,5},{8,10},{9,11},{10,... | collective-permute-start | bytes 393224 | tf_op jit(solution)/shard_map/ppermute | solution.py:183
  35.0 1.7 %shard_map.105 = (bf16[10,512,256]{2,1,0:T(8,128)(2,1)S(1)}, f32[80,256]{1,0:T(8,128)S(1)}) custom-call(bf16[128,2560]{1,0:T(8,128)(2,1)S(1)} %bitcast.9, bf16[128,3200]{1,0:T(8,128)(2,1)S(1)} %get-tuple-element.61.h0.p0, bf16[128,5760]{1,0:T(8,128)(2,1)S(1)} %collective-permute-done.h1.p1, bf16[128,3200]{1,0:T(8,128)(2,1)S(1)} %collective-permute-done.1.h2.p2, ...), custom_call_target="tpu_custom_call" | custom-call | flops 2684354560 | bytes 6000000 | tf_op jit(solution)/shard_map/pallas_call | solution.py:376
  36.7 2.6 %collective-permute-done.10.rv = bf16[512,128]{1,0:T(8,128)(2,1)S(1)} collective-permute-done((bf16[512,128]{1,0:T(8,128)(2,1)S(1)}, bf16[512,128]{1,0:T(8,128)(2,1)S(1)}, u32[]{:S(2)}, u32[]{:S(2)}) %collective-permute-start.10) | collective-permute-done | bytes 131104 | tf_op jit(solution)/shard_map/ppermute | solution.py:183
  39.3 1.8 %shard_map.106 = (bf16[512,640]{1,0:T(8,128)(2,1)S(1)}, bf16[512,128]{1,0:T(8,128)(2,1)S(1)}, bf16[528,128]{1,0:T(8,128)(2,1)S(1)}) custom-call(bf16[10,512,256]{2,1,0:T(8,128)(2,1)S(1)} %get-tuple-element.72.e_ref, f32[80,256]{1,0:T(8,128)S(1)} %get-tuple-element.73.inv_ref, bf16[128,2560]{1,0:T(8,128)(2,1)S(1)} %bitcast.10, ...), custom_call_target="tpu_custom_call" | custom-call | flops 3355443200 | bytes 3000000 | tf_op jit(solution)/shard_map/pallas_call | solution.py:457
  41.7 1.8 %shard_map.107 = (bf16[128,1280]{1,0:T(8,128)(2,1)S(1)}, bf16[128,1280]{1,0:T(8,128)(2,1)S(1)}, bf16[128,256]{1,0:T(8,128)(2,1)S(1)}, bf16[128,256]{1,0:T(8,128)...) custom-call(bf16[10,512,256]{2,1,0:T(8,128)(2,1)S(1)} %get-tuple-element.72.e_ref, ...), custom_call_target="tpu_custom_call" | custom-call | flops 3355443200 | bytes 3000000 | tf_op jit(solution)/shard_map/pallas_call | solution.py:471
  43.5 1.6 %collective-permute-start.13 = (bf16[512,128]{1,0:T(8,128)(2,1)S(1)}, bf16[512,128]{1,0:T(8,128)(2,1)S(1)}, u32[]{:S(2)}, u32[]{:S(2)}) collective-permute-start(bf16[512,128]{1,0:T(8,128)(2,1)S(1)} %get-tuple-element.78.dv1), channel_id=1, source_target_pairs={{0,2},{1,3},{2,0},{3,1},{4,6},{5,7},{6,4},{7,5},{8,10},{9,11},{10,... | collective-permute-start | bytes 393224 | tf_op jit(solution)/shard_map/ppermute | solution.py:183
  45.2 3.9 %collective-permute-done.13.rdv1 = bf16[512,128]{1,0:T(8,128)(2,1)S(1)} collective-permute-done((bf16[512,128]{1,0:T(8,128)(2,1)S(1)}, bf16[512,128]{1,0:T(8,128)(2,1)S(1)}, u32[]{:S(2)}, u32[]{:S(2)}) %collective-permute-start.13) | collective-permute-done | bytes 131104 | tf_op jit(solution)/shard_map/ppermute | solution.py:183
  50.3 1.6 %collective-permute-start.18 = (bf16[336,256]{1,0:T(8,128)(2,1)S(1)}, bf16[336,256]{1,0:T(8,128)(2,1)S(1)}, u32[]{:S(2)}, u32[]{:S(2)}) collective-permute-start(bf16[336,256]{1,0:T(8,128)(2,1)S(1)} %get-tuple-element.96), channel_id=1, source_target_pairs={{0,4},{4,0},{8,12},{12,8},{16,20},{20,16},{24,28},{28,24},{1,5},{5... | collective-permute-start | bytes 516104 | tf_op jit(solution)/shard_map/ppermute | solution.py:183
  53.3 1.2 %collective-permute-start.24 = (bf16[128,3072]{1,0:T(8,128)(2,1)S(1)}, bf16[128,3072]{1,0:T(8,128)(2,1)S(1)}, u32[]{:S(2)}, u32[]{:S(2)}) collective-permute-start(bf16[128,3072]{1,0:T(8,128)(2,1)S(1)} %get-tuple-element.104), channel_id=1, source_target_pairs={{0,2},{1,3},{2,0},{3,1},{4,6},{5,7},{6,4},{7,5},{8,10},{9,11},{10,... | collective-permute-start | bytes 2359304 | tf_op jit(solution)/shard_map/ppermute | solution.py:183
  55.3 1.9 %collective-permute-start.17 = (bf16[640,256]{1,0:T(8,128)(2,1)S(1)}, bf16[640,256]{1,0:T(8,128)(2,1)S(1)}, u32[]{:S(2)}, u32[]{:S(2)}) collective-permute-start(bf16[640,256]{1,0:T(8,128)(2,1)S(1)} %get-tuple-element.88), channel_id=1, source_target_pairs={{0,8},{4,12},{8,0},{12,4},{16,24},{20,28},{24,16},{28,20},{1,9},{5... | collective-permute-start | bytes 983048 | tf_op jit(solution)/shard_map/ppermute | solution.py:183
  57.9 2.7 %collective-permute-start.19 = (bf16[336,256]{1,0:T(8,128)(2,1)S(1)}, bf16[336,256]{1,0:T(8,128)(2,1)S(1)}, u32[]{:S(2)}, u32[]{:S(2)}) collective-permute-start(bf16[336,256]{1,0:T(8,128)(2,1)S(1)} %shard_map.115), channel_id=1, source_target_pairs={{0,16},{4,20},{8,24},{12,28},{16,0},{20,4},{24,8},{28,12},{1,17},{... | collective-permute-start | bytes 516104 | tf_op jit(solution)/shard_map/ppermute | solution.py:183
  60.6 2.2 %collective-permute-start.21 = (bf16[320,256]{1,0:T(8,128)(2,1)S(1)}, bf16[320,256]{1,0:T(8,128)(2,1)S(1)}, u32[]{:S(2)}, u32[]{:S(2)}) collective-permute-start(bf16[320,256]{1,0:T(8,128)(2,1)S(1)} %shard_map.116), channel_id=1, source_target_pairs={{0,24},{4,28},{8,16},{12,20},{16,8},{20,12},{24,0},{28,4},{1,25},{... | collective-permute-start | bytes 491528 | tf_op jit(solution)/shard_map/ppermute | solution.py:183
  62.8 1.2 %shard_map.112 = (bf16[128,2560]{1,0:T(8,128)(2,1)}, bf16[128,2560]{1,0:T(8,128)(2,1)}) custom-call(bf16[128,1280]{1,0:T(8,128)(2,1)S(1)} %get-tuple-element.90.o0, bf16[128,1280]{1,0:T(8,128)(2,1)S(1)} %get-tuple-element.91.dq0, bf16[128,3072]{1,0:T(8,128)(2,1)S(1)} %collective-permute-done.16.swapped), custom_call_target="tpu_custom_call" | custom-call | bytes 4000000 | tf_op jit(solution)/shard_map/pallas_call | solution.py:646
  63.9 4.1 %collective-permute-done.17.b = bf16[640,256]{1,0:T(8,128)(2,1)S(1)} collective-permute-done((bf16[640,256]{1,0:T(8,128)(2,1)S(1)}, bf16[640,256]{1,0:T(8,128)(2,1)S(1)}, u32[]{:S(2)}, u32[]{:S(2)}) %collective-permute-start.17) | collective-permute-done | bytes 327712 | tf_op jit(solution)/shard_map/ppermute | solution.py:183
  68.1 1.6 %collective-permute-start.22 = (bf16[320,256]{1,0:T(8,128)(2,1)S(1)}, bf16[320,256]{1,0:T(8,128)(2,1)S(1)}, u32[]{:S(2)}, u32[]{:S(2)}) collective-permute-start(bf16[320,256]{1,0:T(8,128)(2,1)S(1)} %get-tuple-element.103), channel_id=1, source_target_pairs={{0,4},{4,0},{8,12},{12,8},{16,20},{20,16},{24,28},{28,24},{1,5},{5... | collective-permute-start | bytes 491528 | tf_op jit(solution)/shard_map/ppermute | solution.py:183
  69.6 4.2 %collective-permute-done.21.b = bf16[320,256]{1,0:T(8,128)(2,1)S(1)} collective-permute-done((bf16[320,256]{1,0:T(8,128)(2,1)S(1)}, bf16[320,256]{1,0:T(8,128)(2,1)S(1)}, u32[]{:S(2)}, u32[]{:S(2)}) %collective-permute-start.21) | collective-permute-done | bytes 163872 | tf_op jit(solution)/shard_map/ppermute | solution.py:183
  73.9 1.0 %collective-permute-start.23 = (bf16[320,256]{1,0:T(8,128)(2,1)S(1)}, bf16[320,256]{1,0:T(8,128)(2,1)S(1)}, u32[]{:S(2)}, u32[]{:S(2)}) collective-permute-start(bf16[320,256]{1,0:T(8,128)(2,1)S(1)} %shard_map.118.p0), channel_id=1, source_target_pairs={{0,2},{1,3},{2,0},{3,1},{4,6},{5,7},{6,4},{7,5},{8,10},{9,11},{10,... | collective-permute-start | bytes 491528 | tf_op jit(solution)/shard_map/ppermute | solution.py:183
  74.9 1.4 %shard_map.119 = (bf16[128,5120]{1,0:T(8,128)(2,1)}, bf16[128,512]{1,0:T(8,128)(2,1)}) custom-call(bf16[128,2560]{1,0:T(8,128)(2,1)S(1)} %get-tuple-element.85.own_ref, bf16[128,3072]{1,0:T(8,128)(2,1)S(1)} %collective-permute-done.24.far_ref, bf16[128,256]{1,0:T(8,128)(2,1)S(1)} %get-tuple-element.105.dk0, bf16[128,3072]{1,0:T(8,128)(2,1)S(1)} %collective-permute-done.16.swapped), custom_call_target="tpu_custom_call" | custom-call | bytes 3000000 | tf_op jit(solution)/shard_map/pallas_call | solution.py:625
  76.3 3.0 %collective-permute-done.23.p2 = bf16[320,256]{1,0:T(8,128)(2,1)S(1)} collective-permute-done((bf16[320,256]{1,0:T(8,128)(2,1)S(1)}, bf16[320,256]{1,0:T(8,128)(2,1)S(1)}, u32[]{:S(2)}, u32[]{:S(2)}) %collective-permute-start.23) | collective-permute-done | bytes 163872 | tf_op jit(solution)/shard_map/ppermute | solution.py:183
  79.3 1.4 %collective-permute-done.26.p3 = bf16[320,256]{1,0:T(8,128)(2,1)S(1)} collective-permute-done((bf16[320,256]{1,0:T(8,128)(2,1)S(1)}, bf16[320,256]{1,0:T(8,128)(2,1)S(1)}, u32[]{:S(2)}, u32[]{:S(2)}) %collective-permute-start.26) | collective-permute-done | bytes 163872 | tf_op jit(solution)/shard_map/ppermute | solution.py:183
  80.7 1.2 %shard_map.120 = f32[640,512]{1,0:T(8,128)} custom-call(bf16[320,256]{1,0:T(8,128)(2,1)S(1)} %shard_map.118.p0, bf16[320,256]{1,0:T(8,128)(2,1)S(1)} %collective-permute-done.25.p1, bf16[320,256]{1,0:T(8,128)(2,1)S(1)} %collective-permute-done.23.p2, bf16[320,256]{1,0:T(8,128)(2,1)S(1)} %collective-permute-done.26.p3), custom_call_target="tpu_custom_call" | custom-call | bytes 2000000 | tf_op jit(solution)/shard_map/pallas_call | solution.py:730
  (50 shorter events, 9.5 us)
Async XLA Ops:
  3.5 6.7 %collective-permute-start = (bf16[128,5760]{1,0:T(8,128)(2,1)}, bf16[128,5760]{1,0:T(8,128)(2,1)S(1)}, u32[]{:S(2)}, u32[]{:S(2)}) collective-permute-start(bf16[128,5760]{1,0:T(8,128)(2,1)} %get-tuple-element.59.p), channel_id=1, source_target_pairs={{0,1},{1,0},{2,3},{3,2},{4,5},{5,4},{6,7},{7,6},{8,9},{9,8},{10,11... | collective-permute-start | bytes 4423688 | tf_op jit(solution)/shard_map/ppermute | solution.py:183
  4.0 22.2 %collective-permute-start.1 = (bf16[128,3200]{1,0:T(8,128)(2,1)}, bf16[128,3200]{1,0:T(8,128)(2,1)S(1)}, u32[]{:S(2)}, u32[]{:S(2)}) collective-permute-start(bf16[128,3200]{1,0:T(8,128)(2,1)} %get-tuple-element.62), channel_id=1, source_target_pairs={{0,2},{1,3},{2,0},{3,1},{4,6},{5,7},{6,4},{7,5},{8,10},{9,11},{10,... | collective-permute-start | bytes 2457608 | tf_op jit(solution)/shard_map/ppermute | solution.py:183
  6.6 9.1 %collective-permute-start.7 = (bf16[320,256]{1,0:T(8,128)(2,1)}, bf16[320,256]{1,0:T(8,128)(2,1)S(1)}, u32[]{:S(2)}, u32[]{:S(2)}) collective-permute-start(bf16[320,256]{1,0:T(8,128)(2,1)} %get-tuple-element.64.w), channel_id=1, source_target_pairs={{0,24},{4,28},{8,16},{12,20},{16,8},{20,12},{24,0},{28,4},{1,25},{... | collective-permute-start | bytes 491528 | tf_op jit(solution)/shard_map/ppermute | solution.py:183
  10.2 14.4 %collective-permute-start.5 = (bf16[320,256]{1,0:T(8,128)(2,1)}, bf16[320,256]{1,0:T(8,128)(2,1)S(1)}, u32[]{:S(2)}, u32[]{:S(2)}) collective-permute-start(bf16[320,256]{1,0:T(8,128)(2,1)} %get-tuple-element.64.w), channel_id=1, source_target_pairs={{0,16},{4,20},{8,24},{12,28},{16,0},{20,4},{24,8},{28,12},{1,17},{... | collective-permute-start | bytes 491528 | tf_op jit(solution)/shard_map/ppermute | solution.py:183
  10.2 14.4 %collective-permute-start.3 = (bf16[320,256]{1,0:T(8,128)(2,1)}, bf16[320,256]{1,0:T(8,128)(2,1)S(1)}, u32[]{:S(2)}, u32[]{:S(2)}) collective-permute-start(bf16[320,256]{1,0:T(8,128)(2,1)} %get-tuple-element.64.w), channel_id=1, source_target_pairs={{0,8},{4,12},{8,0},{12,4},{16,24},{20,28},{24,16},{28,20},{1,9},{5... | collective-permute-start | bytes 491528 | tf_op jit(solution)/shard_map/ppermute | solution.py:183
  11.0 13.6 %collective-permute-start.2 = (bf16[320,256]{1,0:T(8,128)(2,1)}, bf16[320,256]{1,0:T(8,128)(2,1)S(1)}, u32[]{:S(2)}, u32[]{:S(2)}) collective-permute-start(bf16[320,256]{1,0:T(8,128)(2,1)} %get-tuple-element.64.w), channel_id=1, source_target_pairs={{0,4},{4,0},{8,12},{12,8},{16,20},{20,16},{24,28},{28,24},{1,5},{5... | collective-permute-start | bytes 491528 | tf_op jit(solution)/shard_map/ppermute | solution.py:183
  12.5 1.4 %copy-start = (bf16[128,5760]{1,0:T(8,128)(2,1)S(1)}, bf16[128,5760]{1,0:T(8,128)(2,1)}, u32[]{:S(2)}) copy-start(bf16[128,5760]{1,0:T(8,128)(2,1)} %get-tuple-element.59.p) | copy-start | bytes 4423684
  13.9 0.9 %copy-start.3 = (bf16[320,256]{1,0:T(8,128)(2,1)S(1)}, bf16[320,256]{1,0:T(8,128)(2,1)}, u32[]{:S(2)}) copy-start(bf16[320,256]{1,0:T(8,128)(2,1)} %get-tuple-element.64.w) | copy-start | bytes 491524
  15.8 10.5 %collective-permute-start.8 = (bf16[320,256]{1,0:T(8,128)(2,1)S(1)}, bf16[320,256]{1,0:T(8,128)(2,1)S(1)}, u32[]{:S(2)}, u32[]{:S(2)}) collective-permute-start(bf16[320,256]{1,0:T(8,128)(2,1)S(1)} %collective-permute-done.7.w6), channel_id=1, source_target_pairs={{0,4},{4,0},{8,12},{12,8},{16,20},{20,16},{24,28},{28,24},{1,5},{5... | collective-permute-start | bytes 491528 | tf_op jit(solution)/shard_map/ppermute | solution.py:183
  24.7 5.4 %collective-permute-start.4 = (bf16[320,256]{1,0:T(8,128)(2,1)S(1)}, bf16[320,256]{1,0:T(8,128)(2,1)S(1)}, u32[]{:S(2)}, u32[]{:S(2)}) collective-permute-start(bf16[320,256]{1,0:T(8,128)(2,1)S(1)} %collective-permute-done.2.w1), channel_id=1, source_target_pairs={{0,8},{4,12},{8,0},{12,4},{16,24},{20,28},{24,16},{28,20},{1,9},{5... | collective-permute-start | bytes 491528 | tf_op jit(solution)/shard_map/ppermute | solution.py:183
  24.7 5.5 %collective-permute-start.6 = (bf16[320,256]{1,0:T(8,128)(2,1)S(1)}, bf16[320,256]{1,0:T(8,128)(2,1)S(1)}, u32[]{:S(2)}, u32[]{:S(2)}) collective-permute-start(bf16[320,256]{1,0:T(8,128)(2,1)S(1)} %collective-permute-done.5.w4), channel_id=1, source_target_pairs={{0,4},{4,0},{8,12},{12,8},{16,20},{20,16},{24,28},{28,24},{1,5},{5... | collective-permute-start | bytes 491528 | tf_op jit(solution)/shard_map/ppermute | solution.py:183
  30.2 2.3 %collective-permute-start.9 = (bf16[128,3200]{1,0:T(8,128)(2,1)S(1)}, bf16[128,3200]{1,0:T(8,128)(2,1)S(1)}, u32[]{:S(2)}, u32[]{:S(2)}) collective-permute-start(bf16[128,3200]{1,0:T(8,128)(2,1)S(1)} %collective-permute-done.1.h2.p2), channel_id=1, source_target_pairs={{0,1},{1,0},{2,3},{3,2},{4,5},{5,4},{6,7},{7,6},{8,9},{9,8},{10,11... | collective-permute-start | bytes 2457608 | tf_op jit(solution)/shard_map/ppermute | solution.py:183
  30.9 4.1 %copy-start.1 = (bf16[1,128,2560]{2,1,0:T(8,128)(2,1)S(1)}, bf16[1,128,2560]{2,1,0:T(8,128)(2,1)}, u32[]{:S(2)}) copy-start(bf16[1,128,2560]{2,1,0:T(8,128)(2,1)} %param.7) | copy-start | bytes 1966084
  30.9 21.5 %collective-permute-start.15 = (bf16[2560,256]{1,0:T(8,128)(2,1)S(1)}, bf16[2560,256]{1,0:T(8,128)(2,1)S(1)}, u32[]{:S(2)}, u32[]{:S(2)}) collective-permute-start(bf16[2560,256]{1,0:T(8,128)(2,1)S(1)} %get-tuple-element.69.wp), channel_id=1, source_target_pairs={{0,1},{1,0},{2,3},{3,2},{4,5},{5,4},{6,7},{7,6},{8,9},{9,8},{10,11... | collective-permute-start | bytes 3932168 | tf_op jit(solution)/shard_map/ppermute | solution.py:183
  32.9 6.4 %collective-permute-start.10 = (bf16[512,128]{1,0:T(8,128)(2,1)S(1)}, bf16[512,128]{1,0:T(8,128)(2,1)S(1)}, u32[]{:S(2)}, u32[]{:S(2)}) collective-permute-start(bf16[512,128]{1,0:T(8,128)(2,1)S(1)} %get-tuple-element.70.vp), channel_id=1, source_target_pairs={{0,2},{1,3},{2,0},{3,1},{4,6},{5,7},{6,4},{7,5},{8,10},{9,11},{10,... | collective-permute-start | bytes 393224 | tf_op jit(solution)/shard_map/ppermute | solution.py:183
  33.4 5.9 %copy-start.2 = (bf16[1,128,2560]{2,1,0:T(8,128)(2,1)S(1)}, bf16[1,128,2560]{2,1,0:T(8,128)(2,1)}, u32[]{:S(2)}) copy-start(bf16[1,128,2560]{2,1,0:T(8,128)(2,1)} %param.11) | copy-start | bytes 1966084
  33.4 8.2 %collective-permute-start.11 = (bf16[512,128]{1,0:T(8,128)(2,1)S(1)}, bf16[512,128]{1,0:T(8,128)(2,1)S(1)}, u32[]{:S(2)}, u32[]{:S(2)}) collective-permute-start(bf16[512,128]{1,0:T(8,128)(2,1)S(1)} %get-tuple-element.75.vp), channel_id=1, source_target_pairs={{0,2},{1,3},{2,0},{3,1},{4,6},{5,7},{6,4},{7,5},{8,10},{9,11},{10,... | collective-permute-start | bytes 393224 | tf_op jit(solution)/shard_map/ppermute | solution.py:183
  41.1 7.9 %collective-permute-start.12 = (bf16[528,128]{1,0:T(8,128)(2,1)S(1)}, bf16[528,128]{1,0:T(8,128)(2,1)S(1)}, u32[]{:S(2)}, u32[]{:S(2)}) collective-permute-start(bf16[528,128]{1,0:T(8,128)(2,1)S(1)} %get-tuple-element.74.dv0), channel_id=1, source_target_pairs={{0,2},{1,3},{2,0},{3,1},{4,6},{5,7},{6,4},{7,5},{8,10},{9,11},{10,... | collective-permute-start | bytes 405512 | tf_op jit(solution)/shard_map/ppermute | solution.py:183
  43.5 5.5 %collective-permute-start.13 = (bf16[512,128]{1,0:T(8,128)(2,1)S(1)}, bf16[512,128]{1,0:T(8,128)(2,1)S(1)}, u32[]{:S(2)}, u32[]{:S(2)}) collective-permute-start(bf16[512,128]{1,0:T(8,128)(2,1)S(1)} %get-tuple-element.78.dv1), channel_id=1, source_target_pairs={{0,2},{1,3},{2,0},{3,1},{4,6},{5,7},{6,4},{7,5},{8,10},{9,11},{10,... | collective-permute-start | bytes 393224 | tf_op jit(solution)/shard_map/ppermute | solution.py:183
  49.1 3.3 %collective-permute-start.16 = (bf16[128,3072]{1,0:T(8,128)(2,1)S(1)}, bf16[128,3072]{1,0:T(8,128)(2,1)S(1)}, u32[]{:S(2)}, u32[]{:S(2)}) collective-permute-start(bf16[128,3072]{1,0:T(8,128)(2,1)S(1)} %get-tuple-element.84), channel_id=1, source_target_pairs={{0,1},{1,0},{2,3},{3,2},{4,5},{5,4},{6,7},{7,6},{8,9},{9,8},{10,11... | collective-permute-start | bytes 2359304 | tf_op jit(solution)/shard_map/ppermute | solution.py:183
  49.2 3.2 %collective-permute-start.14 = (bf16[256,256]{1,0:T(8,128)(2,1)S(1)}, bf16[256,256]{1,0:T(8,128)(2,1)S(1)}, u32[]{:S(2)}, u32[]{:S(2)}) collective-permute-start(bf16[256,256]{1,0:T(8,128)(2,1)S(1)} %get-tuple-element.81), channel_id=1, source_target_pairs={{0,1},{1,0},{2,3},{3,2},{4,5},{5,4},{6,7},{7,6},{8,9},{9,8},{10,11... | collective-permute-start | bytes 393224 | tf_op jit(solution)/shard_map/ppermute | solution.py:183
  50.3 7.5 %collective-permute-start.18 = (bf16[336,256]{1,0:T(8,128)(2,1)S(1)}, bf16[336,256]{1,0:T(8,128)(2,1)S(1)}, u32[]{:S(2)}, u32[]{:S(2)}) collective-permute-start(bf16[336,256]{1,0:T(8,128)(2,1)S(1)} %get-tuple-element.96), channel_id=1, source_target_pairs={{0,4},{4,0},{8,12},{12,8},{16,20},{20,16},{24,28},{28,24},{1,5},{5... | collective-permute-start | bytes 516104 | tf_op jit(solution)/shard_map/ppermute | solution.py:183
  51.8 8.7 %collective-permute-start.20 = (bf16[320,256]{1,0:T(8,128)(2,1)S(1)}, bf16[320,256]{1,0:T(8,128)(2,1)S(1)}, u32[]{:S(2)}, u32[]{:S(2)}) collective-permute-start(bf16[320,256]{1,0:T(8,128)(2,1)S(1)} %get-tuple-element.100), channel_id=1, source_target_pairs={{0,4},{4,0},{8,12},{12,8},{16,20},{20,16},{24,28},{28,24},{1,5},{5... | collective-permute-start | bytes 491528 | tf_op jit(solution)/shard_map/ppermute | solution.py:183
  53.3 21.7 %collective-permute-start.24 = (bf16[128,3072]{1,0:T(8,128)(2,1)S(1)}, bf16[128,3072]{1,0:T(8,128)(2,1)S(1)}, u32[]{:S(2)}, u32[]{:S(2)}) collective-permute-start(bf16[128,3072]{1,0:T(8,128)(2,1)S(1)} %get-tuple-element.104), channel_id=1, source_target_pairs={{0,2},{1,3},{2,0},{3,1},{4,6},{5,7},{6,4},{7,5},{8,10},{9,11},{10,... | collective-permute-start | bytes 2359304 | tf_op jit(solution)/shard_map/ppermute | solution.py:183
  55.3 12.7 %collective-permute-start.17 = (bf16[640,256]{1,0:T(8,128)(2,1)S(1)}, bf16[640,256]{1,0:T(8,128)(2,1)S(1)}, u32[]{:S(2)}, u32[]{:S(2)}) collective-permute-start(bf16[640,256]{1,0:T(8,128)(2,1)S(1)} %get-tuple-element.88), channel_id=1, source_target_pairs={{0,8},{4,12},{8,0},{12,4},{16,24},{20,28},{24,16},{28,20},{1,9},{5... | collective-permute-start | bytes 983048 | tf_op jit(solution)/shard_map/ppermute | solution.py:183
  57.9 15.9 %collective-permute-start.19 = (bf16[336,256]{1,0:T(8,128)(2,1)S(1)}, bf16[336,256]{1,0:T(8,128)(2,1)S(1)}, u32[]{:S(2)}, u32[]{:S(2)}) collective-permute-start(bf16[336,256]{1,0:T(8,128)(2,1)S(1)} %shard_map.115), channel_id=1, source_target_pairs={{0,16},{4,20},{8,24},{12,28},{16,0},{20,4},{24,8},{28,12},{1,17},{... | collective-permute-start | bytes 516104 | tf_op jit(solution)/shard_map/ppermute | solution.py:183
  60.6 13.2 %collective-permute-start.21 = (bf16[320,256]{1,0:T(8,128)(2,1)S(1)}, bf16[320,256]{1,0:T(8,128)(2,1)S(1)}, u32[]{:S(2)}, u32[]{:S(2)}) collective-permute-start(bf16[320,256]{1,0:T(8,128)(2,1)S(1)} %shard_map.116), channel_id=1, source_target_pairs={{0,24},{4,28},{8,16},{12,20},{16,8},{20,12},{24,0},{28,4},{1,25},{... | collective-permute-start | bytes 491528 | tf_op jit(solution)/shard_map/ppermute | solution.py:183
  68.1 5.8 %collective-permute-start.22 = (bf16[320,256]{1,0:T(8,128)(2,1)S(1)}, bf16[320,256]{1,0:T(8,128)(2,1)S(1)}, u32[]{:S(2)}, u32[]{:S(2)}) collective-permute-start(bf16[320,256]{1,0:T(8,128)(2,1)S(1)} %get-tuple-element.103), channel_id=1, source_target_pairs={{0,4},{4,0},{8,12},{12,8},{16,20},{20,16},{24,28},{28,24},{1,5},{5... | collective-permute-start | bytes 491528 | tf_op jit(solution)/shard_map/ppermute | solution.py:183
  73.9 5.4 %collective-permute-start.23 = (bf16[320,256]{1,0:T(8,128)(2,1)S(1)}, bf16[320,256]{1,0:T(8,128)(2,1)S(1)}, u32[]{:S(2)}, u32[]{:S(2)}) collective-permute-start(bf16[320,256]{1,0:T(8,128)(2,1)S(1)} %shard_map.118.p0), channel_id=1, source_target_pairs={{0,2},{1,3},{2,0},{3,1},{4,6},{5,7},{6,4},{7,5},{8,10},{9,11},{10,... | collective-permute-start | bytes 491528 | tf_op jit(solution)/shard_map/ppermute | solution.py:183
  74.9 4.4 %collective-permute-start.25 = (bf16[320,256]{1,0:T(8,128)(2,1)S(1)}, bf16[320,256]{1,0:T(8,128)(2,1)S(1)}, u32[]{:S(2)}, u32[]{:S(2)}) collective-permute-start(bf16[320,256]{1,0:T(8,128)(2,1)S(1)} %shard_map.118.p0), channel_id=1, source_target_pairs={{0,1},{1,0},{2,3},{3,2},{4,5},{5,4},{6,7},{7,6},{8,9},{9,8},{10,11... | collective-permute-start | bytes 491528 | tf_op jit(solution)/shard_map/ppermute | solution.py:183
  79.3 1.4 %collective-permute-start.26 = (bf16[320,256]{1,0:T(8,128)(2,1)S(1)}, bf16[320,256]{1,0:T(8,128)(2,1)S(1)}, u32[]{:S(2)}, u32[]{:S(2)}) collective-permute-start(bf16[320,256]{1,0:T(8,128)(2,1)S(1)} %collective-permute-done.23.p2), channel_id=1, source_target_pairs={{0,1},{1,0},{2,3},{3,2},{4,5},{5,4},{6,7},{7,6},{8,9},{9,8},{10,11... | collective-permute-start | bytes 491528 | tf_op jit(solution)/shard_map/ppermute | solution.py:183

commit v6 on v5

--- a/solution.py
+++ b/solution.py
@@ -683,12 +683,12 @@
         in_specs=[VM] * 2,
         out_specs=VM,
         compiler_params=params(),
-        cost_estimate=cost(0 if spare else 1e9, 1e3),
+        cost_estimate=cost(1e9, 1e3),
     )(a, b)
 
 
 def add_two_kernel(a, b, o):
-    o[...] = a[0:HALF, :].astype(F32) + b[...].astype(F32)
+    o[...] = a[...].astype(F32) + b[...].astype(F32)
 
 
 def add_two(a, b):
@@ -768,7 +768,7 @@
     gh0, gh_send = hidden_grad(gv_keep, gvs, wp, wps, dk2, swapped)
     send_b, own_b = weight_grad_near(after(gv, gh0), ps)
     far_b = swap(send_b, "dp", 2)
-    s4 = add_one(own4, far5, SPARE)
+    s4 = add_one(own4, far5, 0)
     t4 = swap(s4, "dp", 4)
     s6 = add_one(own6, after(far7, s4), 0)
     t6 = swap(s6, "dp", 6)

time: 82.1 us -> 81.6 us (level)
  transfers between devices with their start and end apart: 27 -> 27, of which waited for: 11 -> 12; matrix products, arithmetic and copies ran while one was open for 0% -> 0% of each run, Pallas kernels for 15% -> 15%
where the time goes in v6:
time: 81.6 us; the launch traced here: 81.4 us
  waiting for transfers between devices  31.8 us (39%)
  starting transfers between devices  30.2 us (37%)
  Pallas kernels  16.3 us (20%)
  local copies, waits for them, and re-layouts  2.3 us (3%)
    ppermute x27, waiting for transfers between devices, swap(): return lax.ppermute(x, axis, [(i, i ^ k) for i in range(size)])  31.8 us
    ppermute x27, starting transfers between devices, swap(): return lax.ppermute(x, axis, [(i, i ^ k) for i in range(size)])  30.2 us
    pallas_call x1, Pallas kernels, pack(): pl.pallas_call(pack_kernel, out_shape=(sds((ROWS, QUERY_AT)), sds((ROWS,...  2.89 us
    unnamed x8, local copies, waits for them, and re-layouts  2.3 us
    pallas_call x1, Pallas kernels, attention_second(): pl.pallas_call(attention_second_kernel, out_shape=(sds((ROWS, CORE_Q)),)...  1.85 us
    pallas_call x1, Pallas kernels, attention_first(): pl.pallas_call(attention_first_kernel, out_shape=(sds((4 * ROWS, QUERY_PE...  1.83 us
    pallas_call x1, Pallas kernels, scores(): pl.pallas_call(scores_kernel, out_shape=(sds((10, 4 * ROWS, 2 * ROWS)), s...  1.71 us
  transfers between devices with their start and end apart: 27, of which 12 were waited for; matrix products, arithmetic and copies ran while one was open for 0% of the time, Pallas kernels for 15%

profile of v6, /device:TPU:0, one launch (start us, length us, event | category | flops | bytes accessed | tf_op | source)
XLA Modules:
  0.0 81.4 jit_solution(5205805246540453672)
XLA Ops:
  0.6 2.9 %shard_map.101 = (bf16[128,3200]{1,0:T(8,128)(2,1)}, bf16[128,5760]{1,0:T(8,128)(2,1)}, bf16[320,256]{1,0:T(8,128)(2,1)}) custom-call(bf16[128,5120]{1,0:T(8,128)(2,1)} %bitcast.15, bf16[128,512]{1,0:T(8,128)(2,1)} %bitcast.16, s32[1,128]{1,0:T(1,128)} %doc.1, bf16[640,512]{1,0:T(8,128)(2,1)} %w.1, bf16[128,2560]{1,0:T(8,128)(2,1)} %bitcast.8, ...), custom_call_target="tpu_custom_call" | custom-call | bytes 3000000 | tf_op jit(solution)/shard_map/pallas_call | solution.py:265
  4.0 2.6 %collective-permute-start.1 = (bf16[128,3200]{1,0:T(8,128)(2,1)}, bf16[128,3200]{1,0:T(8,128)(2,1)S(1)}, u32[]{:S(2)}, u32[]{:S(2)}) collective-permute-start(bf16[128,3200]{1,0:T(8,128)(2,1)} %get-tuple-element.62), channel_id=1, source_target_pairs={{0,2},{1,3},{2,0},{3,1},{4,6},{5,7},{6,4},{7,5},{8,10},{9,11},{10,... | collective-permute-start | bytes 2457608 | tf_op jit(solution)/shard_map/ppermute | solution.py:183
  6.6 3.6 %collective-permute-start.7 = (bf16[320,256]{1,0:T(8,128)(2,1)}, bf16[320,256]{1,0:T(8,128)(2,1)S(1)}, u32[]{:S(2)}, u32[]{:S(2)}) collective-permute-start(bf16[320,256]{1,0:T(8,128)(2,1)} %get-tuple-element.64.w), channel_id=1, source_target_pairs={{0,24},{4,28},{8,16},{12,20},{16,8},{20,12},{24,0},{28,4},{1,25},{... | collective-permute-start | bytes 491528 | tf_op jit(solution)/shard_map/ppermute | solution.py:183
  11.0 1.5 %collective-permute-start.2 = (bf16[320,256]{1,0:T(8,128)(2,1)}, bf16[320,256]{1,0:T(8,128)(2,1)S(1)}, u32[]{:S(2)}, u32[]{:S(2)}) collective-permute-start(bf16[320,256]{1,0:T(8,128)(2,1)} %get-tuple-element.64.w), channel_id=1, source_target_pairs={{0,4},{4,0},{8,12},{12,8},{16,20},{20,16},{24,28},{28,24},{1,5},{5... | collective-permute-start | bytes 491528 | tf_op jit(solution)/shard_map/ppermute | solution.py:183
  12.5 1.4 %copy-done = bf16[128,5760]{1,0:T(8,128)(2,1)S(1)} copy-done((bf16[128,5760]{1,0:T(8,128)(2,1)S(1)}, bf16[128,5760]{1,0:T(8,128)(2,1)}, u32[]{:S(2)}) %copy-start) | copy-done | bytes 1474584
  15.8 1.5 %collective-permute-start.8 = (bf16[320,256]{1,0:T(8,128)(2,1)S(1)}, bf16[320,256]{1,0:T(8,128)(2,1)S(1)}, u32[]{:S(2)}, u32[]{:S(2)}) collective-permute-start(bf16[320,256]{1,0:T(8,128)(2,1)S(1)} %collective-permute-done.7.w6), channel_id=1, source_target_pairs={{0,4},{4,0},{8,12},{12,8},{16,20},{20,16},{24,28},{28,24},{1,5},{5... | collective-permute-start | bytes 491528 | tf_op jit(solution)/shard_map/ppermute | solution.py:183
  17.3 7.4 %collective-permute-done.5.w4 = bf16[320,256]{1,0:T(8,128)(2,1)S(1)} collective-permute-done((bf16[320,256]{1,0:T(8,128)(2,1)}, bf16[320,256]{1,0:T(8,128)(2,1)S(1)}, u32[]{:S(2)}, u32[]{:S(2)}) %collective-permute-start.5) | collective-permute-done | bytes 163872 | tf_op jit(solution)/shard_map/ppermute | solution.py:183
  24.7 1.6 %collective-permute-start.6 = (bf16[320,256]{1,0:T(8,128)(2,1)S(1)}, bf16[320,256]{1,0:T(8,128)(2,1)S(1)}, u32[]{:S(2)}, u32[]{:S(2)}) collective-permute-start(bf16[320,256]{1,0:T(8,128)(2,1)S(1)} %collective-permute-done.5.w4), channel_id=1, source_target_pairs={{0,4},{4,0},{8,12},{12,8},{16,20},{20,16},{24,28},{28,24},{1,5},{5... | collective-permute-start | bytes 491528 | tf_op jit(solution)/shard_map/ppermute | solution.py:183
  26.2 3.9 %collective-permute-done.4.w3 = bf16[320,256]{1,0:T(8,128)(2,1)S(1)} collective-permute-done((bf16[320,256]{1,0:T(8,128)(2,1)S(1)}, bf16[320,256]{1,0:T(8,128)(2,1)S(1)}, u32[]{:S(2)}, u32[]{:S(2)}) %collective-permute-start.4) | collective-permute-done | bytes 163872 | tf_op jit(solution)/shard_map/ppermute | solution.py:183
  31.5 1.0 %collective-permute-done.9.h3.p3 = bf16[128,3200]{1,0:T(8,128)(2,1)S(1)} collective-permute-done((bf16[128,3200]{1,0:T(8,128)(2,1)S(1)}, bf16[128,3200]{1,0:T(8,128)(2,1)S(1)}, u32[]{:S(2)}, u32[]{:S(2)}) %collective-permute-start.9) | collective-permute-done | bytes 819232 | tf_op jit(solution)/shard_map/ppermute | solution.py:183
  33.4 1.5 %collective-permute-start.11 = (bf16[512,128]{1,0:T(8,128)(2,1)S(1)}, bf16[512,128]{1,0:T(8,128)(2,1)S(1)}, u32[]{:S(2)}, u32[]{:S(2)}) collective-permute-start(bf16[512,128]{1,0:T(8,128)(2,1)S(1)} %get-tuple-element.75.vp), channel_id=1, source_target_pairs={{0,2},{1,3},{2,0},{3,1},{4,6},{5,7},{6,4},{7,5},{8,10},{9,11},{10,... | collective-permute-start | bytes 393224 | tf_op jit(solution)/shard_map/ppermute | solution.py:183
  35.0 1.7 %shard_map.105 = (bf16[10,512,256]{2,1,0:T(8,128)(2,1)S(1)}, f32[80,256]{1,0:T(8,128)S(1)}) custom-call(bf16[128,2560]{1,0:T(8,128)(2,1)S(1)} %bitcast.9, bf16[128,3200]{1,0:T(8,128)(2,1)S(1)} %get-tuple-element.61.h0.p0, bf16[128,5760]{1,0:T(8,128)(2,1)S(1)} %collective-permute-done.h1.p1, bf16[128,3200]{1,0:T(8,128)(2,1)S(1)} %collective-permute-done.1.h2.p2, ...), custom_call_target="tpu_custom_call" | custom-call | flops 2684354560 | bytes 6000000 | tf_op jit(solution)/shard_map/pallas_call | solution.py:376
  36.7 2.6 %collective-permute-done.10.rv = bf16[512,128]{1,0:T(8,128)(2,1)S(1)} collective-permute-done((bf16[512,128]{1,0:T(8,128)(2,1)S(1)}, bf16[512,128]{1,0:T(8,128)(2,1)S(1)}, u32[]{:S(2)}, u32[]{:S(2)}) %collective-permute-start.10) | collective-permute-done | bytes 131104 | tf_op jit(solution)/shard_map/ppermute | solution.py:183
  39.3 1.8 %shard_map.106 = (bf16[512,640]{1,0:T(8,128)(2,1)S(1)}, bf16[512,128]{1,0:T(8,128)(2,1)S(1)}, bf16[528,128]{1,0:T(8,128)(2,1)S(1)}) custom-call(bf16[10,512,256]{2,1,0:T(8,128)(2,1)S(1)} %get-tuple-element.72.e_ref, f32[80,256]{1,0:T(8,128)S(1)} %get-tuple-element.73.inv_ref, bf16[128,2560]{1,0:T(8,128)(2,1)S(1)} %bitcast.10, ...), custom_call_target="tpu_custom_call" | custom-call | flops 3355443200 | bytes 3000000 | tf_op jit(solution)/shard_map/pallas_call | solution.py:457
  41.7 1.8 %shard_map.107 = (bf16[128,1280]{1,0:T(8,128)(2,1)S(1)}, bf16[128,1280]{1,0:T(8,128)(2,1)S(1)}, bf16[128,256]{1,0:T(8,128)(2,1)S(1)}, bf16[128,256]{1,0:T(8,128)...) custom-call(bf16[10,512,256]{2,1,0:T(8,128)(2,1)S(1)} %get-tuple-element.72.e_ref, ...), custom_call_target="tpu_custom_call" | custom-call | flops 3355443200 | bytes 3000000 | tf_op jit(solution)/shard_map/pallas_call | solution.py:471
  43.5 1.6 %collective-permute-start.13 = (bf16[512,128]{1,0:T(8,128)(2,1)S(1)}, bf16[512,128]{1,0:T(8,128)(2,1)S(1)}, u32[]{:S(2)}, u32[]{:S(2)}) collective-permute-start(bf16[512,128]{1,0:T(8,128)(2,1)S(1)} %get-tuple-element.78.dv1), channel_id=1, source_target_pairs={{0,2},{1,3},{2,0},{3,1},{4,6},{5,7},{6,4},{7,5},{8,10},{9,11},{10,... | collective-permute-start | bytes 393224 | tf_op jit(solution)/shard_map/ppermute | solution.py:183
  45.2 3.9 %collective-permute-done.13.rdv1 = bf16[512,128]{1,0:T(8,128)(2,1)S(1)} collective-permute-done((bf16[512,128]{1,0:T(8,128)(2,1)S(1)}, bf16[512,128]{1,0:T(8,128)(2,1)S(1)}, u32[]{:S(2)}, u32[]{:S(2)}) %collective-permute-start.13) | collective-permute-done | bytes 131104 | tf_op jit(solution)/shard_map/ppermute | solution.py:183
  50.3 1.6 %collective-permute-start.18 = (bf16[336,256]{1,0:T(8,128)(2,1)S(1)}, bf16[336,256]{1,0:T(8,128)(2,1)S(1)}, u32[]{:S(2)}, u32[]{:S(2)}) collective-permute-start(bf16[336,256]{1,0:T(8,128)(2,1)S(1)} %get-tuple-element.96), channel_id=1, source_target_pairs={{0,4},{4,0},{8,12},{12,8},{16,20},{20,16},{24,28},{28,24},{1,5},{5... | collective-permute-start | bytes 516104 | tf_op jit(solution)/shard_map/ppermute | solution.py:183
  54.8 1.9 %collective-permute-start.17 = (bf16[640,256]{1,0:T(8,128)(2,1)S(1)}, bf16[640,256]{1,0:T(8,128)(2,1)S(1)}, u32[]{:S(2)}, u32[]{:S(2)}) collective-permute-start(bf16[640,256]{1,0:T(8,128)(2,1)S(1)} %get-tuple-element.88), channel_id=1, source_target_pairs={{0,8},{4,12},{8,0},{12,4},{16,24},{20,28},{24,16},{28,20},{1,9},{5... | collective-permute-start | bytes 983048 | tf_op jit(solution)/shard_map/ppermute | solution.py:183
  56.7 1.1 %collective-permute-start.24 = (bf16[128,3072]{1,0:T(8,128)(2,1)S(1)}, bf16[128,3072]{1,0:T(8,128)(2,1)S(1)}, u32[]{:S(2)}, u32[]{:S(2)}) collective-permute-start(bf16[128,3072]{1,0:T(8,128)(2,1)S(1)} %get-tuple-element.104), channel_id=1, source_target_pairs={{0,2},{1,3},{2,0},{3,1},{4,6},{5,7},{6,4},{7,5},{8,10},{9,11},{10,... | collective-permute-start | bytes 2359304 | tf_op jit(solution)/shard_map/ppermute | solution.py:183
  57.8 2.7 %collective-permute-start.19 = (bf16[320,256]{1,0:T(8,128)(2,1)S(1)}, bf16[320,256]{1,0:T(8,128)(2,1)S(1)}, u32[]{:S(2)}, u32[]{:S(2)}) collective-permute-start(bf16[320,256]{1,0:T(8,128)(2,1)S(1)} %shard_map.115), channel_id=1, source_target_pairs={{0,16},{4,20},{8,24},{12,28},{16,0},{20,4},{24,8},{28,12},{1,17},{... | collective-permute-start | bytes 491528 | tf_op jit(solution)/shard_map/ppermute | solution.py:183
  60.6 2.2 %collective-permute-start.21 = (bf16[320,256]{1,0:T(8,128)(2,1)S(1)}, bf16[320,256]{1,0:T(8,128)(2,1)S(1)}, u32[]{:S(2)}, u32[]{:S(2)}) collective-permute-start(bf16[320,256]{1,0:T(8,128)(2,1)S(1)} %shard_map.116), channel_id=1, source_target_pairs={{0,24},{4,28},{8,16},{12,20},{16,8},{20,12},{24,0},{28,4},{1,25},{... | collective-permute-start | bytes 491528 | tf_op jit(solution)/shard_map/ppermute | solution.py:183
  62.8 1.2 %shard_map.112 = (bf16[128,2560]{1,0:T(8,128)(2,1)}, bf16[128,2560]{1,0:T(8,128)(2,1)}) custom-call(bf16[128,1280]{1,0:T(8,128)(2,1)S(1)} %get-tuple-element.90.o0, bf16[128,1280]{1,0:T(8,128)(2,1)S(1)} %get-tuple-element.91.dq0, bf16[128,3072]{1,0:T(8,128)(2,1)S(1)} %collective-permute-done.16.swapped), custom_call_target="tpu_custom_call" | custom-call | bytes 4000000 | tf_op jit(solution)/shard_map/pallas_call | solution.py:646
  63.9 3.6 %collective-permute-done.17.b = bf16[640,256]{1,0:T(8,128)(2,1)S(1)} collective-permute-done((bf16[640,256]{1,0:T(8,128)(2,1)S(1)}, bf16[640,256]{1,0:T(8,128)(2,1)S(1)}, u32[]{:S(2)}, u32[]{:S(2)}) %collective-permute-start.17) | collective-permute-done | bytes 327712 | tf_op jit(solution)/shard_map/ppermute | solution.py:183
  67.7 1.5 %collective-permute-start.22 = (bf16[320,256]{1,0:T(8,128)(2,1)S(1)}, bf16[320,256]{1,0:T(8,128)(2,1)S(1)}, u32[]{:S(2)}, u32[]{:S(2)}) collective-permute-start(bf16[320,256]{1,0:T(8,128)(2,1)S(1)} %get-tuple-element.103), channel_id=1, source_target_pairs={{0,4},{4,0},{8,12},{12,8},{16,20},{20,16},{24,28},{28,24},{1,5},{5... | collective-permute-start | bytes 491528 | tf_op jit(solution)/shard_map/ppermute | solution.py:183
  69.2 4.2 %collective-permute-done.21.b = bf16[320,256]{1,0:T(8,128)(2,1)S(1)} collective-permute-done((bf16[320,256]{1,0:T(8,128)(2,1)S(1)}, bf16[320,256]{1,0:T(8,128)(2,1)S(1)}, u32[]{:S(2)}, u32[]{:S(2)}) %collective-permute-start.21) | collective-permute-done | bytes 163872 | tf_op jit(solution)/shard_map/ppermute | solution.py:183
  73.5 1.2 %collective-permute-start.23 = (bf16[320,256]{1,0:T(8,128)(2,1)S(1)}, bf16[320,256]{1,0:T(8,128)(2,1)S(1)}, u32[]{:S(2)}, u32[]{:S(2)}) collective-permute-start(bf16[320,256]{1,0:T(8,128)(2,1)S(1)} %shard_map.118.p0), channel_id=1, source_target_pairs={{0,2},{1,3},{2,0},{3,1},{4,6},{5,7},{6,4},{7,5},{8,10},{9,11},{10,... | collective-permute-start | bytes 491528 | tf_op jit(solution)/shard_map/ppermute | solution.py:183
  74.7 1.3 %collective-permute-done.24.far_ref = bf16[128,3072]{1,0:T(8,128)(2,1)S(1)} collective-permute-done((bf16[128,3072]{1,0:T(8,128)(2,1)S(1)}, bf16[128,3072]{1,0:T(8,128)(2,1)S(1)}, u32[]{:S(2)}, u32[]{:S(2)}) %collective-permute-start.24) | collective-permute-done | bytes 786464 | tf_op jit(solution)/shard_map/ppermute | solution.py:183
  76.0 1.4 %shard_map.119 = (bf16[128,5120]{1,0:T(8,128)(2,1)}, bf16[128,512]{1,0:T(8,128)(2,1)}) custom-call(bf16[128,2560]{1,0:T(8,128)(2,1)S(1)} %get-tuple-element.85.own_ref, bf16[128,3072]{1,0:T(8,128)(2,1)S(1)} %collective-permute-done.24.far_ref, bf16[128,256]{1,0:T(8,128)(2,1)S(1)} %get-tuple-element.105.dk0, bf16[128,3072]{1,0:T(8,128)(2,1)S(1)} %collective-permute-done.16.swapped), custom_call_target="tpu_custom_call" | custom-call | bytes 3000000 | tf_op jit(solution)/shard_map/pallas_call | solution.py:625
  77.3 1.5 %collective-permute-done.23.p2 = bf16[320,256]{1,0:T(8,128)(2,1)S(1)} collective-permute-done((bf16[320,256]{1,0:T(8,128)(2,1)S(1)}, bf16[320,256]{1,0:T(8,128)(2,1)S(1)}, u32[]{:S(2)}, u32[]{:S(2)}) %collective-permute-start.23) | collective-permute-done | bytes 163872 | tf_op jit(solution)/shard_map/ppermute | solution.py:183
  78.9 1.4 %collective-permute-done.26.p3 = bf16[320,256]{1,0:T(8,128)(2,1)S(1)} collective-permute-done((bf16[320,256]{1,0:T(8,128)(2,1)S(1)}, bf16[320,256]{1,0:T(8,128)(2,1)S(1)}, u32[]{:S(2)}, u32[]{:S(2)}) %collective-permute-start.26) | collective-permute-done | bytes 163872 | tf_op jit(solution)/shard_map/ppermute | solution.py:183
  80.3 1.2 %shard_map.120 = f32[640,512]{1,0:T(8,128)} custom-call(bf16[320,256]{1,0:T(8,128)(2,1)S(1)} %shard_map.118.p0, bf16[320,256]{1,0:T(8,128)(2,1)S(1)} %collective-permute-done.25.p1, bf16[320,256]{1,0:T(8,128)(2,1)S(1)} %collective-permute-done.23.p2, bf16[320,256]{1,0:T(8,128)(2,1)S(1)} %collective-permute-done.26.p3), custom_call_target="tpu_custom_call" | custom-call | bytes 2000000 | tf_op jit(solution)/shard_map/pallas_call | solution.py:730
  (50 shorter events, 10.4 us)
Async XLA Ops:
  3.5 6.7 %collective-permute-start = (bf16[128,5760]{1,0:T(8,128)(2,1)}, bf16[128,5760]{1,0:T(8,128)(2,1)S(1)}, u32[]{:S(2)}, u32[]{:S(2)}) collective-permute-start(bf16[128,5760]{1,0:T(8,128)(2,1)} %get-tuple-element.59.p), channel_id=1, source_target_pairs={{0,1},{1,0},{2,3},{3,2},{4,5},{5,4},{6,7},{7,6},{8,9},{9,8},{10,11... | collective-permute-start | bytes 4423688 | tf_op jit(solution)/shard_map/ppermute | solution.py:183
  4.0 22.2 %collective-permute-start.1 = (bf16[128,3200]{1,0:T(8,128)(2,1)}, bf16[128,3200]{1,0:T(8,128)(2,1)S(1)}, u32[]{:S(2)}, u32[]{:S(2)}) collective-permute-start(bf16[128,3200]{1,0:T(8,128)(2,1)} %get-tuple-element.62), channel_id=1, source_target_pairs={{0,2},{1,3},{2,0},{3,1},{4,6},{5,7},{6,4},{7,5},{8,10},{9,11},{10,... | collective-permute-start | bytes 2457608 | tf_op jit(solution)/shard_map/ppermute | solution.py:183
  6.6 9.1 %collective-permute-start.7 = (bf16[320,256]{1,0:T(8,128)(2,1)}, bf16[320,256]{1,0:T(8,128)(2,1)S(1)}, u32[]{:S(2)}, u32[]{:S(2)}) collective-permute-start(bf16[320,256]{1,0:T(8,128)(2,1)} %get-tuple-element.64.w), channel_id=1, source_target_pairs={{0,24},{4,28},{8,16},{12,20},{16,8},{20,12},{24,0},{28,4},{1,25},{... | collective-permute-start | bytes 491528 | tf_op jit(solution)/shard_map/ppermute | solution.py:183
  10.2 14.4 %collective-permute-start.5 = (bf16[320,256]{1,0:T(8,128)(2,1)}, bf16[320,256]{1,0:T(8,128)(2,1)S(1)}, u32[]{:S(2)}, u32[]{:S(2)}) collective-permute-start(bf16[320,256]{1,0:T(8,128)(2,1)} %get-tuple-element.64.w), channel_id=1, source_target_pairs={{0,16},{4,20},{8,24},{12,28},{16,0},{20,4},{24,8},{28,12},{1,17},{... | collective-permute-start | bytes 491528 | tf_op jit(solution)/shard_map/ppermute | solution.py:183
  10.2 14.4 %collective-permute-start.3 = (bf16[320,256]{1,0:T(8,128)(2,1)}, bf16[320,256]{1,0:T(8,128)(2,1)S(1)}, u32[]{:S(2)}, u32[]{:S(2)}) collective-permute-start(bf16[320,256]{1,0:T(8,128)(2,1)} %get-tuple-element.64.w), channel_id=1, source_target_pairs={{0,8},{4,12},{8,0},{12,4},{16,24},{20,28},{24,16},{28,20},{1,9},{5... | collective-permute-start | bytes 491528 | tf_op jit(solution)/shard_map/ppermute | solution.py:183
  11.0 13.6 %collective-permute-start.2 = (bf16[320,256]{1,0:T(8,128)(2,1)}, bf16[320,256]{1,0:T(8,128)(2,1)S(1)}, u32[]{:S(2)}, u32[]{:S(2)}) collective-permute-start(bf16[320,256]{1,0:T(8,128)(2,1)} %get-tuple-element.64.w), channel_id=1, source_target_pairs={{0,4},{4,0},{8,12},{12,8},{16,20},{20,16},{24,28},{28,24},{1,5},{5... | collective-permute-start | bytes 491528 | tf_op jit(solution)/shard_map/ppermute | solution.py:183
  12.5 1.4 %copy-start = (bf16[128,5760]{1,0:T(8,128)(2,1)S(1)}, bf16[128,5760]{1,0:T(8,128)(2,1)}, u32[]{:S(2)}) copy-start(bf16[128,5760]{1,0:T(8,128)(2,1)} %get-tuple-element.59.p) | copy-start | bytes 4423684
  13.9 0.9 %copy-start.3 = (bf16[320,256]{1,0:T(8,128)(2,1)S(1)}, bf16[320,256]{1,0:T(8,128)(2,1)}, u32[]{:S(2)}) copy-start(bf16[320,256]{1,0:T(8,128)(2,1)} %get-tuple-element.64.w) | copy-start | bytes 491524
  15.8 10.5 %collective-permute-start.8 = (bf16[320,256]{1,0:T(8,128)(2,1)S(1)}, bf16[320,256]{1,0:T(8,128)(2,1)S(1)}, u32[]{:S(2)}, u32[]{:S(2)}) collective-permute-start(bf16[320,256]{1,0:T(8,128)(2,1)S(1)} %collective-permute-done.7.w6), channel_id=1, source_target_pairs={{0,4},{4,0},{8,12},{12,8},{16,20},{20,16},{24,28},{28,24},{1,5},{5... | collective-permute-start | bytes 491528 | tf_op jit(solution)/shard_map/ppermute | solution.py:183
  24.7 5.4 %collective-permute-start.4 = (bf16[320,256]{1,0:T(8,128)(2,1)S(1)}, bf16[320,256]{1,0:T(8,128)(2,1)S(1)}, u32[]{:S(2)}, u32[]{:S(2)}) collective-permute-start(bf16[320,256]{1,0:T(8,128)(2,1)S(1)} %collective-permute-done.2.w1), channel_id=1, source_target_pairs={{0,8},{4,12},{8,0},{12,4},{16,24},{20,28},{24,16},{28,20},{1,9},{5... | collective-permute-start | bytes 491528 | tf_op jit(solution)/shard_map/ppermute | solution.py:183
  24.7 5.5 %collective-permute-start.6 = (bf16[320,256]{1,0:T(8,128)(2,1)S(1)}, bf16[320,256]{1,0:T(8,128)(2,1)S(1)}, u32[]{:S(2)}, u32[]{:S(2)}) collective-permute-start(bf16[320,256]{1,0:T(8,128)(2,1)S(1)} %collective-permute-done.5.w4), channel_id=1, source_target_pairs={{0,4},{4,0},{8,12},{12,8},{16,20},{20,16},{24,28},{28,24},{1,5},{5... | collective-permute-start | bytes 491528 | tf_op jit(solution)/shard_map/ppermute | solution.py:183
  30.2 2.3 %collective-permute-start.9 = (bf16[128,3200]{1,0:T(8,128)(2,1)S(1)}, bf16[128,3200]{1,0:T(8,128)(2,1)S(1)}, u32[]{:S(2)}, u32[]{:S(2)}) collective-permute-start(bf16[128,3200]{1,0:T(8,128)(2,1)S(1)} %collective-permute-done.1.h2.p2), channel_id=1, source_target_pairs={{0,1},{1,0},{2,3},{3,2},{4,5},{5,4},{6,7},{7,6},{8,9},{9,8},{10,11... | collective-permute-start | bytes 2457608 | tf_op jit(solution)/shard_map/ppermute | solution.py:183
  30.9 4.1 %copy-start.1 = (bf16[1,128,2560]{2,1,0:T(8,128)(2,1)S(1)}, bf16[1,128,2560]{2,1,0:T(8,128)(2,1)}, u32[]{:S(2)}) copy-start(bf16[1,128,2560]{2,1,0:T(8,128)(2,1)} %param.7) | copy-start | bytes 1966084
  30.9 22.1 %collective-permute-start.15 = (bf16[2560,256]{1,0:T(8,128)(2,1)S(1)}, bf16[2560,256]{1,0:T(8,128)(2,1)S(1)}, u32[]{:S(2)}, u32[]{:S(2)}) collective-permute-start(bf16[2560,256]{1,0:T(8,128)(2,1)S(1)} %get-tuple-element.69.wp), channel_id=1, source_target_pairs={{0,1},{1,0},{2,3},{3,2},{4,5},{5,4},{6,7},{7,6},{8,9},{9,8},{10,11... | collective-permute-start | bytes 3932168 | tf_op jit(solution)/shard_map/ppermute | solution.py:183
  32.9 6.4 %collective-permute-start.10 = (bf16[512,128]{1,0:T(8,128)(2,1)S(1)}, bf16[512,128]{1,0:T(8,128)(2,1)S(1)}, u32[]{:S(2)}, u32[]{:S(2)}) collective-permute-start(bf16[512,128]{1,0:T(8,128)(2,1)S(1)} %get-tuple-element.70.vp), channel_id=1, source_target_pairs={{0,2},{1,3},{2,0},{3,1},{4,6},{5,7},{6,4},{7,5},{8,10},{9,11},{10,... | collective-permute-start | bytes 393224 | tf_op jit(solution)/shard_map/ppermute | solution.py:183
  33.4 5.9 %copy-start.2 = (bf16[1,128,2560]{2,1,0:T(8,128)(2,1)S(1)}, bf16[1,128,2560]{2,1,0:T(8,128)(2,1)}, u32[]{:S(2)}) copy-start(bf16[1,128,2560]{2,1,0:T(8,128)(2,1)} %param.11) | copy-start | bytes 1966084
  33.4 8.2 %collective-permute-start.11 = (bf16[512,128]{1,0:T(8,128)(2,1)S(1)}, bf16[512,128]{1,0:T(8,128)(2,1)S(1)}, u32[]{:S(2)}, u32[]{:S(2)}) collective-permute-start(bf16[512,128]{1,0:T(8,128)(2,1)S(1)} %get-tuple-element.75.vp), channel_id=1, source_target_pairs={{0,2},{1,3},{2,0},{3,1},{4,6},{5,7},{6,4},{7,5},{8,10},{9,11},{10,... | collective-permute-start | bytes 393224 | tf_op jit(solution)/shard_map/ppermute | solution.py:183
  41.1 7.9 %collective-permute-start.12 = (bf16[528,128]{1,0:T(8,128)(2,1)S(1)}, bf16[528,128]{1,0:T(8,128)(2,1)S(1)}, u32[]{:S(2)}, u32[]{:S(2)}) collective-permute-start(bf16[528,128]{1,0:T(8,128)(2,1)S(1)} %get-tuple-element.74.dv0), channel_id=1, source_target_pairs={{0,2},{1,3},{2,0},{3,1},{4,6},{5,7},{6,4},{7,5},{8,10},{9,11},{10,... | collective-permute-start | bytes 405512 | tf_op jit(solution)/shard_map/ppermute | solution.py:183
  43.5 5.5 %collective-permute-start.13 = (bf16[512,128]{1,0:T(8,128)(2,1)S(1)}, bf16[512,128]{1,0:T(8,128)(2,1)S(1)}, u32[]{:S(2)}, u32[]{:S(2)}) collective-permute-start(bf16[512,128]{1,0:T(8,128)(2,1)S(1)} %get-tuple-element.78.dv1), channel_id=1, source_target_pairs={{0,2},{1,3},{2,0},{3,1},{4,6},{5,7},{6,4},{7,5},{8,10},{9,11},{10,... | collective-permute-start | bytes 393224 | tf_op jit(solution)/shard_map/ppermute | solution.py:183
  49.1 3.9 %collective-permute-start.16 = (bf16[128,3072]{1,0:T(8,128)(2,1)S(1)}, bf16[128,3072]{1,0:T(8,128)(2,1)S(1)}, u32[]{:S(2)}, u32[]{:S(2)}) collective-permute-start(bf16[128,3072]{1,0:T(8,128)(2,1)S(1)} %get-tuple-element.84), channel_id=1, source_target_pairs={{0,1},{1,0},{2,3},{3,2},{4,5},{5,4},{6,7},{7,6},{8,9},{9,8},{10,11... | collective-permute-start | bytes 2359304 | tf_op jit(solution)/shard_map/ppermute | solution.py:183
  49.2 3.8 %collective-permute-start.14 = (bf16[256,256]{1,0:T(8,128)(2,1)S(1)}, bf16[256,256]{1,0:T(8,128)(2,1)S(1)}, u32[]{:S(2)}, u32[]{:S(2)}) collective-permute-start(bf16[256,256]{1,0:T(8,128)(2,1)S(1)} %get-tuple-element.81), channel_id=1, source_target_pairs={{0,1},{1,0},{2,3},{3,2},{4,5},{5,4},{6,7},{7,6},{8,9},{9,8},{10,11... | collective-permute-start | bytes 393224 | tf_op jit(solution)/shard_map/ppermute | solution.py:183
  50.3 7.5 %collective-permute-start.18 = (bf16[336,256]{1,0:T(8,128)(2,1)S(1)}, bf16[336,256]{1,0:T(8,128)(2,1)S(1)}, u32[]{:S(2)}, u32[]{:S(2)}) collective-permute-start(bf16[336,256]{1,0:T(8,128)(2,1)S(1)} %get-tuple-element.96), channel_id=1, source_target_pairs={{0,4},{4,0},{8,12},{12,8},{16,20},{20,16},{24,28},{28,24},{1,5},{5... | collective-permute-start | bytes 516104 | tf_op jit(solution)/shard_map/ppermute | solution.py:183
  51.8 8.7 %collective-permute-start.20 = (bf16[320,256]{1,0:T(8,128)(2,1)S(1)}, bf16[320,256]{1,0:T(8,128)(2,1)S(1)}, u32[]{:S(2)}, u32[]{:S(2)}) collective-permute-start(bf16[320,256]{1,0:T(8,128)(2,1)S(1)} %get-tuple-element.100), channel_id=1, source_target_pairs={{0,4},{4,0},{8,12},{12,8},{16,20},{20,16},{24,28},{28,24},{1,5},{5... | collective-permute-start | bytes 491528 | tf_op jit(solution)/shard_map/ppermute | solution.py:183
  54.8 12.8 %collective-permute-start.17 = (bf16[640,256]{1,0:T(8,128)(2,1)S(1)}, bf16[640,256]{1,0:T(8,128)(2,1)S(1)}, u32[]{:S(2)}, u32[]{:S(2)}) collective-permute-start(bf16[640,256]{1,0:T(8,128)(2,1)S(1)} %get-tuple-element.88), channel_id=1, source_target_pairs={{0,8},{4,12},{8,0},{12,4},{16,24},{20,28},{24,16},{28,20},{1,9},{5... | collective-permute-start | bytes 983048 | tf_op jit(solution)/shard_map/ppermute | solution.py:183
  56.7 19.3 %collective-permute-start.24 = (bf16[128,3072]{1,0:T(8,128)(2,1)S(1)}, bf16[128,3072]{1,0:T(8,128)(2,1)S(1)}, u32[]{:S(2)}, u32[]{:S(2)}) collective-permute-start(bf16[128,3072]{1,0:T(8,128)(2,1)S(1)} %get-tuple-element.104), channel_id=1, source_target_pairs={{0,2},{1,3},{2,0},{3,1},{4,6},{5,7},{6,4},{7,5},{8,10},{9,11},{10,... | collective-permute-start | bytes 2359304 | tf_op jit(solution)/shard_map/ppermute | solution.py:183
  57.8 11.4 %collective-permute-start.19 = (bf16[320,256]{1,0:T(8,128)(2,1)S(1)}, bf16[320,256]{1,0:T(8,128)(2,1)S(1)}, u32[]{:S(2)}, u32[]{:S(2)}) collective-permute-start(bf16[320,256]{1,0:T(8,128)(2,1)S(1)} %shard_map.115), channel_id=1, source_target_pairs={{0,16},{4,20},{8,24},{12,28},{16,0},{20,4},{24,8},{28,12},{1,17},{... | collective-permute-start | bytes 491528 | tf_op jit(solution)/shard_map/ppermute | solution.py:183
  60.6 12.8 %collective-permute-start.21 = (bf16[320,256]{1,0:T(8,128)(2,1)S(1)}, bf16[320,256]{1,0:T(8,128)(2,1)S(1)}, u32[]{:S(2)}, u32[]{:S(2)}) collective-permute-start(bf16[320,256]{1,0:T(8,128)(2,1)S(1)} %shard_map.116), channel_id=1, source_target_pairs={{0,24},{4,28},{8,16},{12,20},{16,8},{20,12},{24,0},{28,4},{1,25},{... | collective-permute-start | bytes 491528 | tf_op jit(solution)/shard_map/ppermute | solution.py:183
  67.7 5.8 %collective-permute-start.22 = (bf16[320,256]{1,0:T(8,128)(2,1)S(1)}, bf16[320,256]{1,0:T(8,128)(2,1)S(1)}, u32[]{:S(2)}, u32[]{:S(2)}) collective-permute-start(bf16[320,256]{1,0:T(8,128)(2,1)S(1)} %get-tuple-element.103), channel_id=1, source_target_pairs={{0,4},{4,0},{8,12},{12,8},{16,20},{20,16},{24,28},{28,24},{1,5},{5... | collective-permute-start | bytes 491528 | tf_op jit(solution)/shard_map/ppermute | solution.py:183
  73.5 5.4 %collective-permute-start.23 = (bf16[320,256]{1,0:T(8,128)(2,1)S(1)}, bf16[320,256]{1,0:T(8,128)(2,1)S(1)}, u32[]{:S(2)}, u32[]{:S(2)}) collective-permute-start(bf16[320,256]{1,0:T(8,128)(2,1)S(1)} %shard_map.118.p0), channel_id=1, source_target_pairs={{0,2},{1,3},{2,0},{3,1},{4,6},{5,7},{6,4},{7,5},{8,10},{9,11},{10,... | collective-permute-start | bytes 491528 | tf_op jit(solution)/shard_map/ppermute | solution.py:183
  74.7 4.2 %collective-permute-start.25 = (bf16[320,256]{1,0:T(8,128)(2,1)S(1)}, bf16[320,256]{1,0:T(8,128)(2,1)S(1)}, u32[]{:S(2)}, u32[]{:S(2)}) collective-permute-start(bf16[320,256]{1,0:T(8,128)(2,1)S(1)} %shard_map.118.p0), channel_id=1, source_target_pairs={{0,1},{1,0},{2,3},{3,2},{4,5},{5,4},{6,7},{7,6},{8,9},{9,8},{10,11... | collective-permute-start | bytes 491528 | tf_op jit(solution)/shard_map/ppermute | solution.py:183
  78.9 1.4 %collective-permute-start.26 = (bf16[320,256]{1,0:T(8,128)(2,1)S(1)}, bf16[320,256]{1,0:T(8,128)(2,1)S(1)}, u32[]{:S(2)}, u32[]{:S(2)}) collective-permute-start(bf16[320,256]{1,0:T(8,128)(2,1)S(1)} %collective-permute-done.23.p2), channel_id=1, source_target_pairs={{0,1},{1,0},{2,3},{3,2},{4,5},{5,4},{6,7},{7,6},{8,9},{9,8},{10,11... | collective-permute-start | bytes 491528 | tf_op jit(solution)/shard_map/ppermute | solution.py:183

commit v7 on v6

--- a/solution.py
+++ b/solution.py
@@ -763,8 +763,8 @@
     send5, send7 = weight_grad_sent(gv, ps)
     far5, far7 = swap(send5, "dp", 1), swap(send7, "dp", 1)
     own4, own6 = weight_grad_kept(after(gv, send5), ps)
-    gvs = swap(gv_send, "seq", 1)
-    swapped = swap(after(swap_out, gv), "seq", 1)
+    gvs = swap(after(gv_send, send5), "seq", 1)
+    swapped = swap(after(swap_out, send5), "seq", 1)
     gh0, gh_send = hidden_grad(gv_keep, gvs, wp, wps, dk2, swapped)
     send_b, own_b = weight_grad_near(after(gv, gh0), ps)
     far_b = swap(send_b, "dp", 2)

time: 81.6 us -> 81.6 us (level)
  no operation moved by 1% of the time
where the time goes in v7:
time: 81.6 us; the launch traced here: 81.4 us
  waiting for transfers between devices  31.8 us (39%)
  starting transfers between devices  30.1 us (37%)
  Pallas kernels  16.3 us (20%)
  local copies, waits for them, and re-layouts  2.3 us (3%)
    ppermute x27, waiting for transfers between devices, swap(): return lax.ppermute(x, axis, [(i, i ^ k) for i in range(size)])  31.8 us
    ppermute x27, starting transfers between devices, swap(): return lax.ppermute(x, axis, [(i, i ^ k) for i in range(size)])  30.1 us
    pallas_call x1, Pallas kernels, pack(): pl.pallas_call(pack_kernel, out_shape=(sds((ROWS, QUERY_AT)), sds((ROWS,...  2.89 us
    unnamed x8, local copies, waits for them, and re-layouts  2.3 us
    pallas_call x1, Pallas kernels, attention_second(): pl.pallas_call(attention_second_kernel, out_shape=(sds((ROWS, CORE_Q)),)...  1.85 us
    pallas_call x1, Pallas kernels, attention_first(): pl.pallas_call(attention_first_kernel, out_shape=(sds((4 * ROWS, QUERY_PE...  1.83 us
    pallas_call x1, Pallas kernels, scores(): pl.pallas_call(scores_kernel, out_shape=(sds((10, 4 * ROWS, 2 * ROWS)), s...  1.71 us
  transfers between devices with their start and end apart: 27, of which 12 were waited for; matrix products, arithmetic and copies ran while one was open for 0% of the time, Pallas kernels for 15%

profile of v7, /device:TPU:0, one launch (start us, length us, event | category | flops | bytes accessed | tf_op | source)
XLA Modules:
  0.0 81.4 jit_solution(8515810680688394666)
XLA Ops:
  0.6 2.9 %shard_map.101 = (bf16[128,3200]{1,0:T(8,128)(2,1)}, bf16[128,5760]{1,0:T(8,128)(2,1)}, bf16[320,256]{1,0:T(8,128)(2,1)}) custom-call(bf16[128,5120]{1,0:T(8,128)(2,1)} %bitcast.15, bf16[128,512]{1,0:T(8,128)(2,1)} %bitcast.16, s32[1,128]{1,0:T(1,128)} %doc.1, bf16[640,512]{1,0:T(8,128)(2,1)} %w.1, bf16[128,2560]{1,0:T(8,128)(2,1)} %bitcast.8, ...), custom_call_target="tpu_custom_call" | custom-call | bytes 3000000 | tf_op jit(solution)/shard_map/pallas_call | solution.py:265
  4.0 2.6 %collective-permute-start.1 = (bf16[128,3200]{1,0:T(8,128)(2,1)}, bf16[128,3200]{1,0:T(8,128)(2,1)S(1)}, u32[]{:S(2)}, u32[]{:S(2)}) collective-permute-start(bf16[128,3200]{1,0:T(8,128)(2,1)} %get-tuple-element.63), channel_id=1, source_target_pairs={{0,2},{1,3},{2,0},{3,1},{4,6},{5,7},{6,4},{7,5},{8,10},{9,11},{10,... | collective-permute-start | bytes 2457608 | tf_op jit(solution)/shard_map/ppermute | solution.py:183
  6.6 3.6 %collective-permute-start.7 = (bf16[320,256]{1,0:T(8,128)(2,1)}, bf16[320,256]{1,0:T(8,128)(2,1)S(1)}, u32[]{:S(2)}, u32[]{:S(2)}) collective-permute-start(bf16[320,256]{1,0:T(8,128)(2,1)} %get-tuple-element.65.w), channel_id=1, source_target_pairs={{0,24},{4,28},{8,16},{12,20},{16,8},{20,12},{24,0},{28,4},{1,25},{... | collective-permute-start | bytes 491528 | tf_op jit(solution)/shard_map/ppermute | solution.py:183
  11.0 1.5 %collective-permute-start.2 = (bf16[320,256]{1,0:T(8,128)(2,1)}, bf16[320,256]{1,0:T(8,128)(2,1)S(1)}, u32[]{:S(2)}, u32[]{:S(2)}) collective-permute-start(bf16[320,256]{1,0:T(8,128)(2,1)} %get-tuple-element.65.w), channel_id=1, source_target_pairs={{0,4},{4,0},{8,12},{12,8},{16,20},{20,16},{24,28},{28,24},{1,5},{5... | collective-permute-start | bytes 491528 | tf_op jit(solution)/shard_map/ppermute | solution.py:183
  12.5 1.4 %copy-done = bf16[128,5760]{1,0:T(8,128)(2,1)S(1)} copy-done((bf16[128,5760]{1,0:T(8,128)(2,1)S(1)}, bf16[128,5760]{1,0:T(8,128)(2,1)}, u32[]{:S(2)}) %copy-start) | copy-done | bytes 1474584
  15.8 1.5 %collective-permute-start.8 = (bf16[320,256]{1,0:T(8,128)(2,1)S(1)}, bf16[320,256]{1,0:T(8,128)(2,1)S(1)}, u32[]{:S(2)}, u32[]{:S(2)}) collective-permute-start(bf16[320,256]{1,0:T(8,128)(2,1)S(1)} %collective-permute-done.7.w6), channel_id=1, source_target_pairs={{0,4},{4,0},{8,12},{12,8},{16,20},{20,16},{24,28},{28,24},{1,5},{5... | collective-permute-start | bytes 491528 | tf_op jit(solution)/shard_map/ppermute | solution.py:183
  17.3 7.4 %collective-permute-done.5.w4 = bf16[320,256]{1,0:T(8,128)(2,1)S(1)} collective-permute-done((bf16[320,256]{1,0:T(8,128)(2,1)}, bf16[320,256]{1,0:T(8,128)(2,1)S(1)}, u32[]{:S(2)}, u32[]{:S(2)}) %collective-permute-start.5) | collective-permute-done | bytes 163872 | tf_op jit(solution)/shard_map/ppermute | solution.py:183
  24.7 1.6 %collective-permute-start.6 = (bf16[320,256]{1,0:T(8,128)(2,1)S(1)}, bf16[320,256]{1,0:T(8,128)(2,1)S(1)}, u32[]{:S(2)}, u32[]{:S(2)}) collective-permute-start(bf16[320,256]{1,0:T(8,128)(2,1)S(1)} %collective-permute-done.5.w4), channel_id=1, source_target_pairs={{0,4},{4,0},{8,12},{12,8},{16,20},{20,16},{24,28},{28,24},{1,5},{5... | collective-permute-start | bytes 491528 | tf_op jit(solution)/shard_map/ppermute | solution.py:183
  26.2 3.9 %collective-permute-done.4.w3 = bf16[320,256]{1,0:T(8,128)(2,1)S(1)} collective-permute-done((bf16[320,256]{1,0:T(8,128)(2,1)S(1)}, bf16[320,256]{1,0:T(8,128)(2,1)S(1)}, u32[]{:S(2)}, u32[]{:S(2)}) %collective-permute-start.4) | collective-permute-done | bytes 163872 | tf_op jit(solution)/shard_map/ppermute | solution.py:183
  31.5 1.0 %collective-permute-done.9.h3.p3 = bf16[128,3200]{1,0:T(8,128)(2,1)S(1)} collective-permute-done((bf16[128,3200]{1,0:T(8,128)(2,1)S(1)}, bf16[128,3200]{1,0:T(8,128)(2,1)S(1)}, u32[]{:S(2)}, u32[]{:S(2)}) %collective-permute-start.9) | collective-permute-done | bytes 819232 | tf_op jit(solution)/shard_map/ppermute | solution.py:183
  33.4 1.5 %collective-permute-start.11 = (bf16[512,128]{1,0:T(8,128)(2,1)S(1)}, bf16[512,128]{1,0:T(8,128)(2,1)S(1)}, u32[]{:S(2)}, u32[]{:S(2)}) collective-permute-start(bf16[512,128]{1,0:T(8,128)(2,1)S(1)} %get-tuple-element.76.vp), channel_id=1, source_target_pairs={{0,2},{1,3},{2,0},{3,1},{4,6},{5,7},{6,4},{7,5},{8,10},{9,11},{10,... | collective-permute-start | bytes 393224 | tf_op jit(solution)/shard_map/ppermute | solution.py:183
  35.0 1.7 %shard_map.105 = (bf16[10,512,256]{2,1,0:T(8,128)(2,1)S(1)}, f32[80,256]{1,0:T(8,128)S(1)}) custom-call(bf16[128,2560]{1,0:T(8,128)(2,1)S(1)} %bitcast.9, bf16[128,3200]{1,0:T(8,128)(2,1)S(1)} %get-tuple-element.62.h0.p0, bf16[128,5760]{1,0:T(8,128)(2,1)S(1)} %collective-permute-done.h1.p1, bf16[128,3200]{1,0:T(8,128)(2,1)S(1)} %collective-permute-done.1.h2.p2, ...), custom_call_target="tpu_custom_call" | custom-call | flops 2684354560 | bytes 6000000 | tf_op jit(solution)/shard_map/pallas_call | solution.py:376
  36.7 2.6 %collective-permute-done.10.rv = bf16[512,128]{1,0:T(8,128)(2,1)S(1)} collective-permute-done((bf16[512,128]{1,0:T(8,128)(2,1)S(1)}, bf16[512,128]{1,0:T(8,128)(2,1)S(1)}, u32[]{:S(2)}, u32[]{:S(2)}) %collective-permute-start.10) | collective-permute-done | bytes 131104 | tf_op jit(solution)/shard_map/ppermute | solution.py:183
  39.3 1.8 %shard_map.106 = (bf16[512,640]{1,0:T(8,128)(2,1)S(1)}, bf16[512,128]{1,0:T(8,128)(2,1)S(1)}, bf16[528,128]{1,0:T(8,128)(2,1)S(1)}) custom-call(bf16[10,512,256]{2,1,0:T(8,128)(2,1)S(1)} %get-tuple-element.73.e_ref, f32[80,256]{1,0:T(8,128)S(1)} %get-tuple-element.74.inv_ref, bf16[128,2560]{1,0:T(8,128)(2,1)S(1)} %bitcast.10, ...), custom_call_target="tpu_custom_call" | custom-call | flops 3355443200 | bytes 3000000 | tf_op jit(solution)/shard_map/pallas_call | solution.py:457
  41.7 1.8 %shard_map.107 = (bf16[128,1280]{1,0:T(8,128)(2,1)S(1)}, bf16[128,1280]{1,0:T(8,128)(2,1)S(1)}, bf16[128,256]{1,0:T(8,128)(2,1)S(1)}, bf16[128,256]{1,0:T(8,128)...) custom-call(bf16[10,512,256]{2,1,0:T(8,128)(2,1)S(1)} %get-tuple-element.73.e_ref, ...), custom_call_target="tpu_custom_call" | custom-call | flops 3355443200 | bytes 3000000 | tf_op jit(solution)/shard_map/pallas_call | solution.py:471
  43.5 1.6 %collective-permute-start.13 = (bf16[512,128]{1,0:T(8,128)(2,1)S(1)}, bf16[512,128]{1,0:T(8,128)(2,1)S(1)}, u32[]{:S(2)}, u32[]{:S(2)}) collective-permute-start(bf16[512,128]{1,0:T(8,128)(2,1)S(1)} %get-tuple-element.79.dv1), channel_id=1, source_target_pairs={{0,2},{1,3},{2,0},{3,1},{4,6},{5,7},{6,4},{7,5},{8,10},{9,11},{10,... | collective-permute-start | bytes 393224 | tf_op jit(solution)/shard_map/ppermute | solution.py:183
  45.2 3.9 %collective-permute-done.13.rdv1 = bf16[512,128]{1,0:T(8,128)(2,1)S(1)} collective-permute-done((bf16[512,128]{1,0:T(8,128)(2,1)S(1)}, bf16[512,128]{1,0:T(8,128)(2,1)S(1)}, u32[]{:S(2)}, u32[]{:S(2)}) %collective-permute-start.13) | collective-permute-done | bytes 131104 | tf_op jit(solution)/shard_map/ppermute | solution.py:183
  50.3 1.5 %collective-permute-start.18 = (bf16[336,256]{1,0:T(8,128)(2,1)S(1)}, bf16[336,256]{1,0:T(8,128)(2,1)S(1)}, u32[]{:S(2)}, u32[]{:S(2)}) collective-permute-start(bf16[336,256]{1,0:T(8,128)(2,1)S(1)} %get-tuple-element.83), channel_id=1, source_target_pairs={{0,4},{4,0},{8,12},{12,8},{16,20},{20,16},{24,28},{28,24},{1,5},{5... | collective-permute-start | bytes 516104 | tf_op jit(solution)/shard_map/ppermute | solution.py:183
  54.7 1.9 %collective-permute-start.17 = (bf16[640,256]{1,0:T(8,128)(2,1)S(1)}, bf16[640,256]{1,0:T(8,128)(2,1)S(1)}, u32[]{:S(2)}, u32[]{:S(2)}) collective-permute-start(bf16[640,256]{1,0:T(8,128)(2,1)S(1)} %get-tuple-element.91), channel_id=1, source_target_pairs={{0,8},{4,12},{8,0},{12,4},{16,24},{20,28},{24,16},{28,20},{1,9},{5... | collective-permute-start | bytes 983048 | tf_op jit(solution)/shard_map/ppermute | solution.py:183
  56.6 1.1 %collective-permute-start.24 = (bf16[128,3072]{1,0:T(8,128)(2,1)S(1)}, bf16[128,3072]{1,0:T(8,128)(2,1)S(1)}, u32[]{:S(2)}, u32[]{:S(2)}) collective-permute-start(bf16[128,3072]{1,0:T(8,128)(2,1)S(1)} %get-tuple-element.106), channel_id=1, source_target_pairs={{0,2},{1,3},{2,0},{3,1},{4,6},{5,7},{6,4},{7,5},{8,10},{9,11},{10,... | collective-permute-start | bytes 2359304 | tf_op jit(solution)/shard_map/ppermute | solution.py:183
  57.8 2.7 %collective-permute-start.19 = (bf16[320,256]{1,0:T(8,128)(2,1)S(1)}, bf16[320,256]{1,0:T(8,128)(2,1)S(1)}, u32[]{:S(2)}, u32[]{:S(2)}) collective-permute-start(bf16[320,256]{1,0:T(8,128)(2,1)S(1)} %shard_map.115), channel_id=1, source_target_pairs={{0,16},{4,20},{8,24},{12,28},{16,0},{20,4},{24,8},{28,12},{1,17},{... | collective-permute-start | bytes 491528 | tf_op jit(solution)/shard_map/ppermute | solution.py:183
  60.5 2.2 %collective-permute-start.21 = (bf16[320,256]{1,0:T(8,128)(2,1)S(1)}, bf16[320,256]{1,0:T(8,128)(2,1)S(1)}, u32[]{:S(2)}, u32[]{:S(2)}) collective-permute-start(bf16[320,256]{1,0:T(8,128)(2,1)S(1)} %shard_map.116), channel_id=1, source_target_pairs={{0,24},{4,28},{8,16},{12,20},{16,8},{20,12},{24,0},{28,4},{1,25},{... | collective-permute-start | bytes 491528 | tf_op jit(solution)/shard_map/ppermute | solution.py:183
  62.7 1.2 %shard_map.113 = (bf16[128,2560]{1,0:T(8,128)(2,1)}, bf16[128,2560]{1,0:T(8,128)(2,1)}) custom-call(bf16[128,1280]{1,0:T(8,128)(2,1)S(1)} %get-tuple-element.93.o0, bf16[128,1280]{1,0:T(8,128)(2,1)S(1)} %get-tuple-element.94.dq0, bf16[128,3072]{1,0:T(8,128)(2,1)S(1)} %collective-permute-done.16.swapped), custom_call_target="tpu_custom_call" | custom-call | bytes 4000000 | tf_op jit(solution)/shard_map/pallas_call | solution.py:646
  63.9 3.6 %collective-permute-done.17.b = bf16[640,256]{1,0:T(8,128)(2,1)S(1)} collective-permute-done((bf16[640,256]{1,0:T(8,128)(2,1)S(1)}, bf16[640,256]{1,0:T(8,128)(2,1)S(1)}, u32[]{:S(2)}, u32[]{:S(2)}) %collective-permute-start.17) | collective-permute-done | bytes 327712 | tf_op jit(solution)/shard_map/ppermute | solution.py:183
  67.6 1.6 %collective-permute-start.22 = (bf16[320,256]{1,0:T(8,128)(2,1)S(1)}, bf16[320,256]{1,0:T(8,128)(2,1)S(1)}, u32[]{:S(2)}, u32[]{:S(2)}) collective-permute-start(bf16[320,256]{1,0:T(8,128)(2,1)S(1)} %get-tuple-element.105), channel_id=1, source_target_pairs={{0,4},{4,0},{8,12},{12,8},{16,20},{20,16},{24,28},{28,24},{1,5},{5... | collective-permute-start | bytes 491528 | tf_op jit(solution)/shard_map/ppermute | solution.py:183
  69.2 4.2 %collective-permute-done.21.b = bf16[320,256]{1,0:T(8,128)(2,1)S(1)} collective-permute-done((bf16[320,256]{1,0:T(8,128)(2,1)S(1)}, bf16[320,256]{1,0:T(8,128)(2,1)S(1)}, u32[]{:S(2)}, u32[]{:S(2)}) %collective-permute-start.21) | collective-permute-done | bytes 163872 | tf_op jit(solution)/shard_map/ppermute | solution.py:183
  73.4 1.2 %collective-permute-start.23 = (bf16[320,256]{1,0:T(8,128)(2,1)S(1)}, bf16[320,256]{1,0:T(8,128)(2,1)S(1)}, u32[]{:S(2)}, u32[]{:S(2)}) collective-permute-start(bf16[320,256]{1,0:T(8,128)(2,1)S(1)} %shard_map.118.p0), channel_id=1, source_target_pairs={{0,2},{1,3},{2,0},{3,1},{4,6},{5,7},{6,4},{7,5},{8,10},{9,11},{10,... | collective-permute-start | bytes 491528 | tf_op jit(solution)/shard_map/ppermute | solution.py:183
  74.6 1.3 %collective-permute-done.24.far_ref = bf16[128,3072]{1,0:T(8,128)(2,1)S(1)} collective-permute-done((bf16[128,3072]{1,0:T(8,128)(2,1)S(1)}, bf16[128,3072]{1,0:T(8,128)(2,1)S(1)}, u32[]{:S(2)}, u32[]{:S(2)}) %collective-permute-start.24) | collective-permute-done | bytes 786464 | tf_op jit(solution)/shard_map/ppermute | solution.py:183
  75.9 1.4 %shard_map.119 = (bf16[128,5120]{1,0:T(8,128)(2,1)}, bf16[128,512]{1,0:T(8,128)(2,1)}) custom-call(bf16[128,2560]{1,0:T(8,128)(2,1)S(1)} %get-tuple-element.88.own_ref, bf16[128,3072]{1,0:T(8,128)(2,1)S(1)} %collective-permute-done.24.far_ref, bf16[128,256]{1,0:T(8,128)(2,1)S(1)} %get-tuple-element.107.dk0, bf16[128,3072]{1,0:T(8,128)(2,1)S(1)} %collective-permute-done.16.swapped), custom_call_target="tpu_custom_call" | custom-call | bytes 3000000 | tf_op jit(solution)/shard_map/pallas_call | solution.py:625
  77.3 1.5 %collective-permute-done.23.p2 = bf16[320,256]{1,0:T(8,128)(2,1)S(1)} collective-permute-done((bf16[320,256]{1,0:T(8,128)(2,1)S(1)}, bf16[320,256]{1,0:T(8,128)(2,1)S(1)}, u32[]{:S(2)}, u32[]{:S(2)}) %collective-permute-start.23) | collective-permute-done | bytes 163872 | tf_op jit(solution)/shard_map/ppermute | solution.py:183
  78.8 1.4 %collective-permute-done.26.p3 = bf16[320,256]{1,0:T(8,128)(2,1)S(1)} collective-permute-done((bf16[320,256]{1,0:T(8,128)(2,1)S(1)}, bf16[320,256]{1,0:T(8,128)(2,1)S(1)}, u32[]{:S(2)}, u32[]{:S(2)}) %collective-permute-start.26) | collective-permute-done | bytes 163872 | tf_op jit(solution)/shard_map/ppermute | solution.py:183
  80.2 1.2 %shard_map.120 = f32[640,512]{1,0:T(8,128)} custom-call(bf16[320,256]{1,0:T(8,128)(2,1)S(1)} %shard_map.118.p0, bf16[320,256]{1,0:T(8,128)(2,1)S(1)} %collective-permute-done.25.p1, bf16[320,256]{1,0:T(8,128)(2,1)S(1)} %collective-permute-done.23.p2, bf16[320,256]{1,0:T(8,128)(2,1)S(1)} %collective-permute-done.26.p3), custom_call_target="tpu_custom_call" | custom-call | bytes 2000000 | tf_op jit(solution)/shard_map/pallas_call | solution.py:730
  (50 shorter events, 10.4 us)
Async XLA Ops:
  3.5 6.7 %collective-permute-start = (bf16[128,5760]{1,0:T(8,128)(2,1)}, bf16[128,5760]{1,0:T(8,128)(2,1)S(1)}, u32[]{:S(2)}, u32[]{:S(2)}) collective-permute-start(bf16[128,5760]{1,0:T(8,128)(2,1)} %get-tuple-element.60.p), channel_id=1, source_target_pairs={{0,1},{1,0},{2,3},{3,2},{4,5},{5,4},{6,7},{7,6},{8,9},{9,8},{10,11... | collective-permute-start | bytes 4423688 | tf_op jit(solution)/shard_map/ppermute | solution.py:183
  4.0 22.2 %collective-permute-start.1 = (bf16[128,3200]{1,0:T(8,128)(2,1)}, bf16[128,3200]{1,0:T(8,128)(2,1)S(1)}, u32[]{:S(2)}, u32[]{:S(2)}) collective-permute-start(bf16[128,3200]{1,0:T(8,128)(2,1)} %get-tuple-element.63), channel_id=1, source_target_pairs={{0,2},{1,3},{2,0},{3,1},{4,6},{5,7},{6,4},{7,5},{8,10},{9,11},{10,... | collective-permute-start | bytes 2457608 | tf_op jit(solution)/shard_map/ppermute | solution.py:183
  6.6 9.1 %collective-permute-start.7 = (bf16[320,256]{1,0:T(8,128)(2,1)}, bf16[320,256]{1,0:T(8,128)(2,1)S(1)}, u32[]{:S(2)}, u32[]{:S(2)}) collective-permute-start(bf16[320,256]{1,0:T(8,128)(2,1)} %get-tuple-element.65.w), channel_id=1, source_target_pairs={{0,24},{4,28},{8,16},{12,20},{16,8},{20,12},{24,0},{28,4},{1,25},{... | collective-permute-start | bytes 491528 | tf_op jit(solution)/shard_map/ppermute | solution.py:183
  10.2 14.4 %collective-permute-start.5 = (bf16[320,256]{1,0:T(8,128)(2,1)}, bf16[320,256]{1,0:T(8,128)(2,1)S(1)}, u32[]{:S(2)}, u32[]{:S(2)}) collective-permute-start(bf16[320,256]{1,0:T(8,128)(2,1)} %get-tuple-element.65.w), channel_id=1, source_target_pairs={{0,16},{4,20},{8,24},{12,28},{16,0},{20,4},{24,8},{28,12},{1,17},{... | collective-permute-start | bytes 491528 | tf_op jit(solution)/shard_map/ppermute | solution.py:183
  10.2 14.4 %collective-permute-start.3 = (bf16[320,256]{1,0:T(8,128)(2,1)}, bf16[320,256]{1,0:T(8,128)(2,1)S(1)}, u32[]{:S(2)}, u32[]{:S(2)}) collective-permute-start(bf16[320,256]{1,0:T(8,128)(2,1)} %get-tuple-element.65.w), channel_id=1, source_target_pairs={{0,8},{4,12},{8,0},{12,4},{16,24},{20,28},{24,16},{28,20},{1,9},{5... | collective-permute-start | bytes 491528 | tf_op jit(solution)/shard_map/ppermute | solution.py:183
  11.0 13.6 %collective-permute-start.2 = (bf16[320,256]{1,0:T(8,128)(2,1)}, bf16[320,256]{1,0:T(8,128)(2,1)S(1)}, u32[]{:S(2)}, u32[]{:S(2)}) collective-permute-start(bf16[320,256]{1,0:T(8,128)(2,1)} %get-tuple-element.65.w), channel_id=1, source_target_pairs={{0,4},{4,0},{8,12},{12,8},{16,20},{20,16},{24,28},{28,24},{1,5},{5... | collective-permute-start | bytes 491528 | tf_op jit(solution)/shard_map/ppermute | solution.py:183
  12.5 1.4 %copy-start = (bf16[128,5760]{1,0:T(8,128)(2,1)S(1)}, bf16[128,5760]{1,0:T(8,128)(2,1)}, u32[]{:S(2)}) copy-start(bf16[128,5760]{1,0:T(8,128)(2,1)} %get-tuple-element.60.p) | copy-start | bytes 4423684
  13.9 0.9 %copy-start.3 = (bf16[320,256]{1,0:T(8,128)(2,1)S(1)}, bf16[320,256]{1,0:T(8,128)(2,1)}, u32[]{:S(2)}) copy-start(bf16[320,256]{1,0:T(8,128)(2,1)} %get-tuple-element.65.w) | copy-start | bytes 491524
  15.8 10.5 %collective-permute-start.8 = (bf16[320,256]{1,0:T(8,128)(2,1)S(1)}, bf16[320,256]{1,0:T(8,128)(2,1)S(1)}, u32[]{:S(2)}, u32[]{:S(2)}) collective-permute-start(bf16[320,256]{1,0:T(8,128)(2,1)S(1)} %collective-permute-done.7.w6), channel_id=1, source_target_pairs={{0,4},{4,0},{8,12},{12,8},{16,20},{20,16},{24,28},{28,24},{1,5},{5... | collective-permute-start | bytes 491528 | tf_op jit(solution)/shard_map/ppermute | solution.py:183
  24.7 5.4 %collective-permute-start.4 = (bf16[320,256]{1,0:T(8,128)(2,1)S(1)}, bf16[320,256]{1,0:T(8,128)(2,1)S(1)}, u32[]{:S(2)}, u32[]{:S(2)}) collective-permute-start(bf16[320,256]{1,0:T(8,128)(2,1)S(1)} %collective-permute-done.2.w1), channel_id=1, source_target_pairs={{0,8},{4,12},{8,0},{12,4},{16,24},{20,28},{24,16},{28,20},{1,9},{5... | collective-permute-start | bytes 491528 | tf_op jit(solution)/shard_map/ppermute | solution.py:183
  24.7 5.5 %collective-permute-start.6 = (bf16[320,256]{1,0:T(8,128)(2,1)S(1)}, bf16[320,256]{1,0:T(8,128)(2,1)S(1)}, u32[]{:S(2)}, u32[]{:S(2)}) collective-permute-start(bf16[320,256]{1,0:T(8,128)(2,1)S(1)} %collective-permute-done.5.w4), channel_id=1, source_target_pairs={{0,4},{4,0},{8,12},{12,8},{16,20},{20,16},{24,28},{28,24},{1,5},{5... | collective-permute-start | bytes 491528 | tf_op jit(solution)/shard_map/ppermute | solution.py:183
  30.2 2.3 %collective-permute-start.9 = (bf16[128,3200]{1,0:T(8,128)(2,1)S(1)}, bf16[128,3200]{1,0:T(8,128)(2,1)S(1)}, u32[]{:S(2)}, u32[]{:S(2)}) collective-permute-start(bf16[128,3200]{1,0:T(8,128)(2,1)S(1)} %collective-permute-done.1.h2.p2), channel_id=1, source_target_pairs={{0,1},{1,0},{2,3},{3,2},{4,5},{5,4},{6,7},{7,6},{8,9},{9,8},{10,11... | collective-permute-start | bytes 2457608 | tf_op jit(solution)/shard_map/ppermute | solution.py:183
  30.9 4.1 %copy-start.1 = (bf16[1,128,2560]{2,1,0:T(8,128)(2,1)S(1)}, bf16[1,128,2560]{2,1,0:T(8,128)(2,1)}, u32[]{:S(2)}) copy-start(bf16[1,128,2560]{2,1,0:T(8,128)(2,1)} %param.7) | copy-start | bytes 1966084
  30.9 22.0 %collective-permute-start.15 = (bf16[2560,256]{1,0:T(8,128)(2,1)S(1)}, bf16[2560,256]{1,0:T(8,128)(2,1)S(1)}, u32[]{:S(2)}, u32[]{:S(2)}) collective-permute-start(bf16[2560,256]{1,0:T(8,128)(2,1)S(1)} %get-tuple-element.70.wp), channel_id=1, source_target_pairs={{0,1},{1,0},{2,3},{3,2},{4,5},{5,4},{6,7},{7,6},{8,9},{9,8},{10,11... | collective-permute-start | bytes 3932168 | tf_op jit(solution)/shard_map/ppermute | solution.py:183
  32.9 6.4 %collective-permute-start.10 = (bf16[512,128]{1,0:T(8,128)(2,1)S(1)}, bf16[512,128]{1,0:T(8,128)(2,1)S(1)}, u32[]{:S(2)}, u32[]{:S(2)}) collective-permute-start(bf16[512,128]{1,0:T(8,128)(2,1)S(1)} %get-tuple-element.71.vp), channel_id=1, source_target_pairs={{0,2},{1,3},{2,0},{3,1},{4,6},{5,7},{6,4},{7,5},{8,10},{9,11},{10,... | collective-permute-start | bytes 393224 | tf_op jit(solution)/shard_map/ppermute | solution.py:183
  33.4 5.9 %copy-start.2 = (bf16[1,128,2560]{2,1,0:T(8,128)(2,1)S(1)}, bf16[1,128,2560]{2,1,0:T(8,128)(2,1)}, u32[]{:S(2)}) copy-start(bf16[1,128,2560]{2,1,0:T(8,128)(2,1)} %param.11) | copy-start | bytes 1966084
  33.4 8.2 %collective-permute-start.11 = (bf16[512,128]{1,0:T(8,128)(2,1)S(1)}, bf16[512,128]{1,0:T(8,128)(2,1)S(1)}, u32[]{:S(2)}, u32[]{:S(2)}) collective-permute-start(bf16[512,128]{1,0:T(8,128)(2,1)S(1)} %get-tuple-element.76.vp), channel_id=1, source_target_pairs={{0,2},{1,3},{2,0},{3,1},{4,6},{5,7},{6,4},{7,5},{8,10},{9,11},{10,... | collective-permute-start | bytes 393224 | tf_op jit(solution)/shard_map/ppermute | solution.py:183
  41.1 7.9 %collective-permute-start.12 = (bf16[528,128]{1,0:T(8,128)(2,1)S(1)}, bf16[528,128]{1,0:T(8,128)(2,1)S(1)}, u32[]{:S(2)}, u32[]{:S(2)}) collective-permute-start(bf16[528,128]{1,0:T(8,128)(2,1)S(1)} %get-tuple-element.75.dv0), channel_id=1, source_target_pairs={{0,2},{1,3},{2,0},{3,1},{4,6},{5,7},{6,4},{7,5},{8,10},{9,11},{10,... | collective-permute-start | bytes 405512 | tf_op jit(solution)/shard_map/ppermute | solution.py:183
  43.5 5.5 %collective-permute-start.13 = (bf16[512,128]{1,0:T(8,128)(2,1)S(1)}, bf16[512,128]{1,0:T(8,128)(2,1)S(1)}, u32[]{:S(2)}, u32[]{:S(2)}) collective-permute-start(bf16[512,128]{1,0:T(8,128)(2,1)S(1)} %get-tuple-element.79.dv1), channel_id=1, source_target_pairs={{0,2},{1,3},{2,0},{3,1},{4,6},{5,7},{6,4},{7,5},{8,10},{9,11},{10,... | collective-permute-start | bytes 393224 | tf_op jit(solution)/shard_map/ppermute | solution.py:183
  49.7 3.2 %collective-permute-start.16 = (bf16[128,3072]{1,0:T(8,128)(2,1)S(1)}, bf16[128,3072]{1,0:T(8,128)(2,1)S(1)}, u32[]{:S(2)}, u32[]{:S(2)}) collective-permute-start(bf16[128,3072]{1,0:T(8,128)(2,1)S(1)} %get-tuple-element.87), channel_id=1, source_target_pairs={{0,1},{1,0},{2,3},{3,2},{4,5},{5,4},{6,7},{7,6},{8,9},{9,8},{10,11... | collective-permute-start | bytes 2359304 | tf_op jit(solution)/shard_map/ppermute | solution.py:183
  49.8 3.1 %collective-permute-start.14 = (bf16[256,256]{1,0:T(8,128)(2,1)S(1)}, bf16[256,256]{1,0:T(8,128)(2,1)S(1)}, u32[]{:S(2)}, u32[]{:S(2)}) collective-permute-start(bf16[256,256]{1,0:T(8,128)(2,1)S(1)} %get-tuple-element.84), channel_id=1, source_target_pairs={{0,1},{1,0},{2,3},{3,2},{4,5},{5,4},{6,7},{7,6},{8,9},{9,8},{10,11... | collective-permute-start | bytes 393224 | tf_op jit(solution)/shard_map/ppermute | solution.py:183
  50.3 7.4 %collective-permute-start.18 = (bf16[336,256]{1,0:T(8,128)(2,1)S(1)}, bf16[336,256]{1,0:T(8,128)(2,1)S(1)}, u32[]{:S(2)}, u32[]{:S(2)}) collective-permute-start(bf16[336,256]{1,0:T(8,128)(2,1)S(1)} %get-tuple-element.83), channel_id=1, source_target_pairs={{0,4},{4,0},{8,12},{12,8},{16,20},{20,16},{24,28},{28,24},{1,5},{5... | collective-permute-start | bytes 516104 | tf_op jit(solution)/shard_map/ppermute | solution.py:183
  51.8 8.7 %collective-permute-start.20 = (bf16[320,256]{1,0:T(8,128)(2,1)S(1)}, bf16[320,256]{1,0:T(8,128)(2,1)S(1)}, u32[]{:S(2)}, u32[]{:S(2)}) collective-permute-start(bf16[320,256]{1,0:T(8,128)(2,1)S(1)} %get-tuple-element.102), channel_id=1, source_target_pairs={{0,4},{4,0},{8,12},{12,8},{16,20},{20,16},{24,28},{28,24},{1,5},{5... | collective-permute-start | bytes 491528 | tf_op jit(solution)/shard_map/ppermute | solution.py:183
  54.7 12.8 %collective-permute-start.17 = (bf16[640,256]{1,0:T(8,128)(2,1)S(1)}, bf16[640,256]{1,0:T(8,128)(2,1)S(1)}, u32[]{:S(2)}, u32[]{:S(2)}) collective-permute-start(bf16[640,256]{1,0:T(8,128)(2,1)S(1)} %get-tuple-element.91), channel_id=1, source_target_pairs={{0,8},{4,12},{8,0},{12,4},{16,24},{20,28},{24,16},{28,20},{1,9},{5... | collective-permute-start | bytes 983048 | tf_op jit(solution)/shard_map/ppermute | solution.py:183
  56.6 19.3 %collective-permute-start.24 = (bf16[128,3072]{1,0:T(8,128)(2,1)S(1)}, bf16[128,3072]{1,0:T(8,128)(2,1)S(1)}, u32[]{:S(2)}, u32[]{:S(2)}) collective-permute-start(bf16[128,3072]{1,0:T(8,128)(2,1)S(1)} %get-tuple-element.106), channel_id=1, source_target_pairs={{0,2},{1,3},{2,0},{3,1},{4,6},{5,7},{6,4},{7,5},{8,10},{9,11},{10,... | collective-permute-start | bytes 2359304 | tf_op jit(solution)/shard_map/ppermute | solution.py:183
  57.8 11.4 %collective-permute-start.19 = (bf16[320,256]{1,0:T(8,128)(2,1)S(1)}, bf16[320,256]{1,0:T(8,128)(2,1)S(1)}, u32[]{:S(2)}, u32[]{:S(2)}) collective-permute-start(bf16[320,256]{1,0:T(8,128)(2,1)S(1)} %shard_map.115), channel_id=1, source_target_pairs={{0,16},{4,20},{8,24},{12,28},{16,0},{20,4},{24,8},{28,12},{1,17},{... | collective-permute-start | bytes 491528 | tf_op jit(solution)/shard_map/ppermute | solution.py:183
  60.5 12.8 %collective-permute-start.21 = (bf16[320,256]{1,0:T(8,128)(2,1)S(1)}, bf16[320,256]{1,0:T(8,128)(2,1)S(1)}, u32[]{:S(2)}, u32[]{:S(2)}) collective-permute-start(bf16[320,256]{1,0:T(8,128)(2,1)S(1)} %shard_map.116), channel_id=1, source_target_pairs={{0,24},{4,28},{8,16},{12,20},{16,8},{20,12},{24,0},{28,4},{1,25},{... | collective-permute-start | bytes 491528 | tf_op jit(solution)/shard_map/ppermute | solution.py:183
  67.6 5.8 %collective-permute-start.22 = (bf16[320,256]{1,0:T(8,128)(2,1)S(1)}, bf16[320,256]{1,0:T(8,128)(2,1)S(1)}, u32[]{:S(2)}, u32[]{:S(2)}) collective-permute-start(bf16[320,256]{1,0:T(8,128)(2,1)S(1)} %get-tuple-element.105), channel_id=1, source_target_pairs={{0,4},{4,0},{8,12},{12,8},{16,20},{20,16},{24,28},{28,24},{1,5},{5... | collective-permute-start | bytes 491528 | tf_op jit(solution)/shard_map/ppermute | solution.py:183
  73.4 5.4 %collective-permute-start.23 = (bf16[320,256]{1,0:T(8,128)(2,1)S(1)}, bf16[320,256]{1,0:T(8,128)(2,1)S(1)}, u32[]{:S(2)}, u32[]{:S(2)}) collective-permute-start(bf16[320,256]{1,0:T(8,128)(2,1)S(1)} %shard_map.118.p0), channel_id=1, source_target_pairs={{0,2},{1,3},{2,0},{3,1},{4,6},{5,7},{6,4},{7,5},{8,10},{9,11},{10,... | collective-permute-start | bytes 491528 | tf_op jit(solution)/shard_map/ppermute | solution.py:183
  74.6 4.2 %collective-permute-start.25 = (bf16[320,256]{1,0:T(8,128)(2,1)S(1)}, bf16[320,256]{1,0:T(8,128)(2,1)S(1)}, u32[]{:S(2)}, u32[]{:S(2)}) collective-permute-start(bf16[320,256]{1,0:T(8,128)(2,1)S(1)} %shard_map.118.p0), channel_id=1, source_target_pairs={{0,1},{1,0},{2,3},{3,2},{4,5},{5,4},{6,7},{7,6},{8,9},{9,8},{10,11... | collective-permute-start | bytes 491528 | tf_op jit(solution)/shard_map/ppermute | solution.py:183
  78.8 1.4 %collective-permute-start.26 = (bf16[320,256]{1,0:T(8,128)(2,1)S(1)}, bf16[320,256]{1,0:T(8,128)(2,1)S(1)}, u32[]{:S(2)}, u32[]{:S(2)}) collective-permute-start(bf16[320,256]{1,0:T(8,128)(2,1)S(1)} %collective-permute-done.23.p2), channel_id=1, source_target_pairs={{0,1},{1,0},{2,3},{3,2},{4,5},{5,4},{6,7},{7,6},{8,9},{9,8},{10,11... | collective-permute-start | bytes 491528 | tf_op jit(solution)/shard_map/ppermute | solution.py:183
